TPU v7x, 32 devices: a whole 2x2x4 slice. The times are simulated.
32 devices in a mesh: groups: 2 (over y), geo: 16 (over z, x, core).
Axes of the slice: x: 2, y: 2, z: 4, core: 2. Of those that a mesh axis runs over, the one named last changes fastest.
Arguments:
- initial_spectrum: float32 [1296, 16384], P(None, ('groups', 'geo')), parts along dimension 1, may hold values from 0.05 to 1
- wind_forcing: float32 [2, 16384], P(None, ('groups', 'geo')), parts along dimension 1, may hold values from 0.2 to 1.5
- sea_mask: int32 [16384], P(('groups', 'geo')), parts along dimension 0, may hold values 0 or 1
- courant: float32 [36], replicated, may hold values from 0.2 to 0.7
- input_rate: float32 [1296], replicated, may hold values from 0.02 to 0.2
- damping: float32 [1296], replicated, may hold values from 0.2 to 1
- steep_weight: float32 [1296], replicated, may hold values from 0.0002 to 0.002
- obs_owner: int32 [4096, 1], P(('groups', 'geo')), parts along dimension 0, may hold values from 0 to 15; in each aligned block of 128 rows (0 to 127, 128 to 255, ...) at most 16 rows name the same one
- obs_point: int32 [4096], P(('groups', 'geo')), parts along dimension 0, may hold values from 0 to 511
- obs_value: float32 [4096, 36], P(('groups', 'geo')), parts along dimension 0, may hold values from -4 to 4
- obs_weight: float32 [4096], P(('groups', 'geo')), parts along dimension 0, may hold values from 4 to 40
Outputs:
- grad_wind: float32 [2, 16384], P(None, ('groups', 'geo')), parts along dimension 1
- grad_initial: float32 [1296, 16384], P(None, ('groups', 'geo')), parts along dimension 1
There are 2 independent parts, one for each index of `groups`. A program takes and returns all parts, laid end to end along the dimension named above; an argument that names none is the same for every part. Nothing has to cross between parts.
Inputs may be any that keep to these rules, and one draw needn't show every extreme that they name: `obs_owner`: among the 128 rows of one device, at most 16 name the same owner, a bound that some block reaches of them.
All inputs are finite; a program needn't handle non-finite values. No bound on the sum of `sea_mask` on one device may be relied on, other than what follows from the above.
Results may differ from a plain program's by a relative error of at most 0.0001.
Values sent between devices are 32-bit elements; how exact they have to be, the bound alone decides.
No kernel may reach another device: no remote copies, remote signals or barrier semaphores. Data moves between devices by JAX's collectives and lax.ppermute only.
A program may use at most 64 MiB of HBM per device.

v0:
```python
import math

import jax
import jax.numpy as jnp
from jax import lax
from jax.sharding import PartitionSpec as P

ND = 36
NF = 36
NB = 1296
W = 128
CYCLES = 2


def extended(cells, sides, width):
    for axis, dim in sides:
        count = lax.axis_size(axis)
        ends = count - 1
        head = lax.slice_in_dim(cells, 0, width, axis=dim)
        tail = lax.slice_in_dim(cells, cells.shape[dim] - width, cells.shape[dim], axis=dim)
        cells = jnp.concatenate(
            [
                lax.ppermute(tail, axis, [(i, (i + 1) % count) for i in range(ends)]),
                cells,
                lax.ppermute(head, axis, [((i + 1) % count, i) for i in range(ends)]),
            ],
            axis=dim,
        )
    return cells


def stencil(courant, reverse):
    angle = 2.0 * math.pi * jnp.arange(ND, dtype=jnp.float32) / ND
    cosine = jnp.cos(angle)[None, :]
    sine = jnp.sin(angle)[None, :]
    if reverse:
        cosine = -cosine
        sine = -sine
    speed = courant[:, None]
    centre = (1.0 - speed * (jnp.abs(cosine) + jnp.abs(sine))).reshape(NB, 1)
    west = (speed * jnp.maximum(cosine, 0.0)).reshape(NB, 1)
    east = (speed * jnp.maximum(-cosine, 0.0)).reshape(NB, 1)
    south = (speed * jnp.maximum(sine, 0.0)).reshape(NB, 1)
    north = (speed * jnp.maximum(-sine, 0.0)).reshape(NB, 1)
    return (centre, west, east, south, north)


def propagate(field, sea, coeffs):
    centre, west, east, south, north = coeffs
    count = field.shape[1]
    column = jnp.arange(count, dtype=jnp.int32) % W
    masked = field * sea[None, :]
    padded = extended(masked, (("geo", 1),), W)
    from_west = padded[:, W - 1 : W - 1 + count] * (column > 0).astype(jnp.float32)[None, :]
    from_east = padded[:, W + 1 : W + 1 + count] * (column < W - 1).astype(jnp.float32)[None, :]
    from_south = padded[:, 0:count]
    from_north = padded[:, 2 * W : 2 * W + count]
    total = (
        centre * masked
        + west * from_west
        + east * from_east
        + south * from_south
        + north * from_north
    )
    return total * sea[None, :]


def growth(state, wind_row, input_rate, damping, steep_weight):
    steep = jnp.sum(steep_weight[:, None] * state, axis=0)
    return jnp.exp(input_rate[:, None] * wind_row[None, :] - damping[:, None] * steep[None, :])


def body(
    initial_spectrum,
    wind_forcing,
    sea_mask,
    courant,
    input_rate,
    damping,
    steep_weight,
    obs_owner,
    obs_point,
    obs_value,
    obs_weight,
):
    sea = sea_mask.astype(jnp.float32)
    forward = stencil(courant, False)
    backward = stencil(courant, True)
    spectrum = initial_spectrum
    saved = []
    for cycle in range(CYCLES):
        state = propagate(spectrum, sea, forward)
        saved.append(state)
        spectrum = state * growth(state, wind_forcing[cycle], input_rate, damping, steep_weight)
    count = spectrum.shape[1]
    mean_dir = jnp.mean(spectrum.reshape(NF, ND, count), axis=1)
    ranks = lax.axis_size("geo")
    rows = obs_point.shape[0]
    capacity = max(2, 2 * rows // ranks)
    owner = obs_owner[:, 0]
    onehot = (owner[:, None] == jnp.arange(ranks, dtype=jnp.int32)[None, :]).astype(jnp.int32)
    order = jnp.sum(jnp.cumsum(onehot, axis=0) * onehot, axis=1) - 1
    target = owner * capacity + order
    slots = ranks * capacity
    point_buffer = jnp.zeros((slots,), jnp.int32).at[target].set(obs_point)
    arrived = lax.all_to_all(point_buffer, "geo", split_axis=0, concat_axis=0, tiled=True)
    model_slots = mean_dir[:, arrived].T
    returned = lax.all_to_all(model_slots, "geo", split_axis=0, concat_axis=0, tiled=True)
    misfit = obs_weight[:, None] * (returned[target] - obs_value)
    misfit_buffer = jnp.zeros((slots, NF), jnp.float32).at[target].set(misfit)
    slot_misfit = lax.all_to_all(misfit_buffer, "geo", split_axis=0, concat_axis=0, tiled=True)
    adjoint_f = jnp.zeros((NF, count), jnp.float32).at[:, arrived].add(slot_misfit.T)
    adjoint = jnp.broadcast_to((adjoint_f / ND)[:, None, :], (NF, ND, count)).reshape(NB, count)
    grads = []
    for cycle in range(CYCLES - 1, -1, -1):
        state = saved[cycle]
        factor = growth(state, wind_forcing[cycle], input_rate, damping, steep_weight)
        product = adjoint * state * factor
        grads.append(jnp.sum(input_rate[:, None] * product, axis=0))
        tendency = -jnp.sum(damping[:, None] * product, axis=0)
        adjoint = propagate(
            adjoint * factor + steep_weight[:, None] * tendency[None, :], sea, backward
        )
    grad_wind = jnp.stack(grads[::-1], axis=0)
    return (grad_wind, adjoint)


def solution(mesh):
    return jax.shard_map(
        body,
        mesh=mesh,
        in_specs=(
            P(None, ("groups", "geo")),
            P(None, ("groups", "geo")),
            P(("groups", "geo")),
            P(),
            P(),
            P(),
            P(),
            P(("groups", "geo"), None),
            P(("groups", "geo")),
            P(("groups", "geo"), None),
            P(("groups", "geo")),
        ),
        out_specs=(P(None, ("groups", "geo")), P(None, ("groups", "geo"))),
        check_vma=False,
    )
```

profile of v0, /device:TPU:1, one launch (start us, length us, event | category | flops | bytes accessed | tf_op | source)
XLA Modules:
  0.0 162.3 jit_solution(12566882974459830872)
XLA Ops:
  0.6 0.7 convert_element_type.39
  1.3 2.1 %broadcast_multiply_fusion = f32[1296,512]{1,0:T(8,128)S(1)} fusion(f32[1296,512]{1,0:T(8,128)} %param.11, f32[512]{0:T(512)S(1)} %convert_element_type.39), kind=kLoop, calls=%fused_computation.95 | loop fusion | flops 663552 | bytes 5310464 | tf_op jit(solution)/shard_map/mul | solution.py:52
  3.4 1.1 fusion.76
  4.6 4.5 %collective-permute-start = (f32[1296,128]{1,0:T(8,128)}, f32[1296,128]{1,0:T(8,128)S(1)}, u32[]{:S(2)}, u32[]{:S(2)}) collective-permute-start(f32[1296,128]{1,0:T(8,128)} %get-tuple-element.18), channel_id=1, source_target_pairs={{0,1},{1,2},{2,3},{3,4},{4,5},{5,6},{6,7},{7,8},{8,9},{9,10},{10,1... | collective-permute-start | bytes 1990664 | tf_op jit(solution)/shard_map/ppermute | solution.py:23
  9.1 1.9 %collective-permute-start.1 = (f32[1296,128]{1,0:T(8,128)}, f32[1296,128]{1,0:T(8,128)}, u32[]{:S(2)}, u32[]{:S(2)}) collective-permute-start(f32[1296,128]{1,0:T(8,128)} %get-tuple-element.19), channel_id=1, source_target_pairs={{1,0},{2,1},{3,2},{4,3},{5,4},{6,5},{7,6},{8,7},{9,8},{10,9},{11,1... | collective-permute-start | bytes 1990664 | tf_op jit(solution)/shard_map/ppermute | solution.py:25
  12.1 12.0 %collective-permute-done = f32[1296,128]{1,0:T(8,128)S(1)} collective-permute-done((f32[1296,128]{1,0:T(8,128)}, f32[1296,128]{1,0:T(8,128)S(1)}, u32[]{:S(2)}, u32[]{:S(2)}) %collective-permute-start) | collective-permute-done | bytes 663584 | tf_op jit(solution)/shard_map/ppermute | solution.py:23
  24.1 5.6 %multiply_reduce_fusion.5 = (f32[512]{0:T(512)S(1)}, f32[1296,512]{1,0:T(8,128)S(1)}) fusion(f32[1296]{0:T(1024)S(1)} %copy-done.7, f32[512]{0:T(512)S(1)} %convert_element_type.39, f32[1296,128]{1,0:T(8,128)} %collective-permute-done.1, f32[1296,512]{1,0:T(8,128)S(1)} %broadcast_multiply_fusion, f32[1296]{0:T(1024)S(1)} %mul.277, ...), kind=kLoop, calls=%fused_computation.94 | loop fusion | flops 11943424 | bytes 6674816 | tf_op jit(solution)/shard_map/reduce_sum | solution.py:69
  29.8 0.7 multiply_multiply_fusion.2
  30.5 0.8 copy-done
  31.4 1.4 copy-done.3
  32.8 4.3 %collective-permute-start.2 = (f32[1296,128]{1,0:T(8,128)S(1)}, f32[1296,128]{1,0:T(8,128)S(1)}, u32[]{:S(2)}, u32[]{:S(2)}) collective-permute-start(f32[1296,128]{1,0:T(8,128)S(1)} %get-tuple-element.16), channel_id=1, source_target_pairs={{0,1},{1,2},{2,3},{3,4},{4,5},{5,6},{6,7},{7,8},{8,9},{9,10},{10,1... | collective-permute-start | bytes 1990664 | tf_op jit(solution)/shard_map/ppermute | solution.py:23
  37.1 1.9 %collective-permute-start.3 = (f32[1296,128]{1,0:T(8,128)S(1)}, f32[1296,128]{1,0:T(8,128)}, u32[]{:S(2)}, u32[]{:S(2)}) collective-permute-start(f32[1296,128]{1,0:T(8,128)S(1)} %get-tuple-element.17), channel_id=1, source_target_pairs={{1,0},{2,1},{3,2},{4,3},{5,4},{6,5},{7,6},{8,7},{9,8},{10,9},{11,1... | collective-permute-start | bytes 1990664 | tf_op jit(solution)/shard_map/ppermute | solution.py:25
  39.2 1.1 scatter_custom_fusion
  40.4 11.5 %all_to_all.36 = s32[16,16,1]{1,2,0:T(1,128)S(1)} all-to-all(s32[16,16,1]{1,2,0:T(1,128)S(1)} %bitcast.30), channel_id=1, replica_groups=mesh['groups'=2,'geo'=16] {'geo'}, dimensions={0} | all-to-all | bytes 2048 | tf_op jit(solution)/shard_map/all_to_all | solution.py:106
  51.9 0.5 broadcast.241
  52.4 0.7 reduce.3
  53.2 7.9 %multiply_reduce_fusion.4 = (f32[512]{0:T(512)S(1)}, f32[1296,512]{1,0:T(8,128)S(1)}) fusion(f32[1296]{0:T(1024)S(1)} %copy-done.7, f32[512]{0:T(512)S(1)} %convert_element_type.39, f32[1296,128]{1,0:T(8,128)} %collective-permute-done.3, f32[1296,512]{1,0:T(8,128)} %copy-done.3, f32[1296]{0:T(1024)S(1)} %mul.277, f32[1296,128]{1,0:T(8,128)S(1)} %collective-permute-done.2, ...), kind=kLoop, calls=%fused_computation.90 | loop fusion | flops 11943424 | bytes 6674816 | tf_op jit(solution)/shard_map/reduce_sum | solution.py:69
  61.2 2.1 %fusion.52 = f32[1296,512]{1,0:T(8,128)} fusion(f32[1296,512]{1,0:T(8,128)S(1)} %get-tuple-element.9, f32[512]{0:T(512)S(1)} %get-tuple-element.8, f32[512]{0:T(512)S(1)} %bitcast.27, f32[1296]{0:T(1024)S(1)} %copy-done.5, f32[1296]{0:T(1024)S(1)} %copy-done.6), kind=kLoop, calls=%fused_computation.91 | loop fusion | flops 2654208 | bytes 5322880 | tf_op jit(solution)/shard_map/mul | solution.py:94
  63.3 3.8 %reshape.239 = f32[36,36,512]{2,1,0:T(8,128)} reshape(f32[1296,512]{1,0:T(8,128)} %fusion.52) | data formatting | bytes 5308416 | tf_op jit(solution)/shard_map/reshape | solution.py:96
  67.1 2.3 %reduce_sum.83 = f32[36,512]{1,0:T(8,128)S(1)} reduce(f32[36,36,512]{2,1,0:T(8,128)} %reshape.239, f32[]{:T(128)} %constant.50.clone.1), dimensions={1}, to_apply=%region_5.6 | reduce | flops 645120 | bytes 2727940 | tf_op jit(solution)/shard_map/reduce_sum | solution.py:96
  69.6 0.7 gather_fusion
  70.3 0.8 reshape.296
  71.1 6.2 %all-to-all-start.1 = ((f32[16,1,576]{2,1,0:T(1,128)}), f32[16,1,576]{2,1,0:T(1,128)S(1)}, u32[]{:S(2)}, u32[]{:S(2)}) async-start(f32[16,1,576]{2,1,0:T(1,128)} %reshape.296), calls=%async_computation.1 | async-start | bytes 81920 | tf_op jit(solution)/shard_map/all_to_all | solution.py:108
  77.3 5.9 %all-to-all-done.1 = f32[16,1,576]{2,1,0:T(1,128)S(1)} async-done(((f32[16,1,576]{2,1,0:T(1,128)}), f32[16,1,576]{2,1,0:T(1,128)S(1)}, u32[]{:S(2)}, u32[]{:S(2)}) %all-to-all-start.1) | async-done | bytes 36896 | tf_op jit(solution)/shard_map/all_to_all | solution.py:108
  83.2 0.5 broadcast.242
  83.7 0.7 reduce.4
  84.6 0.6 gather_fusion.1
  85.5 0.9 scatter_custom_fusion.1
  86.5 9.3 %all_to_all.37 = f32[16,1,576]{2,1,0:T(1,128)S(1)} all-to-all(f32[16,1,576]{2,1,0:T(1,128)S(1)} %reshape.298), channel_id=1, replica_groups=mesh['groups'=2,'geo'=16] {'geo'}, dimensions={0} | all-to-all | bytes 73728 | tf_op jit(solution)/shard_map/all_to_all | solution.py:111
  95.8 0.7 reduce.5
  96.7 2.0 %scatter_custom_fusion.2 = f32[36,512]{0,1:T(8,128)S(1)} fusion(s32[256]{0:T(256)S(1)} %bitcast.34, f32[256,36]{1,0:T(8,128)S(1)} %bitcast.23, f32[]{:T(128)} %constant.50.clone.1), kind=kCustom, calls=%fused_computation.96 | custom fusion | flops 9216 | bytes 73732 | tf_op jit(solution)/shard_map/scatter-add | solution.py:112
  98.8 2.0 %broadcast_in_dim.8 = f32[36,36,512]{2,1,0:T(8,128)} broadcast(f32[36,512]{1,0:T(8,128)S(1)} %broadcast_multiply_fusion.1), dimensions={0,2} | broadcast | bytes 2727936 | tf_op jit(solution)/shard_map/broadcast_in_dim | solution.py:113
  100.8 3.9 %reshape.240 = f32[1296,512]{1,0:T(8,128)} reshape(f32[36,36,512]{2,1,0:T(8,128)} %broadcast_in_dim.8) | data formatting | bytes 5308416 | tf_op jit(solution)/shard_map/reshape | solution.py:113
  104.7 2.6 %multiply_reduce_fusion.3 = (f32[512]{0:T(512)S(1)}, f32[512]{0:T(512)S(1)}) fusion(f32[1296]{0:T(1024)S(1)} %copy-done.5, f32[1296]{0:T(1024)S(1)} %copy-done.6, f32[512]{0:T(512)S(1)} %get-tuple-element.8, f32[512]{0:T(512)S(1)} %bitcast.28, f32[1296,512]{1,0:T(8,128)} %reshape.240, f32[1296,512]{1,0:T(8,128)S(1)} %get-tuple-element.9), kind=kLoop, calls=%fused_computation.87 | loop fusion | flops 5970944 | bytes 5326976 | tf_op jit(solution)/shard_map/reduce_sum | solution.py:120
  107.3 1.0 add_multiply_fusion.1
  108.4 1.5 copy-done.4
  109.9 1.2 fusion.74
  111.1 2.9 %collective-permute-start.4 = (f32[1296,128]{1,0:T(8,128)}, f32[1296,128]{1,0:T(8,128)S(1)}, u32[]{:S(2)}, u32[]{:S(2)}) collective-permute-start(f32[1296,128]{1,0:T(8,128)} %get-tuple-element.14), channel_id=1, source_target_pairs={{0,1},{1,2},{2,3},{3,4},{4,5},{5,6},{6,7},{7,8},{8,9},{9,10},{10,1... | collective-permute-start | bytes 1990664 | tf_op jit(solution)/shard_map/ppermute | solution.py:23
  114.0 2.1 %collective-permute-start.5 = (f32[1296,128]{1,0:T(8,128)}, f32[1296,128]{1,0:T(8,128)}, u32[]{:S(2)}, u32[]{:S(2)}) collective-permute-start(f32[1296,128]{1,0:T(8,128)} %get-tuple-element.15), channel_id=1, source_target_pairs={{1,0},{2,1},{3,2},{4,3},{5,4},{6,5},{7,6},{8,7},{9,8},{10,9},{11,1... | collective-permute-start | bytes 1990664 | tf_op jit(solution)/shard_map/ppermute | solution.py:25
  116.2 12.8 %collective-permute-done.4 = f32[1296,128]{1,0:T(8,128)S(1)} collective-permute-done((f32[1296,128]{1,0:T(8,128)}, f32[1296,128]{1,0:T(8,128)S(1)}, u32[]{:S(2)}, u32[]{:S(2)}) %collective-permute-start.4) | collective-permute-done | bytes 663584 | tf_op jit(solution)/shard_map/ppermute | solution.py:23
  129.0 8.1 %multiply_multiply_fusion = (f32[1296,512]{1,0:T(8,128)S(1)}, f32[1296,512]{1,0:T(8,128)S(1)}) fusion(f32[1296,512]{1,0:T(8,128)S(1)} %copy-done.1, f32[512]{0:T(512)S(1)} %get-tuple-element.10, f32[1296]{0:T(1024)S(1)} %copy-done.5, f32[512]{0:T(512)S(1)} %bitcast.25, f32[1296]{0:T(1024)S(1)} %copy-done.6, f32[512]{0:T(512)S(1)} %convert_element_type.39, ...), kind=kLoop, calls=%fused_computation.85 | loop fusion | flops 13934592 | bytes 11990464 | tf_op jit(solution)/shard_map/mul | solution.py:118
  137.1 0.4 multiply_reduce_fusion
  137.6 1.0 add_multiply_fusion
  138.7 4.3 %collective-permute-start.6 = (f32[1296,128]{1,0:T(8,128)S(1)}, f32[1296,128]{1,0:T(8,128)S(1)}, u32[]{:S(2)}, u32[]{:S(2)}) collective-permute-start(f32[1296,128]{1,0:T(8,128)S(1)} %get-tuple-element.12), channel_id=1, source_target_pairs={{0,1},{1,2},{2,3},{3,4},{4,5},{5,6},{6,7},{7,8},{8,9},{9,10},{10,1... | collective-permute-start | bytes 1990664 | tf_op jit(solution)/shard_map/ppermute | solution.py:23
  143.0 1.9 %collective-permute-start.7 = (f32[1296,128]{1,0:T(8,128)S(1)}, f32[1296,128]{1,0:T(8,128)S(1)}, u32[]{:S(2)}, u32[]{:S(2)}) collective-permute-start(f32[1296,128]{1,0:T(8,128)S(1)} %get-tuple-element.13), channel_id=1, source_target_pairs={{1,0},{2,1},{3,2},{4,3},{5,4},{6,5},{7,6},{8,7},{9,8},{10,9},{11,1... | collective-permute-start | bytes 1990664 | tf_op jit(solution)/shard_map/ppermute | solution.py:25
  144.9 0.6 pad_maximum_fusion.8
  145.5 12.2 %collective-permute-done.6 = f32[1296,128]{1,0:T(8,128)S(1)} collective-permute-done((f32[1296,128]{1,0:T(8,128)S(1)}, f32[1296,128]{1,0:T(8,128)S(1)}, u32[]{:S(2)}, u32[]{:S(2)}) %collective-permute-start.6) | collective-permute-done | bytes 663584 | tf_op jit(solution)/shard_map/ppermute | solution.py:23
  157.7 4.6 %fusion.6 = f32[1296,512]{1,0:T(8,128)} fusion(f32[1296,512]{1,0:T(8,128)S(1)} %add_multiply_fusion, f32[1296,128]{1,0:T(8,128)S(1)} %collective-permute-done.7, f32[1296,128]{1,0:T(8,128)S(1)} %collective-permute-done.6, f32[1296]{0:T(1024)S(1)} %mul.277, f32[1296]{0:T(1024)S(1)} %mul.272, f32[512]{0:T(512)S(1)} %get-tuple-element.35, f32[1296]{0:T(1024)S(1)} %mul.265, ...), kind=kLoop, calls=%fused_computation.27 | loop fusion | flops 10616832 | bytes 6667584 | tf_op jit(solution)/shard_map/mul | solution.py:65
  (63 shorter events, 2.5 us)
Async XLA Ops:
  3.4 7.8 %copy-start.11 = (f32[36]{0:T(128)S(1)}, f32[36]{0:T(128)}, u32[]{:S(2)}) copy-start(f32[36]{0:T(128)} %param.14) | copy-start | bytes 436
  3.4 8.4 %copy-start.10 = (s32[128,1]{0,1:T(1,128)S(1)}, s32[128,1]{0,1:T(1,128)}, u32[]{:S(2)}) copy-start(s32[128,1]{0,1:T(1,128)} %param.18) | copy-start | bytes 1540
  3.4 8.6 %copy-start.9 = (f32[2,512]{1,0:T(2,128)S(1)}, f32[2,512]{1,0:T(2,128)}, u32[]{:S(2)}) copy-start(f32[2,512]{1,0:T(2,128)} %param.12) | copy-start | bytes 12292
  3.4 20.7 %copy-start.7 = (f32[1296]{0:T(1024)S(1)}, f32[1296]{0:T(1024)}, u32[]{:S(2)}) copy-start(f32[1296]{0:T(1024)} %param.17) | copy-start | bytes 15556
  4.6 19.5 %collective-permute-start = (f32[1296,128]{1,0:T(8,128)}, f32[1296,128]{1,0:T(8,128)S(1)}, u32[]{:S(2)}, u32[]{:S(2)}) collective-permute-start(f32[1296,128]{1,0:T(8,128)} %get-tuple-element.18), channel_id=1, source_target_pairs={{0,1},{1,2},{2,3},{3,4},{4,5},{5,6},{6,7},{7,8},{8,9},{9,10},{10,1... | collective-permute-start | bytes 1990664 | tf_op jit(solution)/shard_map/ppermute | solution.py:23
  9.1 15.0 %collective-permute-start.1 = (f32[1296,128]{1,0:T(8,128)}, f32[1296,128]{1,0:T(8,128)}, u32[]{:S(2)}, u32[]{:S(2)}) collective-permute-start(f32[1296,128]{1,0:T(8,128)} %get-tuple-element.19), channel_id=1, source_target_pairs={{1,0},{2,1},{3,2},{4,3},{5,4},{6,5},{7,6},{8,7},{9,8},{10,9},{11,1... | collective-permute-start | bytes 1990664 | tf_op jit(solution)/shard_map/ppermute | solution.py:25
  24.1 5.7 %copy-start.5 = (f32[1296]{0:T(1024)S(1)}, f32[1296]{0:T(1024)}, u32[]{:S(2)}) copy-start(f32[1296]{0:T(1024)} %param.16) | copy-start | bytes 15556
  24.1 5.7 %copy-start.6 = (f32[1296]{0:T(1024)S(1)}, f32[1296]{0:T(1024)}, u32[]{:S(2)}) copy-start(f32[1296]{0:T(1024)} %param.15) | copy-start | bytes 15556
  29.8 1.5 copy-start
  31.3 1.5 copy-start.3
  32.8 20.4 %collective-permute-start.2 = (f32[1296,128]{1,0:T(8,128)S(1)}, f32[1296,128]{1,0:T(8,128)S(1)}, u32[]{:S(2)}, u32[]{:S(2)}) collective-permute-start(f32[1296,128]{1,0:T(8,128)S(1)} %get-tuple-element.16), channel_id=1, source_target_pairs={{0,1},{1,2},{2,3},{3,4},{4,5},{5,6},{6,7},{7,8},{8,9},{9,10},{10,1... | collective-permute-start | bytes 1990664 | tf_op jit(solution)/shard_map/ppermute | solution.py:23
  37.1 16.1 %collective-permute-start.3 = (f32[1296,128]{1,0:T(8,128)S(1)}, f32[1296,128]{1,0:T(8,128)}, u32[]{:S(2)}, u32[]{:S(2)}) collective-permute-start(f32[1296,128]{1,0:T(8,128)S(1)} %get-tuple-element.17), channel_id=1, source_target_pairs={{1,0},{2,1},{3,2},{4,3},{5,4},{6,5},{7,6},{8,7},{9,8},{10,9},{11,1... | collective-permute-start | bytes 1990664 | tf_op jit(solution)/shard_map/ppermute | solution.py:25
  67.1 18.2 %copy-start.8 = (f32[128,36]{0,1:T(8,128)S(1)}, f32[128,36]{0,1:T(8,128)}, u32[]{:S(2)}) copy-start(f32[128,36]{0,1:T(8,128)} %param.20) | copy-start | bytes 55300
  67.1 18.2 %copy-start.12 = (f32[128]{0:T(128)S(1)}, f32[128]{0:T(128)}, u32[]{:S(2)}) copy-start(f32[128]{0:T(128)} %param.21) | copy-start | bytes 1540
  71.1 12.2 %all-to-all-start.1 = ((f32[16,1,576]{2,1,0:T(1,128)}), f32[16,1,576]{2,1,0:T(1,128)S(1)}, u32[]{:S(2)}, u32[]{:S(2)}) async-start(f32[16,1,576]{2,1,0:T(1,128)} %reshape.296), calls=%async_computation.1 | async-start | bytes 81920 | tf_op jit(solution)/shard_map/all_to_all | solution.py:108
  104.7 2.7 %copy-start.2 = (f32[1296,512]{1,0:T(8,128)S(1)}, f32[1296,512]{1,0:T(8,128)}, u32[]{:S(2)}) copy-start(f32[1296,512]{1,0:T(8,128)} %reshape.240) | copy-start | bytes 7962628
  108.4 1.5 copy-start.4
  109.9 19.1 %copy-start.1 = (f32[1296,512]{1,0:T(8,128)S(1)}, f32[1296,512]{1,0:T(8,128)}, u32[]{:S(2)}) copy-start(f32[1296,512]{1,0:T(8,128)} %copy-done) | copy-start | bytes 7962628
  111.1 17.9 %collective-permute-start.4 = (f32[1296,128]{1,0:T(8,128)}, f32[1296,128]{1,0:T(8,128)S(1)}, u32[]{:S(2)}, u32[]{:S(2)}) collective-permute-start(f32[1296,128]{1,0:T(8,128)} %get-tuple-element.14), channel_id=1, source_target_pairs={{0,1},{1,2},{2,3},{3,4},{4,5},{5,6},{6,7},{7,8},{8,9},{9,10},{10,1... | collective-permute-start | bytes 1990664 | tf_op jit(solution)/shard_map/ppermute | solution.py:23
  114.0 15.0 %collective-permute-start.5 = (f32[1296,128]{1,0:T(8,128)}, f32[1296,128]{1,0:T(8,128)}, u32[]{:S(2)}, u32[]{:S(2)}) collective-permute-start(f32[1296,128]{1,0:T(8,128)} %get-tuple-element.15), channel_id=1, source_target_pairs={{1,0},{2,1},{3,2},{4,3},{5,4},{6,5},{7,6},{8,7},{9,8},{10,9},{11,1... | collective-permute-start | bytes 1990664 | tf_op jit(solution)/shard_map/ppermute | solution.py:25
  138.7 19.0 %collective-permute-start.6 = (f32[1296,128]{1,0:T(8,128)S(1)}, f32[1296,128]{1,0:T(8,128)S(1)}, u32[]{:S(2)}, u32[]{:S(2)}) collective-permute-start(f32[1296,128]{1,0:T(8,128)S(1)} %get-tuple-element.12), channel_id=1, source_target_pairs={{0,1},{1,2},{2,3},{3,4},{4,5},{5,6},{6,7},{7,8},{8,9},{9,10},{10,1... | collective-permute-start | bytes 1990664 | tf_op jit(solution)/shard_map/ppermute | solution.py:23
  143.0 14.7 %collective-permute-start.7 = (f32[1296,128]{1,0:T(8,128)S(1)}, f32[1296,128]{1,0:T(8,128)S(1)}, u32[]{:S(2)}, u32[]{:S(2)}) collective-permute-start(f32[1296,128]{1,0:T(8,128)S(1)} %get-tuple-element.13), channel_id=1, source_target_pairs={{1,0},{2,1},{3,2},{4,3},{5,4},{6,5},{7,6},{8,7},{9,8},{10,9},{11,1... | collective-permute-start | bytes 1990664 | tf_op jit(solution)/shard_map/ppermute | solution.py:25
where the time goes:
time: 163 us; the launch traced here: 162 us
  other arithmetic  44.7 us (27%)
  waiting for transfers between devices  43 us (26%)
  starting transfers between devices  30 us (18%)
  local copies, waits for them, and re-layouts  22.7 us (14%)
  blocking collectives  20.8 us (13%)
    ppermute x4, waiting for transfers between devices, extended(): lax.ppermute(tail, axis, [(i, (i + 1) % count) for i in range(ends)])  37 us
    ppermute x4, starting transfers between devices, extended(): lax.ppermute(tail, axis, [(i, (i + 1) % count) for i in range(ends)])  15.9 us
    reduce_sum x2, other arithmetic, growth(): steep = jnp.sum(steep_weight[:, None] * state, axis=0)  13.6 us
    all_to_all x1, blocking collectives, body(): lax.all_to_all(point_buffer, 'geo', split_axis=0, concat_axis=0, tiled=True)  11.5 us
    all_to_all x1, blocking collectives, body(): lax.all_to_all(misfit_buffer, 'geo', split_axis=0, concat_axis=0, tiled=T...  9.27 us
    mul x1, other arithmetic, body(): product = adjoint * state * factor  8.15 us
    ppermute x4, starting transfers between devices, extended(): lax.ppermute(head, axis, [((i + 1) % count, i) for i in range(ends)])  7.87 us
    all_to_all x1, starting transfers between devices, body(): lax.all_to_all(model_slots, 'geo', split_axis=0, concat_axis=0, tiled=True)  6.21 us
  transfers between devices with their start and end apart: 9, of which 4 were waited for; matrix products, arithmetic and copies ran while one was open for 3% of the time, Pallas kernels for 0%

commit v1 on v0

v1 whole, which is shorter than its diff:
```python
import math

import jax
import jax.numpy as jnp
import numpy as np
from jax import lax
from jax.experimental import pallas as pl
from jax.experimental.pallas import tpu as pltpu
from jax.sharding import PartitionSpec as P

ND = 36
NF = 36
NB = 1296
W = 128
ROWS = 4
SUB = 8
GROUP = 72
TILES = GROUP // SUB
GROUPS = NB // GROUP
F32 = jnp.float32
LIMIT = 48 * 1024 * 1024

NORTH = (0, 1, 2, 4, 5, 6)
SOUTH = (2, 3, 4, 6, 7, 8)
FROM_WEST = (0, 4, 8)
FROM_EAST = (2, 6)


def direction_tables():
    angle = np.float32(2.0 * math.pi) * np.arange(ND, dtype=np.float32) / np.float32(ND)
    cosine = np.tile(np.cos(angle), 2)[:, None]
    sine = np.tile(np.sin(angle), 2)[:, None]
    lane = np.arange(W)[None, :]
    east = cosine >= 0
    west_ok = (lane > 0).astype(np.float32)
    east_ok = (lane < W - 1).astype(np.float32)
    one = np.ones((1, W), np.float32)
    forward = np.abs(cosine) * np.where(east, west_ok, east_ok)
    backward = np.abs(cosine) * np.where(east, east_ok, west_ok)
    return np.stack(
        [
            (np.abs(cosine) + np.abs(sine)) * one,
            np.abs(sine) * one,
            forward,
            backward,
            np.abs(cosine) * one,
        ]
    ).astype(np.float32)


def sublane():
    return lax.broadcasted_iota(jnp.int32, (SUB, W), 0)


def north_mask(tile, sub):
    return {2: sub < 2, 4: sub >= 4, 6: sub < 6}.get(tile)


def west_mask(tile, sub):
    return {1: sub < 1, 3: sub >= 3, 5: sub < 5, 7: sub >= 7}.get(tile)


def side(tile, sub, value, reverse):
    from_west = pltpu.roll(value, 1, 1) if tile not in (FROM_WEST if reverse else FROM_EAST) else None
    from_east = pltpu.roll(value, W - 1, 1) if tile not in (FROM_EAST if reverse else FROM_WEST) else None
    if from_east is None:
        return from_west
    if from_west is None:
        return from_east
    mask = west_mask(tile, sub)
    return jnp.where(mask, from_east, from_west) if reverse else jnp.where(mask, from_west, from_east)


def pick(tile, sub, north, south):
    mask = north_mask(tile, sub)
    if mask is None:
        return north if tile in NORTH else south
    if north is None:
        return jnp.where(mask, 0.0, south)
    if south is None:
        return jnp.where(mask, north, 0.0)
    return jnp.where(mask, north, south)


def speed(tile, sub, courant, group):
    first, second = courant[2 * group], courant[2 * group + 1]
    if tile == 4:
        return jnp.where(sub < 4, first, second)
    return jnp.full((SUB, W), first if tile < 4 else second, F32)


def weights(tile, sub, table, courant, group, reverse):
    rate = speed(tile, sub, courant, group)
    rows = pl.ds(tile * SUB, SUB)
    centre = 1.0 - rate * table[0, rows, :]
    along = rate * table[3 if reverse else 2, rows, :]
    across = rate * table[1, rows, :]
    return centre, along, across


def lanes(row):
    return pl.ds(row * W, W)


def total(value):
    return jnp.sum(value, axis=0, keepdims=True)


def whole(memory=pltpu.VMEM):
    return pl.BlockSpec(memory_space=memory)


def params():
    return pltpu.CompilerParams(vmem_limit_bytes=LIMIT)


def pack_kernel(field, north, south):
    sub = sublane()
    both = (sub < 2) | ((sub >= 4) & (sub < 6))
    for pair in range(field.shape[0] // 2):
        for row in range(2):
            def cell(half, tile, base):
                return field[2 * pair + half, pl.ds(tile * SUB, SUB), lanes(base + row)]

            def put(ref, tile, value):
                ref[pair, pl.ds(tile * SUB, SUB), lanes(row)] = value

            rest = []
            for half in range(2):
                sixth = cell(half, 6, 2)
                for place, tile in enumerate((0, 1, 5)):
                    put(north, half * 4 + place, cell(half, tile, 2))
                mixed = jnp.where(sub < 2, cell(half, 2, 2), jnp.where(sub < 4, sixth, cell(half, 4, 2)))
                put(north, half * 4 + 3, mixed)
                rest.append(sixth)
            put(north, 8, jnp.where(both, rest[0], pltpu.roll(rest[1], 2, 0)))
            rest = []
            for half in range(2):
                second = cell(half, 2, 0)
                for place, tile in enumerate((3, 7, 8)):
                    put(south, half * 4 + place, cell(half, tile, 0))
                put(south, half * 4 + 3, jnp.where(sub < 4, cell(half, 4, 0), second))
                rest.append(jnp.where(sub < 4, second, cell(half, 6, 0)))
            put(south, 8, jnp.where(both, pltpu.roll(rest[1], 2, 0), rest[0]))


def pack(field):
    steps = 3
    each = GROUPS // steps
    half = jax.ShapeDtypeStruct((GROUPS // 2, GROUP, 2 * W), F32)
    return pl.pallas_call(
        pack_kernel,
        grid=(steps,),
        in_specs=[pl.BlockSpec((each, GROUP, ROWS * W), lambda i: (i, 0, 0))],
        out_specs=[pl.BlockSpec((each // 2, GROUP, 2 * W), lambda i: (i, 0, 0))] * 2,
        out_shape=[half, half],
        compiler_params=params(),
        name="pack",
    )(field)


def unpack_north(halo, pair, half, row, sub):
    def get(tile):
        return halo[pair, pl.ds(tile * SUB, SUB), lanes(row)]

    mixed, last = get(half * 4 + 3), get(8)
    if half:
        last = pltpu.roll(last, 6, 0)
    return {
        0: get(half * 4),
        1: get(half * 4 + 1),
        2: mixed,
        4: mixed,
        5: get(half * 4 + 2),
        6: jnp.where((sub >= 2) & (sub < 4), mixed, last),
    }


def unpack_south(halo, pair, half, row, sub):
    def get(tile):
        return halo[pair, pl.ds(tile * SUB, SUB), lanes(row)]

    mixed, last = get(half * 4 + 3), get(8)
    if half:
        last = pltpu.roll(last, 6, 0)
    return {
        2: jnp.where(sub < 4, last, mixed),
        3: get(half * 4),
        4: mixed,
        6: last,
        7: get(half * 4 + 1),
        8: get(half * 4 + 2),
    }


def spread(row_ref, out):
    for start in range(0, NB, W):
        size = min(W, NB - start)
        chunk = row_ref[:, pl.ds(start, size)]
        square = jnp.broadcast_to(chunk, (W, size)) if size == W else jnp.broadcast_to(chunk, (W, size))
        out[pl.ds(start, size), :] = jnp.transpose(square)


def local_kernel(field, sea_in, wind, courant, rate_in, damp_in, steep_in, table, masked, rate, damp, steep, own, send_a, send_b):
    sub = sublane()
    spread(rate_in, rate)
    spread(damp_in, damp)
    spread(steep_in, steep)
    sea = [jnp.broadcast_to(sea_in[:, lanes(r)].astype(F32), (SUB, W)) for r in range(ROWS)]
    zero = jnp.zeros((SUB, W), F32)

    def step(group, sums):
        sums = list(sums)
        for tile in range(TILES):
            rows = pl.ds(tile * SUB, SUB)
            speeds = speed(tile, sub, courant, group)
            heavy = steep[pl.ds(pl.multiple_of(group * GROUP + tile * SUB, SUB), SUB), :]
            centre = heavy * (1.0 - speeds * table[0, rows, :])
            along = heavy * speeds * table[4, rows, :]
            across = heavy * speeds * table[1, rows, :]
            east = west_mask(tile, sub)
            if east is None:
                west_part, east_part = (along, None) if tile in FROM_WEST else (None, along)
            else:
                west_part, east_part = jnp.where(east, along, 0.0), jnp.where(east, 0.0, along)
            mask = north_mask(tile, sub)
            if mask is None:
                north_part, south_part = (across, None) if tile in NORTH else (None, across)
            else:
                north_part, south_part = jnp.where(mask, across, 0.0), jnp.where(mask, 0.0, across)
            for r in range(ROWS):
                cell = field[group, rows, lanes(r)] * sea[r]
                masked[group, rows, lanes(r)] = cell
                for place, part in enumerate((centre, west_part, east_part, north_part, south_part)):
                    if part is not None:
                        sums[place * ROWS + r] = sums[place * ROWS + r] + part * cell
        return tuple(sums)

    sums = lax.fori_loop(0, GROUPS, step, (zero,) * (5 * ROWS))
    sums = [total(value) for value in sums]
    lane = lax.broadcasted_iota(jnp.int32, (1, W), 1)
    local = []
    for r in range(ROWS):
        value = sums[r]
        value = value + jnp.where(lane > 0, pltpu.roll(sums[ROWS + r], 1, 1), 0.0)
        value = value + jnp.where(lane < W - 1, pltpu.roll(sums[2 * ROWS + r], W - 1, 1), 0.0)
        if r > 0:
            value = value + sums[3 * ROWS + r - 1]
        if r < ROWS - 1:
            value = value + sums[4 * ROWS + r + 1]
        local.append(value * sea[r][0:1, :])
    own[...] = jnp.zeros_like(own)
    for r in range(ROWS):
        own[0:1, lanes(r)] = local[r]
        own[1:2, lanes(r)] = sums[3 * ROWS + r]
        own[2:3, lanes(r)] = sums[4 * ROWS + r]

    def fill(ref, base, passing):
        ref[...] = jnp.zeros_like(ref)
        ref[0:2, :] = wind[:, pl.ds(base * W, 2 * W)]
        ref[2:3, :] = sea_in[:, pl.ds(base * W, 2 * W)].astype(F32)
        ref[3:4, :] = own[0:1, pl.ds(base * W, 2 * W)]
        ref[4:5, :] = own[passing : passing + 1, pl.ds(base * W, 2 * W)]

    even = lax.rem(lax.axis_index("geo"), 2) == 0

    @pl.when(even)
    def _():
        fill(send_a, 2, 1)
        fill(send_b, 0, 2)

    @pl.when(jnp.logical_not(even))
    def _():
        fill(send_a, 0, 2)
        fill(send_b, 2, 1)


def local(field, sea, wind, courant, rate, damp, steep, table):
    cells = (GROUPS, GROUP, ROWS * W)
    small = jax.ShapeDtypeStruct((SUB, 2 * W), F32)
    return pl.pallas_call(
        local_kernel,
        in_specs=[whole(), whole(), whole(), whole(pltpu.SMEM), whole(), whole(), whole(), whole()],
        out_specs=[whole()] * 7,
        out_shape=[
            pltpu.VMEM(cells, F32),
            pltpu.VMEM((NB, W), F32),
            pltpu.VMEM((NB, W), F32),
            pltpu.VMEM((NB, W), F32),
            pltpu.VMEM((SUB, ROWS * W), F32),
            small,
            small,
        ],
        compiler_params=params(),
        name="local",
    )(field, sea, wind, courant, rate, damp, steep, table)


def sort_kernel(owner, point, value, weight, out, flat, load, *, ranks, capacity):
    rows = owner.shape[0]
    flat[...] = jnp.zeros_like(flat)
    flat[0:1, :] = point[...].astype(F32)
    flat[1:2, :] = weight[...]
    columns = jnp.transpose(flat[...])
    load[...] = jnp.zeros_like(load)
    load[:, 0:NF] = value[...] * columns[:, 1:2]
    load[:, NF : NF + 1] = columns[:, 1:2]
    load[:, NF + 1 : NF + 2] = columns[:, 0:1]
    hits = (owner[...] == lax.broadcasted_iota(jnp.int32, (rows, ranks), 1)).astype(F32)
    before = lax.broadcasted_iota(jnp.int32, (rows, rows), 1) < lax.broadcasted_iota(jnp.int32, (rows, rows), 0)
    counts = jnp.dot(before.astype(F32), hits, preferred_element_type=F32)
    order = jnp.sum(counts * hits, axis=1, keepdims=True).astype(jnp.int32)
    target = owner[...] * capacity + order
    places = (target == lax.broadcasted_iota(jnp.int32, (rows, ranks * capacity), 1)).astype(F32)
    out[...] = lax.dot_general(
        places,
        load[...],
        (((0,), (0,)), ((), ())),
        precision=lax.Precision.HIGHEST,
        preferred_element_type=F32,
    )


def sort(owner, point, value, weight, ranks):
    rows = owner.shape[0]
    capacity = max(2, 2 * rows // ranks)

    def kernel(*refs):
        sort_kernel(*refs, ranks=ranks, capacity=capacity)

    return pl.pallas_call(
        kernel,
        in_specs=[whole()] * 4,
        out_specs=whole(),
        out_shape=jax.ShapeDtypeStruct((ranks * capacity, W), F32),
        scratch_shapes=[pltpu.VMEM((SUB, rows), F32), pltpu.VMEM((rows, W), F32)],
        compiler_params=params(),
        name="sort",
    )(owner, point.reshape(1, rows), value, weight.reshape(1, rows))


def place_kernel(arrived, out, weight):
    slots = arrived.shape[0]
    point = arrived[:, NF + 1 : NF + 2].astype(jnp.int32)
    hits = (point == lax.broadcasted_iota(jnp.int32, (slots, ROWS * W), 1)).astype(F32)
    sums = lax.dot_general(
        arrived[...],
        hits,
        (((0,), (0,)), ((), ())),
        precision=lax.Precision.HIGHEST,
        preferred_element_type=F32,
    )
    for f in range(NF):
        out[f // 2, f % 2 : f % 2 + 1, :] = sums[f : f + 1, :]
    weight[...] = jnp.broadcast_to(sums[NF : NF + 1, :], weight.shape)


def place(arrived):
    return pl.pallas_call(
        place_kernel,
        in_specs=[whole()],
        out_specs=[whole()] * 2,
        out_shape=[
            pltpu.VMEM((GROUPS, SUB, ROWS * W), F32),
            pltpu.VMEM((SUB, ROWS * W), F32),
        ],
        compiler_params=params(),
        name="place",
    )(arrived)


def sides(first, second):
    even = lax.rem(lax.axis_index("geo"), 2) == 0
    one, two = first[...], second[...]
    return jnp.where(even, two, one), jnp.where(even, one, two)


def forward_kernel(
    masked, from_south, from_north, aux_a, aux_b, own, wind, sea_in, courant, rate, damp, steep, table, wanted, gain,
    ahead, ahead_south, ahead_north, factor, lam, adjoint, state, send_a, send_b, moved,
):
    sub = sublane()
    south, north = sides(aux_a, aux_b)
    zero = jnp.zeros((SUB, W), F32)

    def full(value):
        return jnp.broadcast_to(value, (SUB, W))

    sea, wind0, steep0 = {}, {}, {}
    for r in range(ROWS):
        sea[r] = full(sea_in[:, lanes(r)].astype(F32))
        wind0[r] = full(wind[0:1, lanes(r)])
        steep0[r] = own[0:1, lanes(r)]
    for r in (0, 1):
        sea[r - 2] = full(south[2:3, r * W : (r + 1) * W])
        sea[r + 4] = full(north[2:3, r * W : (r + 1) * W])
    wind0[-1] = full(south[0:1, W : 2 * W])
    wind0[4] = full(north[0:1, 0:W])
    steep0[0] = steep0[0] + sea[0][0:1, :] * south[4:5, W : 2 * W]
    steep0[3] = steep0[3] + sea[3][0:1, :] * north[4:5, 0:W]
    steep0[-1] = south[3:4, W : 2 * W] + sea[-1][0:1, :] * own[2:3, lanes(0)]
    steep0[4] = north[3:4, 0:W] + sea[4][0:1, :] * own[1:2, lanes(3)]
    state[...] = jnp.zeros_like(state)
    for r in range(-1, 5):
        state[0:1, pl.ds((r + 1) * W, W)] = steep0[r]
        steep0[r] = full(steep0[r])

    def coefficients(group, tile):
        rows = pl.ds(pl.multiple_of(group * GROUP + tile * SUB, SUB), SUB)
        return rate[rows, :], damp[rows, :], steep[rows, :]

    def first(pair, sums):
        sums = list(sums)
        for half in range(2):
            group = 2 * pair + half
            ghosts = {
                -2: unpack_north(from_south, pair, half, 0, sub),
                -1: unpack_north(from_south, pair, half, 1, sub),
                4: unpack_south(from_north, pair, half, 0, sub),
                5: unpack_south(from_north, pair, half, 1, sub),
            }
            for tile in range(TILES):
                rows = pl.ds(tile * SUB, SUB)
                centre, along, across = weights(tile, sub, table, courant, group, False)
                grow, fade, heavy = coefficients(group, tile)
                cell = {r: masked[group, rows, lanes(r)] for r in range(ROWS)}
                for r, parts in ghosts.items():
                    cell[r] = parts[tile] * sea[r] if tile in parts else None

                def move(field, r):
                    value = centre * field[r] + along * side(tile, sub, field[r], False)
                    return sea[r] * (value + across * pick(tile, sub, field.get(r - 1), field.get(r + 1)))

                nxt = {}
                for r in range(-1, 5):
                    if cell[r] is None:
                        nxt[r] = None
                        continue
                    if r == -1:
                        value = centre * cell[r] + along * side(tile, sub, cell[r], False)
                        value = sea[r] * (value + across * cell[-2])
                    elif r == 4:
                        value = centre * cell[r] + along * side(tile, sub, cell[r], False)
                        value = sea[r] * (value + across * cell[5])
                    else:
                        value = move(cell, r)
                    nxt[r] = value * jnp.exp(grow * wind0[r] - fade * steep0[r])
                for r in range(ROWS):
                    ahead[group, rows, lanes(r)] = nxt[r]
                    value = move(nxt, r)
                    moved[group, rows, lanes(r)] = value
                    sums[r] = sums[r] + heavy * value
                if nxt[-1] is not None:
                    ahead_south[group, rows, :] = nxt[-1]
                if nxt[4] is not None:
                    ahead_north[group, rows, :] = nxt[4]
        return tuple(sums)

    sums = lax.fori_loop(0, GROUPS // 2, first, (zero,) * ROWS)
    steep1 = [total(value) for value in sums]
    for r in range(ROWS):
        state[1:2, pl.ds((r + 1) * W, W)] = steep1[r]
    steep1 = [full(value) for value in steep1]
    wind1 = [full(wind[1:2, lanes(r)]) for r in range(ROWS)]
    gains = [gain[0:1, lanes(r)] for r in range(ROWS)]

    def second(group, sums):
        sums = list(sums)
        parts = [[[None] * 3 for _ in range(ROWS)] for _ in range(2)]
        for tile in range(TILES):
            rows = pl.ds(tile * SUB, SUB)
            grow, fade, _ = coefficients(group, tile)
            for r in range(ROWS):
                value = jnp.exp(grow * wind1[r] - fade * steep1[r])
                factor[group, rows, lanes(r)] = value
                value = value * moved[group, rows, lanes(r)]
                for place, term in enumerate((value, grow * value, fade * value)):
                    for f in range(2):
                        if (f == 0 and tile > 4) or (f == 1 and tile < 4):
                            continue
                        mine = term
                        if tile == 4:
                            mine = jnp.where(sub < 4, term, 0.0) if f == 0 else jnp.where(sub < 4, 0.0, term)
                        old = parts[f][r][place]
                        parts[f][r][place] = mine if old is None else old + mine
        for r in range(ROWS):
            for f in range(2):
                mean, up, down = [total(value) for value in parts[f][r]]
                value = (gains[r] * (mean * (1.0 / ND)) - wanted[group, f : f + 1, lanes(r)]) * (1.0 / ND)
                lam[group, f : f + 1, lanes(r)] = value
                sums[r] = sums[r] + value * up
                sums[ROWS + r] = sums[ROWS + r] - value * down
        return tuple(sums)

    sums = lax.fori_loop(0, GROUPS, second, (jnp.zeros((1, W), F32),) * (2 * ROWS))
    for r in range(ROWS):
        state[2:3, pl.ds((r + 1) * W, W)] = sums[ROWS + r]
        state[3:4, pl.ds((r + 1) * W, W)] = sums[r]
    tend = [full(sums[ROWS + r]) for r in range(ROWS)]

    def third(group, sums):
        sums = list(sums)
        for tile in range(TILES):
            rows = pl.ds(tile * SUB, SUB)
            centre, along, across = weights(tile, sub, table, courant, group, True)
            grow, fade, heavy = coefficients(group, tile)
            cell = {}
            for r in range(ROWS):
                cell[r] = sea[r] * (
                    spread_lam(lam, group, tile, lanes(r), sub) * factor[group, rows, lanes(r)] + heavy * tend[r]
                )
            for r in range(ROWS):
                value = centre * cell[r] + along * side(tile, sub, cell[r], True)
                other = pick(tile, sub, cell.get(r + 1), cell.get(r - 1))
                if other is not None:
                    value = value + across * other
                value = sea[r] * value
                adjoint[group, rows, lanes(r)] = value
                value = value * ahead[group, rows, lanes(r)]
                sums[r] = sums[r] + grow * value
                sums[ROWS + r] = sums[ROWS + r] - fade * value
        return tuple(sums)

    sums = lax.fori_loop(0, GROUPS, third, (zero,) * (2 * ROWS))
    for r in range(ROWS):
        state[4:5, pl.ds((r + 1) * W, W)] = total(sums[ROWS + r])
        state[5:6, pl.ds((r + 1) * W, W)] = total(sums[r])

    def fill(ref, base):
        for f in range(NF):
            ref[f : f + 1, :] = lam[f // 2, f % 2 : f % 2 + 1, pl.ds(base * W, 2 * W)]
        here = pl.ds((base + 1) * W, 2 * W)
        ref[NF : NF + 1, :] = state[1:2, here]
        ref[NF + 1 : NF + 2, :] = state[2:3, here]
        ref[NF + 2 : NF + 3, :] = state[4:5, here]
        ref[NF + 3 : NF + 4, :] = state[4:5, here]

    even = lax.rem(lax.axis_index("geo"), 2) == 0

    @pl.when(even)
    def _():
        fill(send_a, 2)
        fill(send_b, 0)

    @pl.when(jnp.logical_not(even))
    def _():
        fill(send_a, 0)
        fill(send_b, 2)


def spread_lam(lam, group, tile, where, sub):
    if tile < 4:
        return lam[group, 0:1, where]
    if tile > 4:
        return lam[group, 1:2, where]
    return jnp.where(sub < 4, lam[group, 0:1, where], lam[group, 1:2, where])


def forward(*args):
    cells = (GROUPS, GROUP, ROWS * W)
    edge = (GROUPS, GROUP, W)
    small = jax.ShapeDtypeStruct((NF + 4, 2 * W), F32)
    specs = [whole()] * len(args)
    specs[8] = whole(pltpu.SMEM)
    return pl.pallas_call(
        forward_kernel,
        in_specs=specs,
        out_specs=[whole()] * 9,
        out_shape=[
            pltpu.VMEM(cells, F32),
            pltpu.VMEM(edge, F32),
            pltpu.VMEM(edge, F32),
            pltpu.VMEM(cells, F32),
            pltpu.VMEM((GROUPS, SUB, ROWS * W), F32),
            pltpu.VMEM(cells, F32),
            pltpu.VMEM((SUB, 6 * W), F32),
            small,
            small,
        ],
        scratch_shapes=[pltpu.VMEM(cells, F32)],
        compiler_params=params(),
        name="forward",
    )(*args)


def backward_kernel(
    ahead, ahead_south, ahead_north, factor, lam, adjoint, state, back_a, back_b, aux_a, aux_b, wind, sea_in, courant,
    rate, damp, steep, table, out, grad, ghost, low, high, fixed,
):
    sub = sublane()
    south, north = sides(aux_a, aux_b)
    back_south, back_north = sides(back_a, back_b)
    zero = jnp.zeros((SUB, W), F32)

    def full(value):
        return jnp.broadcast_to(value, (SUB, W))

    def held(place, r):
        return state[place : place + 1, pl.ds((r + 1) * W, W)]

    sea, wind0, wind1, steep0, steep1, tend1 = {}, {}, {}, {}, {}, {}
    for r in range(ROWS):
        sea[r] = full(sea_in[:, lanes(r)].astype(F32))
        wind0[r] = full(wind[0:1, lanes(r)])
        tend1[r] = full(held(2, r))
    for r in range(-1, 5):
        steep0[r] = full(held(0, r))
    for r in (0, 1):
        here = slice(r * W, (r + 1) * W)
        for place, aux, back in ((r - 2, south, back_south), (r + 4, north, back_north)):
            wind1[place] = full(aux[1:2, here])
            sea[place] = full(aux[2:3, here])
            steep1[place] = full(back[NF : NF + 1, here])
            tend1[place] = full(back[NF + 1 : NF + 2, here])
    wind0[-1] = full(south[0:1, W : 2 * W])
    wind0[4] = full(north[0:1, 0:W])
    for f in range(NF):
        ghost[f // 2, f % 2 : f % 2 + 1, 0 : 2 * W] = back_south[f : f + 1, :]
        ghost[f // 2, f % 2 : f % 2 + 1, 2 * W : 4 * W] = back_north[f : f + 1, :]

    def coefficients(group, tile):
        rows = pl.ds(pl.multiple_of(group * GROUP + tile * SUB, SUB), SUB)
        return rate[rows, :], damp[rows, :], steep[rows, :]

    def first(group, sums):
        sums = list(sums)
        for tile in range(TILES):
            rows = pl.ds(tile * SUB, SUB)
            centre, along, across = weights(tile, sub, table, courant, group, True)
            grow, fade, heavy = coefficients(group, tile)

            def outer(r, place):
                value = spread_lam(ghost, group, tile, lanes(place), sub) * jnp.exp(grow * wind1[r] - fade * steep1[r])
                return sea[r] * (value + heavy * tend1[r])

            def inner(r):
                value = spread_lam(lam, group, tile, lanes(r), sub) * factor[group, rows, lanes(r)]
                return sea[r] * (value + heavy * tend1[r])

            def side_of(near, far, edge, place, mine, keep, behind, slot):
                value = centre * near + along * side(tile, sub, near, True)
                keep[group, rows, :] = sea[edge] * (value + across * far)
                value = sea[mine] * (across * near)
                value = pick(tile, sub, None, value) if edge < 0 else pick(tile, sub, value, None)
                fixed[group, rows, lanes(place)] = value
                value = value * ahead[group, rows, lanes(mine)]
                sums[slot] = sums[slot] + grow * value
                sums[slot + 1] = sums[slot + 1] - fade * value

            if tile in SOUTH:
                side_of(outer(-1, 1), outer(-2, 0), -1, 0, 0, low, None, 0)
            if tile in NORTH:
                side_of(outer(4, 2), outer(5, 3), 4, 1, 3, high, None, 2)
            if tile in NORTH:
                value = across * inner(0) * ahead_south[group, rows, :]
                value = pick(tile, sub, value, None)
                sums[4] = sums[4] - fade * value
            if tile in SOUTH:
                value = across * inner(3) * ahead_north[group, rows, :]
                value = pick(tile, sub, None, value)
                sums[5] = sums[5] - fade * value
        return tuple(sums)

    sums = lax.fori_loop(0, GROUPS, first, (zero,) * 6)
    sums = [total(value) for value in sums]
    tend0 = {r: held(4, r) for r in range(ROWS)}
    tend0[0] = tend0[0] + sums[1]
    tend0[3] = tend0[3] + sums[3]
    tend0[-1] = back_south[NF + 2 : NF + 3, W : 2 * W] + sea[-1][0:1, :] * sums[4]
    tend0[4] = back_north[NF + 2 : NF + 3, 0:W] + sea[4][0:1, :] * sums[5]
    for r in range(ROWS):
        value = held(5, r)
        if r == 0:
            value = value + sums[0]
        if r == 3:
            value = value + sums[2]
        grad[0:1, lanes(r)] = value
        grad[1:2, lanes(r)] = held(3, r)
    tend0 = {r: full(value) for r, value in tend0.items()}

    def second(group, carry):
        for tile in range(TILES):
            rows = pl.ds(tile * SUB, SUB)
            centre, along, across = weights(tile, sub, table, courant, group, True)
            grow, fade, heavy = coefficients(group, tile)
            cell = {}
            for r in range(-1, 5):
                if r == -1:
                    if tile not in SOUTH:
                        continue
                    value = low[group, rows, :]
                elif r == 4:
                    if tile not in NORTH:
                        continue
                    value = high[group, rows, :]
                else:
                    value = adjoint[group, rows, lanes(r)]
                    if r == 0 and tile in SOUTH:
                        value = value + fixed[group, rows, lanes(0)]
                    if r == 3 and tile in NORTH:
                        value = value + fixed[group, rows, lanes(1)]
                value = value * jnp.exp(grow * wind0[r] - fade * steep0[r]) + heavy * tend0[r]
                cell[r] = sea[r] * value
            for r in range(ROWS):
                value = centre * cell[r] + along * side(tile, sub, cell[r], True)
                value = value + across * pick(tile, sub, cell.get(r + 1), cell.get(r - 1))
                out[group, rows, lanes(r)] = sea[r] * value
        return carry

    lax.fori_loop(0, GROUPS, second, 0)


def backward(*args):
    cells = (GROUPS, GROUP, ROWS * W)
    edge = (GROUPS, GROUP, W)
    specs = [whole()] * len(args)
    specs[13] = whole(pltpu.SMEM)
    return pl.pallas_call(
        backward_kernel,
        in_specs=specs,
        out_specs=[whole()] * 2,
        out_shape=[jax.ShapeDtypeStruct(cells, F32), jax.ShapeDtypeStruct((2, ROWS * W), F32)],
        scratch_shapes=[
            pltpu.VMEM((GROUPS, SUB, ROWS * W), F32),
            pltpu.VMEM(edge, F32),
            pltpu.VMEM(edge, F32),
            pltpu.VMEM((GROUPS, GROUP, 2 * W), F32),
        ],
        compiler_params=params(),
        name="backward",
    )(*args)


def swaps(count):
    near = [(i, i ^ 1) for i in range(count)]
    far = []
    for i in range(1, count - 1, 2):
        far += [(i, i + 1), (i + 1, i)]
    return near, far


def body(
    initial_spectrum,
    wind_forcing,
    sea_mask,
    courant,
    input_rate,
    damping,
    steep_weight,
    obs_owner,
    obs_point,
    obs_value,
    obs_weight,
):
    count = lax.axis_size("geo")
    near, far = swaps(count)
    table = jnp.asarray(direction_tables())
    field = initial_spectrum.reshape(GROUPS, GROUP, ROWS * W)
    sea = sea_mask.reshape(1, ROWS * W)
    north, south = pack(field)
    from_south = lax.ppermute(north, "geo", [(i, i + 1) for i in range(count - 1)])
    from_north = lax.ppermute(south, "geo", [(i + 1, i) for i in range(count - 1)])
    masked, rate, damp, steep, own, send_a, send_b = local(
        field,
        sea,
        wind_forcing,
        courant,
        input_rate.reshape(1, NB),
        damping.reshape(1, NB),
        steep_weight.reshape(1, NB),
        table,
    )
    aux_b = lax.ppermute(send_b, "geo", far)
    aux_a = lax.ppermute(send_a, "geo", near)
    slots = sort(obs_owner, obs_point, obs_value, obs_weight, count)
    arrived = lax.all_to_all(slots, "geo", split_axis=0, concat_axis=0, tiled=True)
    wanted, gain = place(arrived)
    ahead, ahead_south, ahead_north, factor, lam, adjoint, state, send_a, send_b = forward(
        masked, from_south, from_north, aux_a, aux_b, own, wind_forcing, sea, courant, rate, damp, steep, table, wanted, gain
    )
    back_b = lax.ppermute(send_b, "geo", far)
    back_a = lax.ppermute(send_a, "geo", near)
    out, grad = backward(
        ahead, ahead_south, ahead_north, factor, lam, adjoint, state, back_a, back_b, aux_a, aux_b, wind_forcing, sea,
        courant, rate, damp, steep, table,
    )
    return grad, out.reshape(NB, ROWS * W)


def solution(mesh):
    return jax.shard_map(
        body,
        mesh=mesh,
        in_specs=(
            P(None, ("groups", "geo")),
            P(None, ("groups", "geo")),
            P(("groups", "geo")),
            P(),
            P(),
            P(),
            P(),
            P(("groups", "geo"), None),
            P(("groups", "geo")),
            P(("groups", "geo"), None),
            P(("groups", "geo")),
        ),
        out_specs=(P(None, ("groups", "geo")), P(None, ("groups", "geo"))),
        check_vma=False,
    )
```

time: 163 us -> 70.4 us (0.43)
  other arithmetic: 44.7 us -> 0 us
  waiting for transfers between devices: 43 us -> 1.89 us
  Pallas kernels: 0 us -> 30.9 us
  blocking collectives: 20.8 us -> 0 us
  starting transfers between devices: 30 us -> 20.8 us
  local copies, waits for them, and re-layouts: 22.7 us -> 15.2 us
    ppermute x8 -> x6, waiting for transfers between devices: 37 us -> 1.88 us  [the longest x1 1.87 us: body(): back_b = lax.ppermute(send_b, 'geo', far)]
    pallas_call x0 -> x6, Pallas kernels: none -> 30.9 us  [the longest x1 15.9 us: forward(): pl.pallas_call(forward_kernel, in_specs=specs, out_specs=[whole()] * 9, o...]
    all_to_all x2 -> x0, blocking collectives: 20.8 us -> none  [the longest x1 11.5 us: body(): lax.all_to_all(point_buffer, 'geo', split_axis=0, concat_axis=0, tiled=True)]
    mul x8 -> x0, other arithmetic: 19.7 us -> none  [the longest x1 8.15 us: body(): product = adjoint * state * factor]
    reduce_sum x6 -> x0, other arithmetic: 19.1 us -> none  [the longest x2 13.6 us: growth(): steep = jnp.sum(steep_weight[:, None] * state, axis=0)]
    unnamed x30 -> x72, local copies, waits for them, and re-layouts: 4.91 us -> 15.2 us
    ppermute x8 -> x6, starting transfers between devices: 23.8 us -> 14.4 us  [the longest x1 4.51 us: body(): lax.ppermute(north, 'geo', [(i, i + 1) for i in range(count - 1)])]
    reshape x2 -> x3, local copies, waits for them, and re-layouts: 7.71 us -> 0.02 us  [the longest x1 0.01 us: body(): damping.reshape(1, NB)]
  transfers between devices with their start and end apart: 9 -> 7, of which waited for: 4 -> 1; matrix products, arithmetic and copies ran while one was open for 3% -> 0% of each run, Pallas kernels for 0% -> 8%
where the time goes in v1:
time: 70.4 us; the launch traced here: 69.8 us
  Pallas kernels  30.9 us (44%)
  starting transfers between devices  20.8 us (30%)
  local copies, waits for them, and re-layouts  15.2 us (22%)
  waiting for transfers between devices  1.89 us (3%)
  between operations  1.01 us (1%)
    pallas_call x1, Pallas kernels, forward(): pl.pallas_call(forward_kernel, in_specs=specs, out_specs=[whole()] * 9, o...  15.9 us
    unnamed x72, local copies, waits for them, and re-layouts  15.2 us
    pallas_call x1, Pallas kernels, backward(): pl.pallas_call(backward_kernel, in_specs=specs, out_specs=[whole()] * 2,...  9.39 us
    all_to_all x1, starting transfers between devices, body(): lax.all_to_all(slots, 'geo', split_axis=0, concat_axis=0, tiled=True)  6.45 us
    ppermute x1, starting transfers between devices, body(): lax.ppermute(north, 'geo', [(i, i + 1) for i in range(count - 1)])  4.51 us
    ppermute x1, starting transfers between devices, body(): back_b = lax.ppermute(send_b, 'geo', far)  4.28 us
    pallas_call x1, Pallas kernels, local(): pl.pallas_call(local_kernel, in_specs=[whole(), whole(), whole(), whole(p...  3.58 us
    ppermute x1, starting transfers between devices, body(): aux_b = lax.ppermute(send_b, 'geo', far)  3.57 us
  transfers between devices with their start and end apart: 7, of which 1 were waited for; matrix products, arithmetic and copies ran while one was open for 0% of the time, Pallas kernels for 8%

profile of v1, /device:TPU:1, one launch (start us, length us, event | category | flops | bytes accessed | tf_op | source)
XLA Modules:
  0.0 69.8 jit_solution(2960118749899338315)
XLA Ops:
  0.7 0.0 copy-start.24
  0.7 0.0 copy-start
  0.7 1.8 %copy-done = f32[1296,512]{1,0:T(8,128)S(1)} copy-done((f32[1296,512]{1,0:T(8,128)S(1)}, f32[1296,512]{1,0:T(8,128)}, u32[]{:S(2)}) %copy-start) | copy-done | bytes 2654232
  2.5 0.0 copy-start.11
  2.5 0.0 copy-start.14
  2.5 0.0 copy-start.20
  2.5 0.2 pack.1
  2.7 4.5 %collective-permute-start = (f32[9,72,256]{2,1,0:T(8,128)S(1)}, f32[9,72,256]{2,1,0:T(8,128)S(1)}, u32[]{:S(2)}, u32[]{:S(2)}) collective-permute-start(f32[9,72,256]{2,1,0:T(8,128)S(1)} %get-tuple-element.25), channel_id=1, source_target_pairs={{0,1},{1,2},{2,3},{3,4},{4,5},{5,6},{6,7},{7,8},{8,9},{9,10},{10,1... | collective-permute-start | bytes 1990664 | tf_op jit(solution)/shard_map/ppermute | solution.py:761
  7.2 1.9 %collective-permute-start.1 = (f32[9,72,256]{2,1,0:T(8,128)S(1)}, f32[9,72,256]{2,1,0:T(8,128)S(1)}, u32[]{:S(2)}, u32[]{:S(2)}) collective-permute-start(f32[9,72,256]{2,1,0:T(8,128)S(1)} %get-tuple-element.26), channel_id=1, source_target_pairs={{1,0},{2,1},{3,2},{4,3},{5,4},{6,5},{7,6},{8,7},{9,8},{10,9},{11,1... | collective-permute-start | bytes 1990664 | tf_op jit(solution)/shard_map/ppermute | solution.py:762
  9.1 0.0 copy-done.34
  9.1 0.1 copy.14.refs_0_
  9.2 0.1 copy.15.refs_2_
  9.4 1.4 %sort.1 = f32[256,128]{1,0:T(8,128)} custom-call(s32[128,1]{1,0:T(8,128)S(1)} %copy.14.refs_0_, s32[1,128]{1,0:T(1,128)S(1)} %bitcast.13, f32[128,36]{1,0:T(8,128)S(1)} %copy.15.refs_2_, f32[1,128]{1,0:T(1,128)S(1)} %bitcast.14), custom_call_target="tpu_custom_call" | custom-call | tf_op jit(solution)/shard_map/sort/pallas_call | solution.py:331
  10.7 6.5 %all-to-all-start = ((f32[16,16,128]{2,1,0:T(8,128)}), f32[16,16,128]{2,1,0:T(8,128)S(1)}, u32[]{:S(2)}, u32[]{:S(2)}) async-start(f32[16,16,128]{2,1,0:T(8,128)} %bitcast.4), calls=%async_computation | async-start | bytes 262144 | tf_op jit(solution)/shard_map/all_to_all | solution.py:776
  17.3 3.6 %local.1 = (f32[18,72,512]{2,1,0:T(8,128)S(1)}, f32[1296,128]{1,0:T(8,128)S(1)}, f32[1296,128]{1,0:T(8,128)S(1)}, f32[1296,128]{1,0:T(8,128)S(1)}, f32[8,512]{1,...) custom-call(f32[18,72,512]{2,1,0:T(8,128)} %bitcast.7, s32[1,512]{1,0:T(1,128)S(1)} %bitcast.11, ...), custom_call_target="tpu_custom_call" | custom-call | tf_op jit(solution)/shard_map/local/pallas_call | solution.py:281
  20.9 0.0 copy-start.1
  20.9 1.5 %copy-done.1 = f32[18,72,512]{2,1,0:T(8,128)} copy-done((f32[18,72,512]{2,1,0:T(8,128)}, f32[18,72,512]{2,1,0:T(8,128)S(1)}, u32[]{:S(2)}) %copy-start.1) | copy-done | bytes 2654232
  22.4 0.9 %copy-done.5 = f32[1296,128]{1,0:T(8,128)} copy-done((f32[1296,128]{1,0:T(8,128)}, f32[1296,128]{1,0:T(8,128)S(1)}, u32[]{:S(2)}) %copy-start.5) | copy-done | bytes 663576
  23.3 0.8 %copy-done.7 = f32[1296,128]{1,0:T(8,128)} copy-done((f32[1296,128]{1,0:T(8,128)}, f32[1296,128]{1,0:T(8,128)S(1)}, u32[]{:S(2)}) %copy-start.7) | copy-done | bytes 663576
  24.1 0.9 %copy-done.9 = f32[1296,128]{1,0:T(8,128)} copy-done((f32[1296,128]{1,0:T(8,128)}, f32[1296,128]{1,0:T(8,128)S(1)}, u32[]{:S(2)}) %copy-start.9) | copy-done | bytes 663576
  25.0 0.6 copy-done.22
  25.6 0.1 collective-permute-start.2
  25.7 3.6 %collective-permute-start.3 = (f32[8,256]{1,0:T(8,128)S(1)}, f32[8,256]{1,0:T(8,128)S(1)}, u32[]{:S(2)}, u32[]{:S(2)}) collective-permute-start(f32[8,256]{1,0:T(8,128)S(1)} %get-tuple-element.28), channel_id=1, source_target_pairs={{1,2},{2,1},{3,4},{4,3},{5,6},{6,5},{7,8},{8,7},{9,10},{10,9},{11,... | collective-permute-start | bytes 24584 | tf_op jit(solution)/shard_map/ppermute | solution.py:773
  29.3 0.0 all-to-all-done
  29.3 0.5 place.1
  29.8 0.7 %copy-done.13 = f32[18,8,512]{2,1,0:T(8,128)} copy-done((f32[18,8,512]{2,1,0:T(8,128)}, f32[18,8,512]{2,1,0:T(8,128)S(1)}, u32[]{:S(2)}) %copy-start.13) | copy-done | bytes 294936
  30.6 0.6 copy-done.23
  31.2 0.0 collective-permute-done.2.aux_a
  31.2 0.0 collective-permute-done.3.aux_b
  31.2 0.0 collective-permute-done.from_south
  31.2 0.0 collective-permute-done.1.from_north
  31.2 0.5 copy-done.16
  31.8 0.3 copy-done.28
  32.1 0.3 copy-done.29
  32.3 0.0 copy-start.15
  32.3 0.0 copy-start.21
  32.3 0.0 copy-start.25
  32.4 15.9 %forward.1 = (f32[18,72,512]{2,1,0:T(8,128)S(1)}, f32[18,72,128]{2,1,0:T(8,128)S(1)}, f32[18,72,128]{2,1,0:T(8,128)S(1)}, f32[18,72,512]{2,1,0:T(8,128)S(1)}, f3...) custom-call(f32[18,72,512]{2,1,0:T(8,128)} %copy-done.1, ...), custom_call_target="tpu_custom_call" | custom-call | tf_op jit(solution)/shard_map/forward/pallas_call | solution.py:565
  48.2 1.5 %copy-done.2 = f32[18,72,512]{2,1,0:T(8,128)} copy-done((f32[18,72,512]{2,1,0:T(8,128)}, f32[18,72,512]{2,1,0:T(8,128)S(1)}, u32[]{:S(2)}) %copy-start.2) | copy-done | bytes 2654232
  49.7 1.5 %copy-done.3 = f32[18,72,512]{2,1,0:T(8,128)} copy-done((f32[18,72,512]{2,1,0:T(8,128)}, f32[18,72,512]{2,1,0:T(8,128)S(1)}, u32[]{:S(2)}) %copy-start.3) | copy-done | bytes 2654232
  51.3 1.5 %copy-done.4 = f32[18,72,512]{2,1,0:T(8,128)} copy-done((f32[18,72,512]{2,1,0:T(8,128)}, f32[18,72,512]{2,1,0:T(8,128)S(1)}, u32[]{:S(2)}) %copy-start.4) | copy-done | bytes 2654232
  52.8 0.0 collective-permute-start.4
  52.8 4.3 %collective-permute-start.5 = (f32[40,256]{1,0:T(8,128)}, f32[40,256]{1,0:T(8,128)S(1)}, u32[]{:S(2)}, u32[]{:S(2)}) collective-permute-start(f32[40,256]{1,0:T(8,128)} %get-tuple-element.43), channel_id=1, source_target_pairs={{1,2},{2,1},{3,4},{4,3},{5,6},{6,5},{7,8},{8,7},{9,10},{10,9},{11,... | collective-permute-start | bytes 122888 | tf_op jit(solution)/shard_map/ppermute | solution.py:781
  57.1 0.0 collective-permute-done.4.back_a
  57.1 1.9 %collective-permute-done.5.back_b = f32[40,256]{1,0:T(8,128)S(1)} collective-permute-done((f32[40,256]{1,0:T(8,128)}, f32[40,256]{1,0:T(8,128)S(1)}, u32[]{:S(2)}, u32[]{:S(2)}) %collective-permute-start.5) | collective-permute-done | bytes 40992 | tf_op jit(solution)/shard_map/ppermute | solution.py:781
  59.0 0.7 copy-done.17
  59.7 0.7 copy-done.19
  60.4 9.4 %backward.1 = (f32[18,72,512]{2,1,0:T(8,128)}, f32[2,512]{1,0:T(2,128)}) custom-call(f32[18,72,512]{2,1,0:T(8,128)} %copy-done.2, f32[18,72,128]{2,1,0:T(8,128)S(1)} %get-tuple-element.36.ahead_south, f32[18,72,128]{2,1,0:T(8,128)S(1)} %get-tuple-element.37.ahead_north, f32[18,72,512]{2,1,0:T(8,128)} %copy-done.3, f32[18,8,512]{2,1,0:T(8,128)S(1)} %get-tuple-element.39.lam, ...), custom_call_target="tpu_custom_call" | custom-call | tf_op jit(solution)/shard_map/backward/pallas_call | solution.py:718
  (47 shorter events, 0.1 us)
Async XLA Ops:
  0.6 8.7 %copy-start.27 = (f32[128]{0:T(128)S(1)}, f32[128]{0:T(128)}, u32[]{:S(2)}) copy-start(f32[128]{0:T(128)} %param.22) | copy-start | bytes 1540
  0.6 8.7 %copy-start.26 = (s32[128]{0:T(128)S(1)}, s32[128]{0:T(128)}, u32[]{:S(2)}) copy-start(s32[128]{0:T(128)} %param.20) | copy-start | bytes 1540
  0.7 16.6 %copy-start.24 = (f32[36]{0:T(128)S(1)}, f32[36]{0:T(128)}, u32[]{:S(2)}) copy-start(f32[36]{0:T(128)} %courant.5) | copy-start | bytes 436
  0.7 1.8 %copy-start = (f32[1296,512]{1,0:T(8,128)S(1)}, f32[1296,512]{1,0:T(8,128)}, u32[]{:S(2)}) copy-start(f32[1296,512]{1,0:T(8,128)} %param.12) | copy-start | bytes 7962628
  2.4 6.7 %copy-start.34 = (s32[128,1]{0,1:T(1,128)S(1)}, s32[128,1]{0,1:T(1,128)}, u32[]{:S(2)}) copy-start(s32[128,1]{0,1:T(1,128)} %param.19) | copy-start | bytes 1540
  2.4 6.8 %copy-start.30 = (f32[128,36]{0,1:T(8,128)S(1)}, f32[128,36]{0,1:T(8,128)}, u32[]{:S(2)}) copy-start(f32[128,36]{0,1:T(8,128)} %param.21) | copy-start | bytes 55300
  2.4 14.7 %copy-start.31 = (f32[1296]{0:T(1024)S(1)}, f32[1296]{0:T(1024)}, u32[]{:S(2)}) copy-start(f32[1296]{0:T(1024)} %param.16) | copy-start | bytes 15556
  2.4 14.8 %copy-start.32 = (f32[1296]{0:T(1024)S(1)}, f32[1296]{0:T(1024)}, u32[]{:S(2)}) copy-start(f32[1296]{0:T(1024)} %param.17) | copy-start | bytes 15556
  2.4 14.8 %copy-start.33 = (f32[1296]{0:T(1024)S(1)}, f32[1296]{0:T(1024)}, u32[]{:S(2)}) copy-start(f32[1296]{0:T(1024)} %param.18) | copy-start | bytes 15556
  2.5 14.8 %copy-start.11 = (f32[5,72,128]{2,1,0:T(8,128)S(1)}, f32[5,72,128]{2,1,0:T(8,128)}, u32[]{:S(2)}) copy-start(f32[5,72,128]{2,1,0:T(8,128)} %constant.2.clone.table) | copy-start | bytes 552964
  2.5 14.8 %copy-start.14 = (f32[2,512]{1,0:T(2,128)S(1)}, f32[2,512]{1,0:T(2,128)}, u32[]{:S(2)}) copy-start(f32[2,512]{1,0:T(2,128)} %wind.5) | copy-start | bytes 12292
  2.5 14.8 %copy-start.20 = (s32[512]{0:T(512)S(1)}, s32[512]{0:T(512)}, u32[]{:S(2)}) copy-start(s32[512]{0:T(512)} %param.14) | copy-start | bytes 6148
  2.7 28.5 %collective-permute-start = (f32[9,72,256]{2,1,0:T(8,128)S(1)}, f32[9,72,256]{2,1,0:T(8,128)S(1)}, u32[]{:S(2)}, u32[]{:S(2)}) collective-permute-start(f32[9,72,256]{2,1,0:T(8,128)S(1)} %get-tuple-element.25), channel_id=1, source_target_pairs={{0,1},{1,2},{2,3},{3,4},{4,5},{5,6},{6,7},{7,8},{8,9},{9,10},{10,1... | collective-permute-start | bytes 1990664 | tf_op jit(solution)/shard_map/ppermute | solution.py:761
  7.2 24.0 %collective-permute-start.1 = (f32[9,72,256]{2,1,0:T(8,128)S(1)}, f32[9,72,256]{2,1,0:T(8,128)S(1)}, u32[]{:S(2)}, u32[]{:S(2)}) collective-permute-start(f32[9,72,256]{2,1,0:T(8,128)S(1)} %get-tuple-element.26), channel_id=1, source_target_pairs={{1,0},{2,1},{3,2},{4,3},{5,4},{6,5},{7,6},{8,7},{9,8},{10,9},{11,1... | collective-permute-start | bytes 1990664 | tf_op jit(solution)/shard_map/ppermute | solution.py:762
  10.7 18.6 %all-to-all-start = ((f32[16,16,128]{2,1,0:T(8,128)}), f32[16,16,128]{2,1,0:T(8,128)S(1)}, u32[]{:S(2)}, u32[]{:S(2)}) async-start(f32[16,16,128]{2,1,0:T(8,128)} %bitcast.4), calls=%async_computation | async-start | bytes 262144 | tf_op jit(solution)/shard_map/all_to_all | solution.py:776
  20.9 1.5 %copy-start.1 = (f32[18,72,512]{2,1,0:T(8,128)}, f32[18,72,512]{2,1,0:T(8,128)S(1)}, u32[]{:S(2)}) copy-start(f32[18,72,512]{2,1,0:T(8,128)S(1)} %get-tuple-element.24.masked) | copy-start | bytes 7962628
  22.4 0.9 %copy-start.5 = (f32[1296,128]{1,0:T(8,128)}, f32[1296,128]{1,0:T(8,128)S(1)}, u32[]{:S(2)}) copy-start(f32[1296,128]{1,0:T(8,128)S(1)} %get-tuple-element.30.rate) | copy-start | bytes 1990660
  23.3 0.8 %copy-start.7 = (f32[1296,128]{1,0:T(8,128)}, f32[1296,128]{1,0:T(8,128)S(1)}, u32[]{:S(2)}) copy-start(f32[1296,128]{1,0:T(8,128)S(1)} %get-tuple-element.31.damp) | copy-start | bytes 1990660
  24.1 0.9 %copy-start.9 = (f32[1296,128]{1,0:T(8,128)}, f32[1296,128]{1,0:T(8,128)S(1)}, u32[]{:S(2)}) copy-start(f32[1296,128]{1,0:T(8,128)S(1)} %get-tuple-element.32.steep) | copy-start | bytes 1990660
  25.0 0.6 copy-start.22
  25.6 5.6 %collective-permute-start.2 = (f32[8,256]{1,0:T(8,128)S(1)}, f32[8,256]{1,0:T(8,128)S(1)}, u32[]{:S(2)}, u32[]{:S(2)}) collective-permute-start(f32[8,256]{1,0:T(8,128)S(1)} %get-tuple-element.27), channel_id=1, source_target_pairs={{0,1},{1,0},{2,3},{3,2},{4,5},{5,4},{6,7},{7,6},{8,9},{9,8},{10,11... | collective-permute-start | bytes 24584 | tf_op jit(solution)/shard_map/ppermute | solution.py:774
  25.7 5.5 %collective-permute-start.3 = (f32[8,256]{1,0:T(8,128)S(1)}, f32[8,256]{1,0:T(8,128)S(1)}, u32[]{:S(2)}, u32[]{:S(2)}) collective-permute-start(f32[8,256]{1,0:T(8,128)S(1)} %get-tuple-element.28), channel_id=1, source_target_pairs={{1,2},{2,1},{3,4},{4,3},{5,6},{6,5},{7,8},{8,7},{9,10},{10,9},{11,... | collective-permute-start | bytes 24584 | tf_op jit(solution)/shard_map/ppermute | solution.py:773
  29.8 0.8 %copy-start.13 = (f32[18,8,512]{2,1,0:T(8,128)}, f32[18,8,512]{2,1,0:T(8,128)S(1)}, u32[]{:S(2)}) copy-start(f32[18,8,512]{2,1,0:T(8,128)S(1)} %get-tuple-element.33.wanted) | copy-start | bytes 884740
  30.6 0.6 copy-start.23
  31.2 0.6 copy-start.16
  31.2 0.6 copy-start.18
  31.2 0.8 %copy-start.28 = (f32[9,72,256]{2,1,0:T(8,128)}, f32[9,72,256]{2,1,0:T(8,128)S(1)}, u32[]{:S(2)}) copy-start(f32[9,72,256]{2,1,0:T(8,128)S(1)} %collective-permute-done.from_south) | copy-start | bytes 1990660
  31.2 1.1 %copy-start.29 = (f32[9,72,256]{2,1,0:T(8,128)}, f32[9,72,256]{2,1,0:T(8,128)S(1)}, u32[]{:S(2)}) copy-start(f32[9,72,256]{2,1,0:T(8,128)S(1)} %collective-permute-done.1.from_north) | copy-start | bytes 1990660
  32.3 26.7 %copy-start.6 = (f32[1296,128]{1,0:T(8,128)S(1)}, f32[1296,128]{1,0:T(8,128)}, u32[]{:S(2)}) copy-start(f32[1296,128]{1,0:T(8,128)} %copy-done.5) | copy-start | bytes 1990660
  32.3 26.7 %copy-start.8 = (f32[1296,128]{1,0:T(8,128)S(1)}, f32[1296,128]{1,0:T(8,128)}, u32[]{:S(2)}) copy-start(f32[1296,128]{1,0:T(8,128)} %copy-done.7) | copy-start | bytes 1990660
  32.3 26.7 %copy-start.10 = (f32[1296,128]{1,0:T(8,128)S(1)}, f32[1296,128]{1,0:T(8,128)}, u32[]{:S(2)}) copy-start(f32[1296,128]{1,0:T(8,128)} %copy-done.9) | copy-start | bytes 1990660
  32.3 26.7 %copy-start.12 = (f32[5,72,128]{2,1,0:T(8,128)S(1)}, f32[5,72,128]{2,1,0:T(8,128)}, u32[]{:S(2)}) copy-start(f32[5,72,128]{2,1,0:T(8,128)} %constant.2.clone.table) | copy-start | bytes 552964
  32.3 26.7 %copy-start.15 = (f32[2,512]{1,0:T(2,128)S(1)}, f32[2,512]{1,0:T(2,128)}, u32[]{:S(2)}) copy-start(f32[2,512]{1,0:T(2,128)} %wind.5) | copy-start | bytes 12292
  32.3 26.7 %copy-start.21 = (s32[512]{0:T(512)S(1)}, s32[512]{0:T(512)}, u32[]{:S(2)}) copy-start(s32[512]{0:T(512)} %param.14) | copy-start | bytes 6148
  32.3 26.7 %copy-start.25 = (f32[36]{0:T(128)S(1)}, f32[36]{0:T(128)}, u32[]{:S(2)}) copy-start(f32[36]{0:T(128)} %courant.5) | copy-start | bytes 436
  48.2 1.5 %copy-start.2 = (f32[18,72,512]{2,1,0:T(8,128)}, f32[18,72,512]{2,1,0:T(8,128)S(1)}, u32[]{:S(2)}) copy-start(f32[18,72,512]{2,1,0:T(8,128)S(1)} %get-tuple-element.35.ahead) | copy-start | bytes 7962628
  49.7 1.5 %copy-start.3 = (f32[18,72,512]{2,1,0:T(8,128)}, f32[18,72,512]{2,1,0:T(8,128)S(1)}, u32[]{:S(2)}) copy-start(f32[18,72,512]{2,1,0:T(8,128)S(1)} %get-tuple-element.38.factor) | copy-start | bytes 7962628
  51.3 1.5 %copy-start.4 = (f32[18,72,512]{2,1,0:T(8,128)}, f32[18,72,512]{2,1,0:T(8,128)S(1)}, u32[]{:S(2)}) copy-start(f32[18,72,512]{2,1,0:T(8,128)S(1)} %get-tuple-element.40.adjoint) | copy-start | bytes 7962628
  52.8 4.3 %collective-permute-start.4 = (f32[40,256]{1,0:T(8,128)}, f32[40,256]{1,0:T(8,128)S(1)}, u32[]{:S(2)}, u32[]{:S(2)}) collective-permute-start(f32[40,256]{1,0:T(8,128)} %get-tuple-element.42), channel_id=1, source_target_pairs={{0,1},{1,0},{2,3},{3,2},{4,5},{5,4},{6,7},{7,6},{8,9},{9,8},{10,11... | collective-permute-start | bytes 122888 | tf_op jit(solution)/shard_map/ppermute | solution.py:782
  52.8 6.2 %collective-permute-start.5 = (f32[40,256]{1,0:T(8,128)}, f32[40,256]{1,0:T(8,128)S(1)}, u32[]{:S(2)}, u32[]{:S(2)}) collective-permute-start(f32[40,256]{1,0:T(8,128)} %get-tuple-element.43), channel_id=1, source_target_pairs={{1,2},{2,1},{3,4},{4,3},{5,6},{6,5},{7,8},{8,7},{9,10},{10,9},{11,... | collective-permute-start | bytes 122888 | tf_op jit(solution)/shard_map/ppermute | solution.py:781
  59.0 0.7 copy-start.17
  59.7 0.7 copy-start.19

commit v2 on v0

v2 whole, which is shorter than its diff:
```python
import math

import jax
import jax.numpy as jnp
import numpy as np
from jax import lax
from jax.experimental import pallas as pl
from jax.experimental.pallas import tpu as pltpu
from jax.sharding import PartitionSpec as P

ND = 36
NF = 36
NB = 1296
W = 128
ROWS = 4
SUB = 8
GROUP = 72
TILES = GROUP // SUB
GROUPS = NB // GROUP
CHUNKS = 6
F32 = jnp.float32
LIMIT = 14 * 1024 * 1024
LOG2E = math.log2(math.e)
LN2 = math.log(2.0)
LAND = 1.0e5

CELLS = (GROUPS, GROUP, ROWS * W)
EDGE = (GROUPS, GROUP, W)
EDGES = (GROUPS, GROUP, 2 * W)
BINS = (NB, W)
STATE = (16, 8 * W)
STEEP0, WIND0, WIND1, SEA, STEEP1, TEND1, GRAD1, TEND0, GRAD0, PASS0 = range(10)

NORTH = (0, 1, 2, 4, 5, 6)
SOUTH = (2, 3, 4, 6, 7, 8)
FROM_WEST = (0, 4, 8)
FROM_EAST = (2, 6)


def direction_tables():
    angle = np.float32(2.0 * math.pi) * np.arange(ND, dtype=np.float32) / np.float32(ND)
    cosine = np.tile(np.cos(angle), 2)[:, None]
    sine = np.tile(np.sin(angle), 2)[:, None]
    lane = np.arange(W)[None, :]
    east = cosine >= 0
    west_ok = (lane > 0).astype(np.float32)
    east_ok = (lane < W - 1).astype(np.float32)
    one = np.ones((1, W), np.float32)
    forward = np.abs(cosine) * np.where(east, west_ok, east_ok)
    backward = np.abs(cosine) * np.where(east, east_ok, west_ok)
    return np.stack(
        [(np.abs(cosine) + np.abs(sine)) * one, np.abs(sine) * one, forward, backward]
    ).astype(np.float32)


def sublane():
    return lax.broadcasted_iota(jnp.int32, (SUB, W), 0)


def north_mask(tile, sub):
    return {2: sub < 2, 4: sub >= 4, 6: sub < 6}.get(tile)


def west_mask(tile, sub):
    return {1: sub < 1, 3: sub >= 3, 5: sub < 5, 7: sub >= 7}.get(tile)


def side(tile, sub, value, reverse):
    west = tile not in (FROM_WEST if reverse else FROM_EAST)
    east = tile not in (FROM_EAST if reverse else FROM_WEST)
    from_west = pltpu.roll(value, 1, 1) if west else None
    from_east = pltpu.roll(value, W - 1, 1) if east else None
    if from_east is None:
        return from_west
    if from_west is None:
        return from_east
    mask = west_mask(tile, sub)
    return jnp.where(mask, from_east, from_west) if reverse else jnp.where(mask, from_west, from_east)


def pick(tile, sub, north, south):
    mask = north_mask(tile, sub)
    if mask is None:
        return north if tile in NORTH else south
    if north is None and south is None:
        return None
    return jnp.where(mask, 0.0 if north is None else north, 0.0 if south is None else south)


def plus(value, other):
    return value if other is None else value + other


def times(factor, value):
    return None if value is None else factor * value


def speed(tile, sub, courant, group):
    first, second = courant[2 * group], courant[2 * group + 1]
    if tile == 4:
        return jnp.where(sub < 4, first, second)
    return jnp.full((SUB, W), first if tile < 4 else second, F32)


def lanes(row):
    return pl.ds(row * W, W)


def column(row):
    return pl.ds((row + 2) * W, W)


def bins(group, tile):
    return pl.ds(pl.multiple_of(group * GROUP + tile * SUB, SUB), SUB)


def total(value):
    return jnp.sum(value, axis=0, keepdims=True)


def full(value):
    return jnp.broadcast_to(value, (SUB, W))


def whole(memory=pltpu.VMEM):
    return pl.BlockSpec(memory_space=memory)


def call(kernel, name, inputs, outputs, scratch=(), smem=(), away=(), out_away=(), aliases=None, cost=0):
    specs, operands = [], []
    for place, (value, resident) in enumerate(inputs):
        specs.append(whole(pltpu.SMEM if place in smem else pl.ANY if place in away else pltpu.VMEM))
        operands.append(pltpu.with_memory_space_constraint(value, pltpu.VMEM) if resident else value)
    shapes = [pltpu.VMEM(shape, F32) if resident else jax.ShapeDtypeStruct(shape, F32) for shape, resident in outputs]
    return pl.pallas_call(
        kernel,
        in_specs=specs,
        out_specs=[whole(pl.ANY if place in out_away else pltpu.VMEM) for place in range(len(outputs))],
        out_shape=shapes,
        scratch_shapes=list(scratch),
        input_output_aliases=aliases or {},
        compiler_params=pltpu.CompilerParams(vmem_limit_bytes=LIMIT),
        cost_estimate=pl.CostEstimate(flops=cost, bytes_accessed=cost, transcendentals=0) if cost else None,
        name=name,
    )(*operands)


def pack_kernel(field, sea_in, north, south):
    sub = sublane()
    both = (sub < 2) | ((sub >= 4) & (sub < 6))
    sea = [full(sea_in[:, lanes(r)].astype(F32)) for r in range(ROWS)]
    for pair in range(field.shape[0] // 2):
        for row in range(2):

            def cell(half, tile, base):
                return field[2 * pair + half, pl.ds(tile * SUB, SUB), lanes(base + row)] * sea[base + row]

            def put(ref, tile, value):
                ref[pair, pl.ds(tile * SUB, SUB), lanes(row)] = value

            rest = []
            for half in range(2):
                sixth = cell(half, 6, 2)
                for place, tile in enumerate((0, 1, 5)):
                    put(north, half * 4 + place, cell(half, tile, 2))
                mixed = jnp.where(sub < 2, cell(half, 2, 2), jnp.where(sub < 4, sixth, cell(half, 4, 2)))
                put(north, half * 4 + 3, mixed)
                rest.append(sixth)
            put(north, 8, jnp.where(both, rest[0], pltpu.roll(rest[1], 2, 0)))
            rest = []
            for half in range(2):
                second = cell(half, 2, 0)
                for place, tile in enumerate((3, 7, 8)):
                    put(south, half * 4 + place, cell(half, tile, 0))
                put(south, half * 4 + 3, jnp.where(sub < 4, cell(half, 4, 0), second))
                rest.append(jnp.where(sub < 4, second, cell(half, 6, 0)))
            put(south, 8, jnp.where(both, pltpu.roll(rest[1], 2, 0), rest[0]))


def pack(field, sea):
    steps = 3
    each = GROUPS // steps
    half = jax.ShapeDtypeStruct((GROUPS // 2, GROUP, 2 * W), F32)
    return pl.pallas_call(
        pack_kernel,
        grid=(steps,),
        in_specs=[pl.BlockSpec((each, GROUP, ROWS * W), lambda i: (i, 0, 0)), whole()],
        out_specs=[pl.BlockSpec((each // 2, GROUP, 2 * W), lambda i: (i, 0, 0))] * 2,
        out_shape=[half, half],
        compiler_params=pltpu.CompilerParams(vmem_limit_bytes=LIMIT),
        name="pack",
    )(pltpu.with_memory_space_constraint(field, pltpu.HBM), sea)


def unpack_north(halo, pair, half, row, sub):
    def get(tile):
        return halo[pair, pl.ds(tile * SUB, SUB), lanes(row)]

    mixed, last = get(half * 4 + 3), get(8)
    if half:
        last = pltpu.roll(last, 6, 0)
    return {
        0: get(half * 4),
        1: get(half * 4 + 1),
        2: mixed,
        4: mixed,
        5: get(half * 4 + 2),
        6: jnp.where((sub >= 2) & (sub < 4), mixed, last),
    }


def unpack_south(halo, pair, half, row, sub):
    def get(tile):
        return halo[pair, pl.ds(tile * SUB, SUB), lanes(row)]

    mixed, last = get(half * 4 + 3), get(8)
    if half:
        last = pltpu.roll(last, 6, 0)
    return {
        2: jnp.where(sub < 4, last, mixed),
        3: get(half * 4),
        4: mixed,
        6: last,
        7: get(half * 4 + 1),
        8: get(half * 4 + 2),
    }


def spread(row_ref, out, scale):
    for start in range(0, NB, W):
        size = min(W, NB - start)
        chunk = row_ref[:, pl.ds(start, size)] * scale
        out[pl.ds(start, size), :] = jnp.transpose(jnp.broadcast_to(chunk, (W, size)))


def layout(rows, ranks):
    lines = max(2, 2 * rows // ranks) // 2
    return lines, -(-(lines + 7) // SUB) * SUB


def sort(owner, point, value, weight, flat, load, ranks):
    rows = owner.shape[0]
    lines, block = layout(rows, ranks)
    flat[...] = jnp.zeros_like(flat)
    flat[0:1, :] = point[...].astype(F32)
    flat[1:2, :] = weight[...]
    columns = jnp.transpose(flat[...])
    load[...] = jnp.zeros_like(load)
    for half in range(2):
        here, base = pl.ds(half * rows, rows), half * (W // 2)
        load[here, pl.ds(base, NF)] = value[...] * columns[:, 1:2]
        load[here, pl.ds(base + NF, 1)] = columns[:, 1:2]
        load[here, pl.ds(base + NF + 1, 1)] = columns[:, 0:1]
    hits = (owner[...] == lax.broadcasted_iota(jnp.int32, (rows, ranks), 1)).astype(F32)
    before = lax.broadcasted_iota(jnp.int32, (rows, rows), 1) < lax.broadcasted_iota(jnp.int32, (rows, rows), 0)
    counts = jnp.dot(before.astype(F32), hits, preferred_element_type=F32)
    order = jnp.sum(counts * hits, axis=1, keepdims=True).astype(jnp.int32)
    target = owner[...] * block + order // 2
    odd = order % 2
    spots = lax.broadcasted_iota(jnp.int32, (rows, ranks * block), 1)
    places = [((target == spots) & (odd == half)).astype(F32) for half in range(2)]
    return lax.dot_general(
        jnp.concatenate(places, axis=0),
        load[...],
        (((0,), (0,)), ((), ())),
        precision=lax.Precision.HIGHEST,
        preferred_element_type=F32,
    )


def local_kernel(
    field, sea_in, wind, courant, rate_in, damp_in, steep_in, table, owner, point, value, weight,
    flow, rate, damp, steep, centre, ahead, back, across, own, slots,
    cells, flat, load, sems, *, ranks,
):
    sub = sublane()
    each = GROUPS // CHUNKS
    copies = [
        pltpu.make_async_copy(field.at[pl.ds(c * each, each)], cells.at[pl.ds(c * each, each)], sems.at[c])
        for c in range(CHUNKS)
    ]
    for copy in copies:
        copy.start()
    spread(rate_in, rate, LOG2E)
    spread(damp_in, damp, LOG2E)
    spread(steep_in, steep, 1.0)
    slots[...] = sort(owner, point, value, weight, flat, load, ranks)
    sea = [full(sea_in[:, lanes(r)].astype(F32)) for r in range(ROWS)]
    zero = jnp.zeros((SUB, W), F32)

    def step(group, sums):
        sums = list(sums)
        for tile in range(TILES):
            rows, spot = pl.ds(tile * SUB, SUB), bins(group, tile)
            pace = speed(tile, sub, courant, group)
            middle = 1.0 - pace * table[0, rows, :]
            over = pace * table[1, rows, :]
            along = pace * table[2, rows, :]
            centre[spot, :] = middle
            across[spot, :] = over
            ahead[spot, :] = along
            back[spot, :] = pace * table[3, rows, :]
            heavy = steep[spot, :]
            cell = {r: cells[group, rows, lanes(r)] * sea[r] for r in range(ROWS)}
            for r in range(ROWS):
                moved = middle * cell[r] + along * side(tile, sub, cell[r], False)
                moved = plus(moved, times(over, pick(tile, sub, cell.get(r - 1), cell.get(r + 1))))
                flow[group, rows, lanes(r)] = moved
                sums[r] = sums[r] + heavy * moved
            gone = heavy * over
            if tile in NORTH:
                sums[ROWS] = sums[ROWS] + pick(tile, sub, gone * cell[ROWS - 1], None)
            if tile in SOUTH:
                sums[ROWS + 1] = sums[ROWS + 1] + pick(tile, sub, None, gone * cell[0])
        return tuple(sums)

    sums = (zero,) * (ROWS + 2)
    for c in range(CHUNKS):
        copies[c].wait()
        sums = lax.fori_loop(c * each, (c + 1) * each, step, sums)
    sums = [total(value) for value in sums]
    own[...] = jnp.zeros_like(own)
    for r in range(ROWS):
        own[0:1, lanes(r)] = sums[r] * sea[r][0:1, :]
    own[1:2, lanes(ROWS - 1)] = sums[ROWS]
    own[1:2, lanes(0)] = sums[ROWS + 1]

    lines, block = layout(owner.shape[0], ranks)
    me = lax.axis_index("geo")

    def hand(near, far, dest):
        last = pl.ds(pl.multiple_of(dest * block + block - SUB, SUB), SUB)
        values = jnp.concatenate(
            [
                slots[last, :][0:1, :],
                wind[0:1, lanes(near)],
                wind[1:2, lanes(far)],
                wind[1:2, lanes(near)],
                sea[far][0:1, :],
                sea[near][0:1, :],
                own[0:1, lanes(near)],
                own[1:2, lanes(near)],
            ],
            axis=0,
        )
        slots[last, :] = values

    @pl.when(me < ranks - 1)
    def _():
        hand(ROWS - 1, ROWS - 2, me + 1)

    @pl.when(me > 0)
    def _():
        hand(0, 1, me - 1)


def local(field, sea, wind, courant, rate, damp, steep, table, owner, point, value, weight, ranks):
    rows = owner.shape[0]
    _, block = layout(rows, ranks)

    def kernel(*refs):
        local_kernel(*refs, ranks=ranks)

    args = (
        pltpu.with_memory_space_constraint(field, pltpu.HBM), sea, wind, courant, rate, damp, steep, table,
        owner, point, value, weight,
    )
    return call(
        kernel,
        "local",
        [(arg, False) for arg in args],
        [(CELLS, True)] + [(BINS, True)] * 7 + [((SUB, ROWS * W), True), ((ranks * block, W), False)],
        [
            pltpu.VMEM(CELLS, F32),
            pltpu.VMEM((SUB, rows), F32),
            pltpu.VMEM((2 * rows, W), F32),
            pltpu.SemaphoreType.DMA((CHUNKS,)),
        ],
        smem=(3,),
        away=(0,),
    )


def place(arrived, ranks, rows, wanted, gain):
    lines, block = layout(rows, ranks)
    size = ranks * block
    held = lax.rem(lax.broadcasted_iota(jnp.int32, (size, W), 0), block) < lines
    load = jnp.where(held, arrived[...], 0.0)
    sums = 0.0
    for half in range(2):
        mine = load[:, half * (W // 2) : (half + 1) * (W // 2)]
        point = mine[:, NF + 1 : NF + 2].astype(jnp.int32)
        hits = (point == lax.broadcasted_iota(jnp.int32, (size, ROWS * W), 1)).astype(F32)
        sums = sums + lax.dot_general(
            mine,
            hits,
            (((0,), (0,)), ((), ())),
            precision=lax.Precision.HIGHEST,
            preferred_element_type=F32,
        )
    for f in range(NF):
        rows_of = slice(4 * (f % 2), 4 * (f % 2) + 4)
        wanted[f // 2, rows_of, :] = jnp.broadcast_to(sums[f : f + 1, :] * (1.0 / ND), (4, ROWS * W))
    gain[...] = jnp.broadcast_to(sums[NF : NF + 1, :] * (1.0 / (ND * ND)), gain.shape)


def early_kernel(
    arrived, flow, own, wind, sea_in, rate, damp, steep, centre, ahead, across, next_, factor, moved, wanted, gain, state,
    *, ranks, rows,
):
    sub = sublane()
    place(arrived, ranks, rows, wanted, gain)
    lines, block = layout(rows, ranks)
    me = lax.axis_index("geo")

    def aux(source, there):
        source = jnp.clip(source, 0, ranks - 1)
        last = pl.ds(pl.multiple_of(source * block + block - SUB, SUB), SUB)
        return jnp.where(there, arrived[last, :], 0.0)

    south, north = aux(me - 1, me > 0), aux(me + 1, me < ranks - 1)
    state[...] = jnp.zeros_like(state)
    for near, far, values in ((-1, -2, south), (4, 5, north)):
        state[WIND0 : WIND0 + 1, column(near)] = values[1:2, :]
        state[WIND1 : WIND1 + 1, column(far)] = values[2:3, :]
        state[WIND1 : WIND1 + 1, column(near)] = values[3:4, :]
        state[SEA : SEA + 1, column(far)] = values[4:5, :]
        state[SEA : SEA + 1, column(near)] = values[5:6, :]
    here = pl.ds(2 * W, ROWS * W)
    state[WIND0 : WIND0 + 1, here] = wind[0:1, :]
    state[WIND1 : WIND1 + 1, here] = wind[1:2, :]
    state[SEA : SEA + 1, here] = sea_in[...].astype(F32)
    steeps = {r: own[0:1, lanes(r)] for r in range(ROWS)}
    steeps[0] = steeps[0] + south[7:8, :]
    steeps[3] = steeps[3] + north[7:8, :]
    steeps[-1] = south[6:7, :] + own[1:2, lanes(0)]
    steeps[4] = north[6:7, :] + own[1:2, lanes(3)]
    for r, value in steeps.items():
        state[STEEP0 : STEEP0 + 1, column(r)] = jnp.where(state[SEA : SEA + 1, column(r)] > 0.5, value, LAND)
    steep0 = [full(state[STEEP0 : STEEP0 + 1, column(r)]) for r in range(ROWS)]
    wind0 = [full(state[WIND0 : WIND0 + 1, column(r)]) for r in range(ROWS)]

    def step(group, sums):
        sums = list(sums)
        for tile in range(TILES):
            rows, spot = pl.ds(tile * SUB, SUB), bins(group, tile)
            grow, fade, heavy = rate[spot, :], damp[spot, :], steep[spot, :]
            middle, along, over = centre[spot, :], ahead[spot, :], across[spot, :]
            cell = {}
            for r in range(ROWS):
                gained = jnp.exp2(grow * wind0[r] - fade * steep0[r])
                factor[group, rows, lanes(r)] = gained
                cell[r] = flow[group, rows, lanes(r)] * gained
                next_[group, rows, lanes(r)] = cell[r]
            for r in range(ROWS):
                value = middle * cell[r] + along * side(tile, sub, cell[r], False)
                value = plus(value, times(over, pick(tile, sub, cell.get(r - 1), cell.get(r + 1))))
                moved[group, rows, lanes(r)] = value
                sums[r] = sums[r] + heavy * value
        return tuple(sums)

    sums = lax.fori_loop(0, GROUPS, step, (jnp.zeros((SUB, W), F32),) * ROWS)
    for r in range(ROWS):
        state[STEEP1 : STEEP1 + 1, column(r)] = total(sums[r])


def early(arrived, flow, own, wind, sea, rate, damp, steep, centre, ahead, across, ranks, rows):
    def kernel(*refs):
        early_kernel(*refs, ranks=ranks, rows=rows)

    inputs = [(arrived, False), (flow, True), (own, True), (wind, False), (sea, False)]
    inputs += [(value, True) for value in (rate, damp, steep, centre, ahead, across)]
    return call(
        kernel,
        "early",
        inputs,
        [(CELLS, True)] * 3 + [((GROUPS, SUB, ROWS * W), True), ((SUB, ROWS * W), True), (STATE, True)],
    )


def split_lam(lam, group, tile, where):
    if tile < 4:
        return lam[group, 0:1, where]
    if tile > 4:
        return lam[group, 4:5, where]
    return lam[group, :, where]


def late_kernel(
    next_in, factor, moved, from_south, from_north, wanted, gain, state_in, rate, damp, steep, centre, ahead, back, across,
    next_, next_south, next_north, source, edges, state, send_a, send_b,
    fixed, growth, lam, halo_south, halo_north, sems,
):
    sub = sublane()
    zero = jnp.zeros((SUB, W), F32)
    each = GROUPS // 2 // 3
    copies = []
    for c in range(3):
        here = pl.ds(c * each, each)
        copies.append(pltpu.make_async_copy(from_south.at[here], halo_south.at[here], sems.at[2 * c]))
        copies.append(pltpu.make_async_copy(from_north.at[here], halo_north.at[here], sems.at[2 * c + 1]))
    for copy in copies:
        copy.start()
    state[...] = state_in[...]

    def held(place, r):
        return full(state[place : place + 1, column(r)])

    steep0 = {r: held(STEEP0, r) for r in (-1, 4)}
    wind0 = {r: held(WIND0, r) for r in (-1, 4)}

    def first(pair, sums):
        sums = list(sums)
        for half in range(2):
            group = 2 * pair + half
            ghosts = {
                -2: unpack_north(halo_south, pair, half, 0, sub),
                -1: unpack_north(halo_south, pair, half, 1, sub),
                4: unpack_south(halo_north, pair, half, 0, sub),
                5: unpack_south(halo_north, pair, half, 1, sub),
            }
            for tile in range(TILES):
                rows, spot = pl.ds(tile * SUB, SUB), bins(group, tile)
                grow, fade, heavy = rate[spot, :], damp[spot, :], steep[spot, :]
                middle, along, over = centre[spot, :], ahead[spot, :], across[spot, :]
                beyond = {}
                changes = {}
                for near, far, mine, second, tiles, north in ((-1, -2, 0, 1, NORTH, True), (4, 5, 3, 2, SOUTH, False)):
                    if tile not in tiles:
                        continue

                    def only(value):
                        return pick(tile, sub, value, None) if north else pick(tile, sub, None, value)

                    cell = ghosts[near][tile]
                    gained = jnp.exp2(grow * wind0[near] - fade * steep0[near])
                    value = middle * cell + along * side(tile, sub, cell, False) + over * ghosts[far][tile]
                    value = value * gained
                    (next_south if north else next_north)[group, rows, :] = value
                    extra = only(over * cell) * factor[group, rows, lanes(mine)]
                    next_[group, rows, lanes(mine)] = next_in[group, rows, lanes(mine)] + extra
                    change = middle * extra + along * side(tile, sub, extra, False) + only(over * value)
                    changes[mine] = plus(change, changes.get(mine))
                    changes[second] = plus(over * extra, changes.get(second))
                for r, change in changes.items():
                    sums[r] = sums[r] + heavy * change
                    fixed[group, rows, lanes(r)] = moved[group, rows, lanes(r)] + change
                for r in range(ROWS):
                    if r not in changes:
                        fixed[group, rows, lanes(r)] = moved[group, rows, lanes(r)]
        return tuple(sums)

    sums = (zero,) * ROWS
    for c in range(3):
        copies[2 * c].wait()
        copies[2 * c + 1].wait()
        sums = lax.fori_loop(c * each, (c + 1) * each, first, sums)
    for r in range(ROWS):
        value = state[STEEP1 : STEEP1 + 1, column(r)] + total(sums[r])
        state[STEEP1 : STEEP1 + 1, column(r)] = jnp.where(state[SEA : SEA + 1, column(r)] > 0.5, value, LAND)
    steep1 = [held(STEEP1, r) for r in range(ROWS)]
    wind1 = [held(WIND1, r) for r in range(ROWS)]
    gains = [gain[:, lanes(r)] for r in range(ROWS)]

    def second(group, sums):
        sums = list(sums)
        means = [[None, None] for _ in range(ROWS)]
        ups = [[None, None] for _ in range(ROWS)]
        downs = [[None, None] for _ in range(ROWS)]
        for tile in range(TILES):
            rows, spot = pl.ds(tile * SUB, SUB), bins(group, tile)
            grow, fade = rate[spot, :], damp[spot, :]
            for r in range(ROWS):
                value = jnp.exp2(grow * wind1[r] - fade * steep1[r])
                growth[group, rows, lanes(r)] = value
                value = value * fixed[group, rows, lanes(r)]
                for parts, term in ((means, value), (ups, grow * value), (downs, fade * value)):
                    if tile == 4:
                        parts[r][0] = plus(jnp.where(sub < 4, term, 0.0), parts[r][0])
                        parts[r][1] = jnp.where(sub < 4, 0.0, term)
                    else:
                        f = 0 if tile < 4 else 1
                        parts[r][f] = plus(term, parts[r][f])
        for r in range(ROWS):
            one, two = means[r]
            one = one + pltpu.roll(one, 4, 0)
            two = two + pltpu.roll(two, 4, 0)
            both = jnp.where(sub < 4, one, two)
            both = both + jnp.where((sub & 2) == 0, pltpu.roll(both, 6, 0), pltpu.roll(both, 2, 0))
            both = both + jnp.where((sub & 1) == 0, pltpu.roll(both, 7, 0), pltpu.roll(both, 1, 0))
            value = gains[r] * both - wanted[group, :, lanes(r)]
            lam[group, :, lanes(r)] = value
            up, down = value[0:1, :], value[4:5, :]
            sums[r] = sums[r] + (up * ups[r][0] + down * ups[r][1])
            sums[ROWS + r] = sums[ROWS + r] + (up * downs[r][0] + down * downs[r][1])
        return tuple(sums)

    sums = lax.fori_loop(0, GROUPS, second, (zero,) * (2 * ROWS))
    for r in range(ROWS):
        state[GRAD1 : GRAD1 + 1, column(r)] = total(sums[r]) * LN2
        state[TEND1 : TEND1 + 1, column(r)] = total(sums[ROWS + r]) * (-LN2)
    tend1 = [held(TEND1, r) for r in range(ROWS)]

    def third(group, sums):
        sums = list(sums)
        for tile in range(TILES):
            rows, spot = pl.ds(tile * SUB, SUB), bins(group, tile)
            grow, fade, heavy = rate[spot, :], damp[spot, :], steep[spot, :]
            middle, along, over = centre[spot, :], back[spot, :], across[spot, :]
            cell = {}
            for r in range(ROWS):
                cell[r] = split_lam(lam, group, tile, lanes(r)) * growth[group, rows, lanes(r)] + heavy * tend1[r]
                source[group, rows, lanes(r)] = cell[r]
            for place, r in enumerate((0, ROWS - 1)):
                value = middle * cell[r] + along * side(tile, sub, cell[r], True)
                value = plus(value, times(over, pick(tile, sub, cell.get(r + 1), cell.get(r - 1))))
                edges[group, rows, lanes(place)] = value
                value = value * next_[group, rows, lanes(r)]
                sums[place] = sums[place] + grow * value
                sums[2 + place] = sums[2 + place] + fade * value
        return tuple(sums)

    sums = lax.fori_loop(0, GROUPS, third, (zero,) * 4)
    for place, r in enumerate((0, ROWS - 1)):
        state[GRAD0 : GRAD0 + 1, column(r)] = total(sums[place]) * LN2
        state[TEND0 : TEND0 + 1, column(r)] = total(sums[2 + place]) * (-LN2)

    def fill(ref, base):
        for f in range(NF):
            ref[f : f + 1, :] = lam[f // 2, 4 * (f % 2) : 4 * (f % 2) + 1, pl.ds(base * W, 2 * W)]
        here = pl.ds((base + 2) * W, 2 * W)
        for place, name in enumerate((STEEP1, TEND1, TEND0, TEND0)):
            ref[NF + place : NF + place + 1, :] = state[name : name + 1, here]

    even = lax.rem(lax.axis_index("geo"), 2) == 0

    @pl.when(even)
    def _():
        fill(send_a, 2)
        fill(send_b, 0)

    @pl.when(jnp.logical_not(even))
    def _():
        fill(send_a, 0)
        fill(send_b, 2)


def late(next_, factor, moved, from_south, from_north, wanted, gain, state, coefficients):
    inputs = [(next_, True), (factor, True), (moved, True), (from_south, False), (from_north, False)]
    inputs += [(value, True) for value in (wanted, gain, state) + coefficients]
    halo = (GROUPS // 2, GROUP, 2 * W)
    return call(
        late_kernel,
        "late",
        inputs,
        [(CELLS, True)] + [(EDGE, True)] * 2 + [(CELLS, True), (EDGES, True), (STATE, True)]
        + [((NF + 4, 2 * W), False)] * 2,
        [
            pltpu.VMEM(CELLS, F32),
            pltpu.VMEM(CELLS, F32),
            pltpu.VMEM((GROUPS, SUB, ROWS * W), F32),
            pltpu.VMEM(halo, F32),
            pltpu.VMEM(halo, F32),
            pltpu.SemaphoreType.DMA((6,)),
        ],
        away=(3, 4),
        aliases={0: 0},
    )


def inner_kernel(
    next_, next_south, next_north, source, state_in, rate, damp, centre, back, across,
    inside, factor_south, factor_north, state,
):
    sub = sublane()
    zero = jnp.zeros((SUB, W), F32)
    state[...] = state_in[...]
    wind0 = {r: full(state[WIND0 : WIND0 + 1, column(r)]) for r in (-1, 4)}
    steep0 = {r: full(state[STEEP0 : STEEP0 + 1, column(r)]) for r in (-1, 4)}

    def step(group, sums):
        sums = list(sums)
        for tile in range(TILES):
            rows, spot = pl.ds(tile * SUB, SUB), bins(group, tile)
            grow, fade = rate[spot, :], damp[spot, :]
            if tile in SOUTH:
                factor_south[group, rows, :] = jnp.exp2(grow * wind0[-1] - fade * steep0[-1])
            if tile in NORTH:
                factor_north[group, rows, :] = jnp.exp2(grow * wind0[4] - fade * steep0[4])
            middle, along, over = centre[spot, :], back[spot, :], across[spot, :]
            cell = {r: source[group, rows, lanes(r)] for r in range(ROWS)}
            for place, r in enumerate((1, 2)):
                value = middle * cell[r] + along * side(tile, sub, cell[r], True)
                value = value + over * pick(tile, sub, cell[r + 1], cell[r - 1])
                inside[group, rows, lanes(place)] = value
                value = value * next_[group, rows, lanes(r)]
                sums[place] = sums[place] + grow * value
                sums[2 + place] = sums[2 + place] + fade * value
            gone = fade * over
            if tile in NORTH:
                value = pick(tile, sub, cell[0] * next_south[group, rows, :], None)
                sums[4] = sums[4] + gone * value
            if tile in SOUTH:
                value = pick(tile, sub, None, cell[3] * next_north[group, rows, :])
                sums[5] = sums[5] + gone * value
        return tuple(sums)

    sums = lax.fori_loop(0, GROUPS, step, (zero,) * 6)
    for place, r in enumerate((1, 2)):
        state[GRAD0 : GRAD0 + 1, column(r)] = total(sums[place]) * LN2
        state[TEND0 : TEND0 + 1, column(r)] = total(sums[2 + place]) * (-LN2)
    state[TEND0 : TEND0 + 1, column(-1)] = total(sums[4]) * (-LN2)
    state[TEND0 : TEND0 + 1, column(4)] = total(sums[5]) * (-LN2)


def inner(*args):
    return call(
        inner_kernel,
        "inner",
        [(arg, True) for arg in args],
        [(EDGES, True), (EDGE, True), (EDGE, True), (STATE, True)],
        cost=1 << 22,
    )


def last_kernel(
    next_, factor, factor_south, factor_north, edges, inside, state, back_a, back_b, rate, damp, steep, centre, back, across,
    out, grad, rims, low, high, ghosts, lam, cells, sems,
):
    sub = sublane()
    zero = jnp.zeros((SUB, W), F32)
    even = lax.rem(lax.axis_index("geo"), 2) == 0
    ghosts[0] = jnp.where(even, back_b[...], back_a[...])
    ghosts[1] = jnp.where(even, back_a[...], back_b[...])
    for group in range(GROUPS):
        for where in range(2):
            for row in range(2):
                one = ghosts[where, 2 * group : 2 * group + 1, lanes(row)]
                two = ghosts[where, 2 * group + 1 : 2 * group + 2, lanes(row)]
                lam[group, :, lanes(2 * where + row)] = jnp.where(sub < 4, one, two)
    sea = {r: full(state[SEA : SEA + 1, column(r)]) for r in range(-2, 6)}
    wind1, steep1, tend1 = {}, {}, {}
    for r in (-2, -1, 4, 5):
        where, here = (0, lanes(r + 2)) if r < 0 else (1, lanes(r - 4))
        wind1[r] = full(state[WIND1 : WIND1 + 1, column(r)])
        value = ghosts[where, NF : NF + 1, here]
        steep1[r] = full(jnp.where(sea[r][0:1, :] > 0.5, value, LAND))
        tend1[r] = full(ghosts[where, NF + 1 : NF + 2, here])

    def first(group, sums):
        sums = list(sums)
        for tile in range(TILES):
            rows, spot = pl.ds(tile * SUB, SUB), bins(group, tile)
            grow, fade, heavy = rate[spot, :], damp[spot, :], steep[spot, :]
            middle, along, over = centre[spot, :], back[spot, :], across[spot, :]

            def ghost(r):
                value = split_lam(lam, group, tile, lanes(r + 2 if r < 0 else r - 2))
                return value * jnp.exp2(grow * wind1[r] - fade * steep1[r]) + heavy * tend1[r]

            for near, far, mine, place, tiles in ((-1, -2, 0, 0, SOUTH), (4, 5, 3, 1, NORTH)):
                if tile not in tiles:
                    continue
                cell = ghost(near)
                value = middle * cell + along * side(tile, sub, cell, True) + over * ghost(far)
                (low if place == 0 else high)[group, rows, :] = value
                value = over * cell
                value = pick(tile, sub, None, value) if place == 0 else pick(tile, sub, value, None)
                rims[group, rows, lanes(place)] = edges[group, rows, lanes(place)] + value
                value = value * next_[group, rows, lanes(mine)]
                sums[place] = sums[place] + grow * value
                sums[2 + place] = sums[2 + place] + fade * value
        return tuple(sums)

    sums = lax.fori_loop(0, GROUPS, first, (zero,) * 4)
    sums = [total(value) * LN2 for value in sums]
    tend0 = {r: state[TEND0 : TEND0 + 1, column(r)] for r in range(-1, 5)}
    grad0 = [state[GRAD0 : GRAD0 + 1, column(r)] for r in range(ROWS)]
    tend0[0], grad0[0] = tend0[0] - sums[2], grad0[0] + sums[0]
    tend0[3], grad0[3] = tend0[3] - sums[3], grad0[3] + sums[1]
    tend0[-1] = tend0[-1] + ghosts[0, NF + 2 : NF + 3, lanes(1)]
    tend0[4] = tend0[4] + ghosts[1, NF + 2 : NF + 3, lanes(0)]
    for r in range(ROWS):
        grad[0:1, lanes(r)] = grad0[r]
        grad[1:2, lanes(r)] = state[GRAD1 : GRAD1 + 1, column(r)]
    tend0 = {r: full(value) for r, value in tend0.items()}

    def second(group, carry):
        for tile in range(TILES):
            rows, spot = pl.ds(tile * SUB, SUB), bins(group, tile)
            heavy = steep[spot, :]
            middle, along, over = centre[spot, :], back[spot, :], across[spot, :]
            cell = {}
            for r in range(-1, 5):
                if r == -1:
                    if tile not in SOUTH:
                        continue
                    value = low[group, rows, :] * factor_south[group, rows, :]
                elif r == 4:
                    if tile not in NORTH:
                        continue
                    value = high[group, rows, :] * factor_north[group, rows, :]
                else:
                    if r == 0:
                        value = (rims if tile in SOUTH else edges)[group, rows, lanes(0)]
                    elif r == 3:
                        value = (rims if tile in NORTH else edges)[group, rows, lanes(1)]
                    else:
                        value = inside[group, rows, lanes(r - 1)]
                    value = value * factor[group, rows, lanes(r)]
                cell[r] = value + heavy * tend0[r]
            for r in range(ROWS):
                value = middle * cell[r] + along * side(tile, sub, cell[r], True)
                value = value + over * pick(tile, sub, cell.get(r + 1), cell.get(r - 1))
                cells[group, rows, lanes(r)] = sea[r] * value
        return carry

    each = GROUPS // CHUNKS
    copies = []
    for c in range(CHUNKS):
        lax.fori_loop(c * each, (c + 1) * each, second, 0)
        here = pl.ds(c * each, each)
        copies.append(pltpu.make_async_copy(cells.at[here], out.at[here], sems.at[c]))
        copies[c].start()
    for copy in copies:
        copy.wait()


def last(next_, factor, factor_south, factor_north, edges, inside, state, back_a, back_b, coefficients):
    inputs = [(value, True) for value in (next_, factor, factor_south, factor_north, edges, inside, state)]
    inputs += [(back_a, False), (back_b, False)]
    inputs += [(value, True) for value in coefficients]
    return call(
        last_kernel,
        "last",
        inputs,
        [(CELLS, False), ((2, ROWS * W), False)],
        [
            pltpu.VMEM(EDGES, F32),
            pltpu.VMEM(EDGE, F32),
            pltpu.VMEM(EDGE, F32),
            pltpu.VMEM((2, NF + 4, 2 * W), F32),
            pltpu.VMEM((GROUPS, SUB, ROWS * W), F32),
            pltpu.VMEM(CELLS, F32),
            pltpu.SemaphoreType.DMA((CHUNKS,)),
        ],
        out_away=(0,),
    )


def swaps(count):
    near = [(i, i ^ 1) for i in range(count)]
    far = []
    for i in range(1, count - 1, 2):
        far += [(i, i + 1), (i + 1, i)]
    return near, far


def body(
    initial_spectrum,
    wind_forcing,
    sea_mask,
    courant,
    input_rate,
    damping,
    steep_weight,
    obs_owner,
    obs_point,
    obs_value,
    obs_weight,
):
    count = lax.axis_size("geo")
    held = obs_point.shape[0]
    near, far = swaps(count)
    field = initial_spectrum.reshape(CELLS)
    sea = sea_mask.reshape(1, ROWS * W)
    north, south = pack(field, sea)
    from_south = lax.ppermute(north, "geo", [(i, i + 1) for i in range(count - 1)])
    from_north = lax.ppermute(south, "geo", [(i + 1, i) for i in range(count - 1)])
    flow, rate, damp, steep, centre, ahead, back, across, own, slots = local(
        field,
        sea,
        wind_forcing,
        courant,
        input_rate.reshape(1, NB),
        damping.reshape(1, NB),
        steep_weight.reshape(1, NB),
        jnp.asarray(direction_tables()),
        obs_owner,
        obs_point.reshape(1, held),
        obs_value,
        obs_weight.reshape(1, held),
        count,
    )
    arrived = lax.all_to_all(slots, "geo", split_axis=0, concat_axis=0, tiled=True)
    next_, factor, moved, wanted, gain, state = early(
        arrived, flow, own, wind_forcing, sea, rate, damp, steep, centre, ahead, across, count, held
    )
    next_, next_south, next_north, source, edges, state, send_a, send_b = late(
        next_, factor, moved, from_south, from_north, wanted, gain, state,
        (rate, damp, steep, centre, ahead, back, across),
    )
    back_b = lax.ppermute(send_b, "geo", far)
    back_a = lax.ppermute(send_a, "geo", near)
    inside, factor_south, factor_north, state = inner(next_, next_south, next_north, source, state, rate, damp, centre, back, across)
    out, grad = last(
        next_, factor, factor_south, factor_north, edges, inside, state, back_a, back_b,
        (rate, damp, steep, centre, back, across),
    )
    return grad, out.reshape(NB, ROWS * W)


def solution(mesh):
    return jax.shard_map(
        body,
        mesh=mesh,
        in_specs=(
            P(None, ("groups", "geo")),
            P(None, ("groups", "geo")),
            P(("groups", "geo")),
            P(),
            P(),
            P(),
            P(),
            P(("groups", "geo"), None),
            P(("groups", "geo")),
            P(("groups", "geo"), None),
            P(("groups", "geo")),
        ),
        out_specs=(P(None, ("groups", "geo")), P(None, ("groups", "geo"))),
        check_vma=False,
    )
```

time: 163 us -> 52.5 us (0.32)
  other arithmetic: 44.7 us -> 0 us
  waiting for transfers between devices: 43 us -> 1.44 us
  Pallas kernels: 0 us -> 26.2 us
  local copies, waits for them, and re-layouts: 22.7 us -> 0.99 us
  starting transfers between devices: 30 us -> 9.57 us
  blocking collectives: 20.8 us -> 13.1 us
    ppermute x8 -> x4, waiting for transfers between devices: 37 us -> 1.44 us  [the longest x1 1.43 us: body(): back_b = lax.ppermute(send_b, 'geo', far)]
    pallas_call x0 -> x6, Pallas kernels: none -> 26.2 us  [the longest x5 23.7 us: call(): pl.pallas_call(kernel, in_specs=specs, out_specs=[whole(pl.ANY if place i...]
    mul x8 -> x0, other arithmetic: 19.7 us -> none  [the longest x1 8.15 us: body(): product = adjoint * state * factor]
    reduce_sum x6 -> x0, other arithmetic: 19.1 us -> none  [the longest x2 13.6 us: growth(): steep = jnp.sum(steep_weight[:, None] * state, axis=0)]
    ppermute x8 -> x4, starting transfers between devices: 23.8 us -> 9.57 us  [the longest x1 4.51 us: body(): lax.ppermute(north, 'geo', [(i, i + 1) for i in range(count - 1)])]
    reshape x2 -> x3, local copies, waits for them, and re-layouts: 7.71 us -> 0.02 us  [the longest x1 0.01 us: body(): input_rate.reshape(1, NB)]
    all_to_all x2 -> x1, blocking collectives: 20.8 us -> 13.1 us  [body(): lax.all_to_all(slots, 'geo', split_axis=0, concat_axis=0, tiled=True)]
    all_to_all x1 -> x0, starting transfers between devices: 6.21 us -> none  [body(): lax.all_to_all(model_slots, 'geo', split_axis=0, concat_axis=0, tiled=True)]
  transfers between devices with their start and end apart: 9 -> 4, of which waited for: 4 -> 1; matrix products, arithmetic and copies ran while one was open for 3% -> 0% of each run, Pallas kernels for 0% -> 21%
where the time goes in v2:
time: 52.5 us; the launch traced here: 52.3 us
  Pallas kernels  26.2 us (50%)
  blocking collectives  13.1 us (25%)
  starting transfers between devices  9.57 us (18%)
  waiting for transfers between devices  1.44 us (3%)
  local copies, waits for them, and re-layouts  0.99 us (2%)
  between operations  0.89 us (2%)
    pallas_call x5, Pallas kernels, call(): pl.pallas_call(kernel, in_specs=specs, out_specs=[whole(pl.ANY if place i...  23.7 us
    all_to_all x1, blocking collectives, body(): lax.all_to_all(slots, 'geo', split_axis=0, concat_axis=0, tiled=True)  13.1 us
    ppermute x1, starting transfers between devices, body(): lax.ppermute(north, 'geo', [(i, i + 1) for i in range(count - 1)])  4.51 us
    pallas_call x1, Pallas kernels, pack(): pl.pallas_call(pack_kernel, grid=(steps,), in_specs=[pl.BlockSpec((each,...  2.58 us
    ppermute x1, starting transfers between devices, body(): lax.ppermute(south, 'geo', [(i + 1, i) for i in range(count - 1)])  1.92 us
    ppermute x1, starting transfers between devices, body(): back_b = lax.ppermute(send_b, 'geo', far)  1.91 us
    ppermute x1, waiting for transfers between devices, body(): back_b = lax.ppermute(send_b, 'geo', far)  1.43 us
    ppermute x1, starting transfers between devices, body(): back_a = lax.ppermute(send_a, 'geo', near)  1.23 us
  transfers between devices with their start and end apart: 4, of which 1 were waited for; matrix products, arithmetic and copies ran while one was open for 0% of the time, Pallas kernels for 21%

profile of v2, /device:TPU:1, one launch (start us, length us, event | category | flops | bytes accessed | tf_op | source)
XLA Modules:
  0.0 52.3 jit_solution(14834261734456003134)
XLA Ops:
  0.6 0.0 copy-start
  0.6 0.0 copy-start.1
  0.7 0.7 %copy-done.1 = s32[512]{0:T(512)S(1)} copy-done((s32[512]{0:T(512)S(1)}, s32[512]{0:T(512)}, u32[]{:S(2)}) %copy-start.1) | copy-done | bytes 2072
  1.4 0.0 copy-start.8
  1.4 0.0 copy-start.9
  1.4 0.0 copy-start.10
  1.4 0.0 copy-start.11
  1.4 0.0 copy-start.7
  1.4 0.0 copy-start.2
  1.4 0.0 copy-start.3
  1.4 0.0 copy-start.4
  1.4 0.0 copy-start.5
  1.4 0.0 copy-start.6
  1.4 2.6 %pack.1 = (f32[9,72,256]{2,1,0:T(8,128)S(1)}, f32[9,72,256]{2,1,0:T(8,128)S(1)}) custom-call(f32[18,72,512]{2,1,0:T(8,128)} %bitcast.14, s32[1,512]{1,0:T(1,128)S(1)} %bitcast.9), custom_call_target="tpu_custom_call" | custom-call | tf_op jit(solution)/shard_map/pack/pallas_call | solution.py:184
  4.0 4.5 %collective-permute-start = (f32[9,72,256]{2,1,0:T(8,128)S(1)}, f32[9,72,256]{2,1,0:T(8,128)S(1)}, u32[]{:S(2)}, u32[]{:S(2)}) collective-permute-start(f32[9,72,256]{2,1,0:T(8,128)S(1)} %get-tuple-element.46), channel_id=1, source_target_pairs={{0,1},{1,2},{2,3},{3,4},{4,5},{5,6},{6,7},{7,8},{8,9},{9,10},{10,1... | collective-permute-start | bytes 1990664 | tf_op jit(solution)/shard_map/ppermute | solution.py:878
  8.5 1.9 %collective-permute-start.1 = (f32[9,72,256]{2,1,0:T(8,128)S(1)}, f32[9,72,256]{2,1,0:T(8,128)S(1)}, u32[]{:S(2)}, u32[]{:S(2)}) collective-permute-start(f32[9,72,256]{2,1,0:T(8,128)S(1)} %get-tuple-element.47), channel_id=1, source_target_pairs={{1,0},{2,1},{3,2},{4,3},{5,4},{6,5},{7,6},{8,7},{9,8},{10,9},{11,1... | collective-permute-start | bytes 1990664 | tf_op jit(solution)/shard_map/ppermute | solution.py:879
  10.5 0.0 copy-done.8
  10.5 0.0 copy-done.9
  10.5 0.0 copy-done.10
  10.5 0.0 copy-done.11
  10.6 0.1 copy.15.refs_8_
  10.7 0.0 copy-done.7
  10.7 0.1 copy.16.refs_10_
  10.8 0.0 copy-done
  10.8 0.0 copy-done.2
  10.8 0.0 copy-done.3
  10.8 0.0 copy-done.4
  10.8 0.0 copy-done.5
  10.8 0.0 copy-done.6
  10.8 5.5 %local.1 = (f32[18,72,512]{2,1,0:T(8,128)S(1)}, f32[1296,128]{1,0:T(8,128)S(1)}, f32[1296,128]{1,0:T(8,128)S(1)}, f32[1296,128]{1,0:T(8,128)S(1)}, f32[1296,128]...) custom-call(f32[18,72,512]{2,1,0:T(8,128)} %bitcast.15, ...), custom_call_target="tpu_custom_call" | custom-call | tf_op jit(solution)/shard_map/local/pallas_call | solution.py:135
  16.3 13.1 %all_to_all.11 = f32[16,16,128]{2,1,0:T(8,128)S(1)} all-to-all(f32[16,16,128]{2,1,0:T(8,128)S(1)} %bitcast.8), channel_id=1, replica_groups=mesh['groups'=2,'geo'=16] {'geo'}, dimensions={0} | all-to-all | bytes 262144 | tf_op jit(solution)/shard_map/all_to_all | solution.py:895
  29.4 3.5 %early.1 = (f32[18,72,512]{2,1,0:T(8,128)S(1)}, f32[18,72,512]{2,1,0:T(8,128)S(1)}, f32[18,72,512]{2,1,0:T(8,128)S(1)}, f32[18,8,512]{2,1,0:T(8,128)S(1)}, f32[8,512]{1,0:T(8,128)S(1)}, /*index=5*/f32[16,1024]{1,0:T(8,128)S(1)}) custom-call(f32[256,128]{1,0:T(8,128)S(1)} %bitcast.7, f32[18,72,512]{2,1,0:T(8,128)S(1)} %get-tuple-element.35.refs_1_, ...), custom_call_target="tpu_custom_call" | custom-call | tf_op jit(solution)/shard_map/early/pallas_call | solution.py:135
  32.9 0.0 collective-permute-done.from_south
  32.9 0.0 collective-permute-done.1.from_north
  32.9 7.0 %late.1 = (f32[18,72,512]{2,1,0:T(8,128)S(1)}, f32[18,72,128]{2,1,0:T(8,128)S(1)}, f32[18,72,128]{2,1,0:T(8,128)S(1)}, f32[18,72,512]{2,1,0:T(8,128)S(1)}, f32[1...) custom-call(f32[18,72,512]{2,1,0:T(8,128)S(1)} %get-tuple-element.43, ...), custom_call_target="tpu_custom_call", output_to_operand_aliasing={{0}: (0, {})} | custom-call | tf_op jit(solution)/shard_map/late/pallas_call | solution.py:135
  39.9 1.2 %collective-permute-start.2 = (f32[40,256]{1,0:T(8,128)S(1)}, f32[40,256]{1,0:T(8,128)S(1)}, u32[]{:S(2)}, u32[]{:S(2)}) collective-permute-start(f32[40,256]{1,0:T(8,128)S(1)} %get-tuple-element.62), channel_id=1, source_target_pairs={{0,1},{1,0},{2,3},{3,2},{4,5},{5,4},{6,7},{7,6},{8,9},{9,8},{10,11... | collective-permute-start | bytes 122888 | tf_op jit(solution)/shard_map/ppermute | solution.py:904
  41.1 1.9 %collective-permute-start.3 = (f32[40,256]{1,0:T(8,128)S(1)}, f32[40,256]{1,0:T(8,128)S(1)}, u32[]{:S(2)}, u32[]{:S(2)}) collective-permute-start(f32[40,256]{1,0:T(8,128)S(1)} %get-tuple-element.63), channel_id=1, source_target_pairs={{1,2},{2,1},{3,4},{4,3},{5,6},{6,5},{7,8},{8,7},{9,10},{10,9},{11,... | collective-permute-start | bytes 122888 | tf_op jit(solution)/shard_map/ppermute | solution.py:903
  43.0 1.9 %inner.1 = (f32[18,72,256]{2,1,0:T(8,128)S(1)}, f32[18,72,128]{2,1,0:T(8,128)S(1)}, f32[18,72,128]{2,1,0:T(8,128)S(1)}, f32[16,1024]{1,0:T(8,128)S(1)}) custom-call(f32[18,72,512]{2,1,0:T(8,128)S(1)} %get-tuple-element.52.next_, f32[18,72,128]{2,1,0:T(8,128)S(1)} %get-tuple-element.53.next_south, f32[18,72,128]{2,1,0:T(8,128)S(1)} %get-tuple-element.54.next_north, ...), custom_call_target="tpu_custom_call" | custom-call | flops 4194304 | bytes 4194304 | tf_op jit(solution)/shard_map/inner/pallas_call | solution.py:135
  45.0 0.0 collective-permute-done.2.back_a
  45.0 1.4 %collective-permute-done.3.back_b = f32[40,256]{1,0:T(8,128)S(1)} collective-permute-done((f32[40,256]{1,0:T(8,128)S(1)}, f32[40,256]{1,0:T(8,128)S(1)}, u32[]{:S(2)}, u32[]{:S(2)}) %collective-permute-start.3) | collective-permute-done | bytes 40992 | tf_op jit(solution)/shard_map/ppermute | solution.py:903
  46.4 5.8 %last.1 = (f32[18,72,512]{2,1,0:T(8,128)}, f32[2,512]{1,0:T(2,128)}) custom-call(f32[18,72,512]{2,1,0:T(8,128)S(1)} %get-tuple-element.52.next_, f32[18,72,512]{2,1,0:T(8,128)S(1)} %get-tuple-element.44.factor, f32[18,72,128]{2,1,0:T(8,128)S(1)} %get-tuple-element.57.factor_south, f32[18,72,128]{2,1,0:T(8,128)S(1)} %get-tuple-element.58.factor_north, ...), custom_call_target="tpu_custom_call" | custom-call | tf_op jit(solution)/shard_map/last/pallas_call | solution.py:135
  (3 shorter events, 0.0 us)
Async XLA Ops:
  0.6 10.1 %copy-start = (f32[4,72,128]{2,1,0:T(8,128)S(1)}, f32[4,72,128]{2,1,0:T(8,128)}, u32[]{:S(2)}) copy-start(f32[4,72,128]{2,1,0:T(8,128)} %constant.2.clone.refs_7_) | copy-start | bytes 442372
  0.6 0.7 %copy-start.1 = (s32[512]{0:T(512)S(1)}, s32[512]{0:T(512)}, u32[]{:S(2)}) copy-start(s32[512]{0:T(512)} %param.14) | copy-start | bytes 6148
  1.4 9.1 %copy-start.8 = (f32[1296]{0:T(1024)S(1)}, f32[1296]{0:T(1024)}, u32[]{:S(2)}) copy-start(f32[1296]{0:T(1024)} %param.16) | copy-start | bytes 15556
  1.4 9.1 %copy-start.9 = (f32[1296]{0:T(1024)S(1)}, f32[1296]{0:T(1024)}, u32[]{:S(2)}) copy-start(f32[1296]{0:T(1024)} %param.17) | copy-start | bytes 15556
  1.4 9.2 %copy-start.10 = (f32[1296]{0:T(1024)S(1)}, f32[1296]{0:T(1024)}, u32[]{:S(2)}) copy-start(f32[1296]{0:T(1024)} %param.18) | copy-start | bytes 15556
  1.4 9.2 %copy-start.11 = (s32[128,1]{0,1:T(1,128)S(1)}, s32[128,1]{0,1:T(1,128)}, u32[]{:S(2)}) copy-start(s32[128,1]{0,1:T(1,128)} %param.19) | copy-start | bytes 1540
  1.4 9.3 %copy-start.7 = (f32[128,36]{0,1:T(8,128)S(1)}, f32[128,36]{0,1:T(8,128)}, u32[]{:S(2)}) copy-start(f32[128,36]{0,1:T(8,128)} %param.21) | copy-start | bytes 55300
  1.4 9.4 %copy-start.2 = (s32[512]{0:T(512)S(1)}, s32[512]{0:T(512)}, u32[]{:S(2)}) copy-start(s32[512]{0:T(512)} %param.14) | copy-start | bytes 6148
  1.4 9.4 %copy-start.3 = (f32[2,512]{1,0:T(2,128)S(1)}, f32[2,512]{1,0:T(2,128)}, u32[]{:S(2)}) copy-start(f32[2,512]{1,0:T(2,128)} %refs_3_.3) | copy-start | bytes 12292
  1.4 9.4 %copy-start.4 = (f32[36]{0:T(128)S(1)}, f32[36]{0:T(128)}, u32[]{:S(2)}) copy-start(f32[36]{0:T(128)} %refs_3_.2) | copy-start | bytes 436
  1.4 9.4 %copy-start.5 = (s32[128]{0:T(128)S(1)}, s32[128]{0:T(128)}, u32[]{:S(2)}) copy-start(s32[128]{0:T(128)} %param.20) | copy-start | bytes 1540
  1.4 9.4 %copy-start.6 = (f32[128]{0:T(128)S(1)}, f32[128]{0:T(128)}, u32[]{:S(2)}) copy-start(f32[128]{0:T(128)} %param.22) | copy-start | bytes 1540
  4.0 28.9 %collective-permute-start = (f32[9,72,256]{2,1,0:T(8,128)S(1)}, f32[9,72,256]{2,1,0:T(8,128)S(1)}, u32[]{:S(2)}, u32[]{:S(2)}) collective-permute-start(f32[9,72,256]{2,1,0:T(8,128)S(1)} %get-tuple-element.46), channel_id=1, source_target_pairs={{0,1},{1,2},{2,3},{3,4},{4,5},{5,6},{6,7},{7,8},{8,9},{9,10},{10,1... | collective-permute-start | bytes 1990664 | tf_op jit(solution)/shard_map/ppermute | solution.py:878
  8.5 24.4 %collective-permute-start.1 = (f32[9,72,256]{2,1,0:T(8,128)S(1)}, f32[9,72,256]{2,1,0:T(8,128)S(1)}, u32[]{:S(2)}, u32[]{:S(2)}) collective-permute-start(f32[9,72,256]{2,1,0:T(8,128)S(1)} %get-tuple-element.47), channel_id=1, source_target_pairs={{1,0},{2,1},{3,2},{4,3},{5,4},{6,5},{7,6},{8,7},{9,8},{10,9},{11,1... | collective-permute-start | bytes 1990664 | tf_op jit(solution)/shard_map/ppermute | solution.py:879
  39.9 5.1 %collective-permute-start.2 = (f32[40,256]{1,0:T(8,128)S(1)}, f32[40,256]{1,0:T(8,128)S(1)}, u32[]{:S(2)}, u32[]{:S(2)}) collective-permute-start(f32[40,256]{1,0:T(8,128)S(1)} %get-tuple-element.62), channel_id=1, source_target_pairs={{0,1},{1,0},{2,3},{3,2},{4,5},{5,4},{6,7},{7,6},{8,9},{9,8},{10,11... | collective-permute-start | bytes 122888 | tf_op jit(solution)/shard_map/ppermute | solution.py:904
  41.1 5.3 %collective-permute-start.3 = (f32[40,256]{1,0:T(8,128)S(1)}, f32[40,256]{1,0:T(8,128)S(1)}, u32[]{:S(2)}, u32[]{:S(2)}) collective-permute-start(f32[40,256]{1,0:T(8,128)S(1)} %get-tuple-element.63), channel_id=1, source_target_pairs={{1,2},{2,1},{3,4},{4,3},{5,6},{6,5},{7,8},{8,7},{9,10},{10,9},{11,... | collective-permute-start | bytes 122888 | tf_op jit(solution)/shard_map/ppermute | solution.py:903

commit v3 on v2

--- a/solution.py
+++ b/solution.py
@@ -19,6 +19,7 @@
 GROUPS = NB // GROUP
 CHUNKS = 6
 F32 = jnp.float32
+BF16 = jnp.bfloat16
 LIMIT = 14 * 1024 * 1024
 LOG2E = math.log2(math.e)
 LN2 = math.log(2.0)
@@ -28,6 +29,9 @@
 EDGE = (GROUPS, GROUP, W)
 EDGES = (GROUPS, GROUP, 2 * W)
 BINS = (NB, W)
+HALF = NB // 2
+HALO = (HALF + SUB, 2 * W)
+LOAD = 40
 STATE = (16, 8 * W)
 STEEP0, WIND0, WIND1, SEA, STEEP1, TEND1, GRAD1, TEND0, GRAD0, PASS0 = range(10)
 
@@ -120,6 +124,15 @@
 
 def full(value):
     return jnp.broadcast_to(value, (SUB, W))
+
+
+def loop(low, high, by, body, init):
+    def passes(index, carry):
+        for k in range(by):
+            carry = body(low + index * by + k, carry)
+        return carry
+
+    return lax.fori_loop(0, (high - low) // by, passes, init)
 
 
 def whole(memory=pltpu.VMEM):
@@ -145,56 +158,104 @@
     )(*operands)
 
 
-def pack_kernel(field, sea_in, north, south):
+def pack_rows(cell, put, sub, north):
+    both = (sub < 2) | ((sub >= 4) & (sub < 6))
+    for row in range(2):
+        rest = []
+        for half in range(2):
+            for place, tile in enumerate((0, 1, 5) if north else (3, 7, 8)):
+                put(half * 4 + place, row, cell(half, tile, row))
+            second, fourth, sixth = [cell(half, tile, row) for tile in (2, 4, 6)]
+            if north:
+                put(half * 4 + 3, row, jnp.where(sub < 2, second, jnp.where(sub < 4, sixth, fourth)))
+                rest.append(sixth)
+            else:
+                put(half * 4 + 3, row, jnp.where(sub < 4, fourth, second))
+                rest.append(jnp.where(sub < 4, second, sixth))
+        other = pltpu.roll(rest[1], 2, 0)
+        put(8, row, jnp.where(both, rest[0], other) if north else jnp.where(both, other, rest[0]))
+
+
+def pack_all(cells, base, sea, out, low, high, north):
     sub = sublane()
-    both = (sub < 2) | ((sub >= 4) & (sub < 6))
-    sea = [full(sea_in[:, lanes(r)].astype(F32)) for r in range(ROWS)]
-    for pair in range(field.shape[0] // 2):
-        for row in range(2):
-
-            def cell(half, tile, base):
-                return field[2 * pair + half, pl.ds(tile * SUB, SUB), lanes(base + row)] * sea[base + row]
-
-            def put(ref, tile, value):
-                ref[pair, pl.ds(tile * SUB, SUB), lanes(row)] = value
-
-            rest = []
-            for half in range(2):
-                sixth = cell(half, 6, 2)
-                for place, tile in enumerate((0, 1, 5)):
-                    put(north, half * 4 + place, cell(half, tile, 2))
-                mixed = jnp.where(sub < 2, cell(half, 2, 2), jnp.where(sub < 4, sixth, cell(half, 4, 2)))
-                put(north, half * 4 + 3, mixed)
-                rest.append(sixth)
-            put(north, 8, jnp.where(both, rest[0], pltpu.roll(rest[1], 2, 0)))
-            rest = []
-            for half in range(2):
-                second = cell(half, 2, 0)
-                for place, tile in enumerate((3, 7, 8)):
-                    put(south, half * 4 + place, cell(half, tile, 0))
-                put(south, half * 4 + 3, jnp.where(sub < 4, cell(half, 4, 0), second))
-                rest.append(jnp.where(sub < 4, second, cell(half, 6, 0)))
-            put(south, 8, jnp.where(both, pltpu.roll(rest[1], 2, 0), rest[0]))
-
-
-def pack(field, sea):
-    steps = 3
-    each = GROUPS // steps
-    half = jax.ShapeDtypeStruct((GROUPS // 2, GROUP, 2 * W), F32)
-    return pl.pallas_call(
-        pack_kernel,
-        grid=(steps,),
-        in_specs=[pl.BlockSpec((each, GROUP, ROWS * W), lambda i: (i, 0, 0)), whole()],
-        out_specs=[pl.BlockSpec((each // 2, GROUP, 2 * W), lambda i: (i, 0, 0))] * 2,
-        out_shape=[half, half],
-        compiler_params=pltpu.CompilerParams(vmem_limit_bytes=LIMIT),
-        name="pack",
-    )(pltpu.with_memory_space_constraint(field, pltpu.HBM), sea)
+
+    def step(pair, carry):
+        def cell(half, tile, row):
+            return cells[2 * pair + half, pl.ds(tile * SUB, SUB), pl.ds(base + row * W, W)] * sea[row]
+
+        def put(tile, row, value):
+            out[pl.ds(pl.multiple_of(pair * GROUP + tile * SUB, SUB), SUB), lanes(row)] = value
+
+        pack_rows(cell, put, sub, north)
+        return carry
+
+    loop(low, high, 1, step, 0)
+
+
+def pack_small(out, wind, sea, base):
+    here = pl.ds(base * W, 2 * W)
+    out[pl.ds(HALF, SUB), :] = jnp.zeros((SUB, 2 * W), F32)
+    out[HALF : HALF + 2, :] = wind[:, here]
+    out[HALF + 2 : HALF + 3, :] = sea[:, here].astype(F32)
+
+
+def far_kernel(field, sea_in, wind_in, out, cells, sea, wind, sems):
+    even = lax.rem(lax.axis_index("geo"), 2) == 0
+    each = GROUPS // 3
+    lane = pl.multiple_of(jnp.where(even, 0, 2 * W), 2 * W)
+    small = [
+        pltpu.make_async_copy(sea_in, sea, sems.at[3]),
+        pltpu.make_async_copy(wind_in, wind, sems.at[4]),
+    ]
+    copies = []
+    for c in range(3):
+        here = pl.ds(c * each, each)
+        copies.append(pltpu.make_async_copy(field.at[here, :, pl.ds(lane, 2 * W)], cells.at[here], sems.at[c]))
+    for copy in small + copies:
+        copy.start()
+    for copy in small:
+        copy.wait()
+    for c in range(3):
+        copies[c].wait()
+
+        @pl.when(even)
+        def _():
+            mask = [full(sea[:, lanes(r)].astype(F32)) for r in (0, 1)]
+            pack_all(cells, 0, mask, out, c * each // 2, (c + 1) * each // 2, False)
+
+        @pl.when(jnp.logical_not(even))
+        def _():
+            mask = [full(sea[:, lanes(r)].astype(F32)) for r in (2, 3)]
+            pack_all(cells, 0, mask, out, c * each // 2, (c + 1) * each // 2, True)
+
+    @pl.when(even)
+    def _():
+        pack_small(out, wind, sea, 0)
+
+    @pl.when(jnp.logical_not(even))
+    def _():
+        pack_small(out, wind, sea, 2)
+
+
+def far_rows(field, sea, wind):
+    return call(
+        far_kernel,
+        "far",
+        [(pltpu.with_memory_space_constraint(value, pltpu.HBM), False) for value in (field, sea, wind)],
+        [(HALO, False)],
+        [
+            pltpu.VMEM((GROUPS, GROUP, 2 * W), F32),
+            pltpu.VMEM((1, ROWS * W), jnp.int32),
+            pltpu.VMEM((2, ROWS * W), F32),
+            pltpu.SemaphoreType.DMA((5,)),
+        ],
+        away=(0, 1, 2),
+    )[0]
 
 
 def unpack_north(halo, pair, half, row, sub):
     def get(tile):
-        return halo[pair, pl.ds(tile * SUB, SUB), lanes(row)]
+        return halo[pl.ds(pl.multiple_of(pair * GROUP + tile * SUB, SUB), SUB), lanes(row)]
 
     mixed, last = get(half * 4 + 3), get(8)
     if half:
@@ -211,7 +272,7 @@
 
 def unpack_south(halo, pair, half, row, sub):
     def get(tile):
-        return halo[pair, pl.ds(tile * SUB, SUB), lanes(row)]
+        return halo[pl.ds(pl.multiple_of(pair * GROUP + tile * SUB, SUB), SUB), lanes(row)]
 
     mixed, last = get(half * 4 + 3), get(8)
     if half:
@@ -226,52 +287,77 @@
     }
 
 
-def spread(row_ref, out, scale):
-    for start in range(0, NB, W):
-        size = min(W, NB - start)
-        chunk = row_ref[:, pl.ds(start, size)] * scale
-        out[pl.ds(start, size), :] = jnp.transpose(jnp.broadcast_to(chunk, (W, size)))
+def pieces(value):
+    high = value.astype(BF16)
+    value = value - high.astype(F32)
+    middle = value.astype(BF16)
+    return high, middle, (value - middle.astype(F32)).astype(BF16)
+
+
+def spread(inputs, outputs, flat):
+    flat[...] = jnp.zeros_like(flat)
+    for place, (row, scale) in enumerate(inputs):
+        for k, piece in enumerate(pieces(row[...] * scale)):
+            flat[3 * place + k : 3 * place + k + 1, 0:NB] = piece.astype(F32)
+    count = len(outputs)
+    shape = (flat.shape[0], count * W)
+    row, lane = lax.broadcasted_iota(jnp.int32, shape, 0), lax.broadcasted_iota(jnp.int32, shape, 1)
+    mask = jnp.zeros(shape, F32)
+    for place in range(count):
+        mine = (row >= 3 * place) & (row < 3 * place + 3) & (lane >= place * W) & (lane < place * W + W)
+        mask = jnp.where(mine, 1.0, mask)
+    wide = lax.dot_general(
+        flat[...].astype(BF16), mask.astype(BF16), (((0,), (0,)), ((), ())), preferred_element_type=F32
+    )
+    for place, out in enumerate(outputs):
+        out[...] = wide[0:NB, place * W : (place + 1) * W]
 
 
 def layout(rows, ranks):
-    lines = max(2, 2 * rows // ranks) // 2
-    return lines, -(-(lines + 7) // SUB) * SUB
-
-
-def sort(owner, point, value, weight, flat, load, ranks):
-    rows = owner.shape[0]
+    lines = -(-max(2, 2 * rows // ranks) // 3)
+    return lines, -(-(lines + 2) // SUB) * SUB
+
+
+def sort(owner, point, value, weight, ranks):
+    rows = owner.shape[1]
     lines, block = layout(rows, ranks)
-    flat[...] = jnp.zeros_like(flat)
-    flat[0:1, :] = point[...].astype(F32)
-    flat[1:2, :] = weight[...]
-    columns = jnp.transpose(flat[...])
-    load[...] = jnp.zeros_like(load)
-    for half in range(2):
-        here, base = pl.ds(half * rows, rows), half * (W // 2)
-        load[here, pl.ds(base, NF)] = value[...] * columns[:, 1:2]
-        load[here, pl.ds(base + NF, 1)] = columns[:, 1:2]
-        load[here, pl.ds(base + NF + 1, 1)] = columns[:, 0:1]
-    hits = (owner[...] == lax.broadcasted_iota(jnp.int32, (rows, ranks), 1)).astype(F32)
-    before = lax.broadcasted_iota(jnp.int32, (rows, rows), 1) < lax.broadcasted_iota(jnp.int32, (rows, rows), 0)
-    counts = jnp.dot(before.astype(F32), hits, preferred_element_type=F32)
-    order = jnp.sum(counts * hits, axis=1, keepdims=True).astype(jnp.int32)
-    target = owner[...] * block + order // 2
-    odd = order % 2
-    spots = lax.broadcasted_iota(jnp.int32, (rows, ranks * block), 1)
-    places = [((target == spots) & (odd == half)).astype(F32) for half in range(2)]
-    return lax.dot_general(
-        jnp.concatenate(places, axis=0),
-        load[...],
-        (((0,), (0,)), ((), ())),
-        precision=lax.Precision.HIGHEST,
-        preferred_element_type=F32,
-    )
+    hits = owner[...] == lax.broadcasted_iota(jnp.int32, (ranks, rows), 0)
+    before = lax.broadcasted_iota(jnp.int32, (rows, rows), 0) < lax.broadcasted_iota(jnp.int32, (rows, rows), 1)
+    counts = jnp.dot(hits.astype(F32).astype(BF16), before.astype(F32).astype(BF16), preferred_element_type=F32)
+    order = jnp.sum(jnp.where(hits, counts, 0.0), axis=0, keepdims=True).astype(jnp.int32)
+    line = (order * 171) >> 9
+    third = order - 3 * line
+    target = owner[...] * block + line
+    spots = lax.broadcasted_iota(jnp.int32, (ranks * block, rows), 0)
+    places = [((target == spots) & (third == k)).astype(F32).astype(BF16) for k in range(3)]
+    load = jnp.concatenate(
+        [
+            value[...] * weight[...],
+            weight[...],
+            point[...].astype(F32),
+            jnp.zeros((LOAD - NF - 2, rows), F32),
+        ],
+        axis=0,
+    )
+    loads = [
+        jnp.concatenate(
+            [jnp.zeros((LOAD * k, rows), F32)] * (k > 0) + [load, jnp.zeros((W - LOAD * (k + 1), rows), F32)], axis=0
+        )
+        for k in range(3)
+    ]
+    places = jnp.concatenate(places, axis=1)
+    result = 0.0
+    for piece in zip(*[pieces(part) for part in loads]):
+        result = result + lax.dot_general(
+            places, jnp.concatenate(piece, axis=1), (((1,), (1,)), ((), ())), preferred_element_type=F32
+        )
+    return result
 
 
 def local_kernel(
     field, sea_in, wind, courant, rate_in, damp_in, steep_in, table, owner, point, value, weight,
-    flow, rate, damp, steep, centre, ahead, back, across, own, slots,
-    cells, flat, load, sems, *, ranks,
+    flow, rate, damp, steep, centre, ahead, back, across, own, slots, near_out,
+    cells, flat, sems, *, ranks,
 ):
     sub = sublane()
     each = GROUPS // CHUNKS
@@ -281,10 +367,8 @@
     ]
     for copy in copies:
         copy.start()
-    spread(rate_in, rate, LOG2E)
-    spread(damp_in, damp, LOG2E)
-    spread(steep_in, steep, 1.0)
-    slots[...] = sort(owner, point, value, weight, flat, load, ranks)
+    spread(((rate_in, LOG2E), (damp_in, LOG2E), (steep_in, 1.0)), (rate, damp, steep), flat)
+    slots[...] = sort(owner, point, value, weight, ranks)
     sea = [full(sea_in[:, lanes(r)].astype(F32)) for r in range(ROWS)]
     zero = jnp.zeros((SUB, W), F32)
 
@@ -317,7 +401,7 @@
     sums = (zero,) * (ROWS + 2)
     for c in range(CHUNKS):
         copies[c].wait()
-        sums = lax.fori_loop(c * each, (c + 1) * each, step, sums)
+        sums = loop(c * each, (c + 1) * each, 3, step, sums)
     sums = [total(value) for value in sums]
     own[...] = jnp.zeros_like(own)
     for r in range(ROWS):
@@ -325,37 +409,37 @@
     own[1:2, lanes(ROWS - 1)] = sums[ROWS]
     own[1:2, lanes(0)] = sums[ROWS + 1]
 
-    lines, block = layout(owner.shape[0], ranks)
+    _, block = layout(owner.shape[1], ranks)
     me = lax.axis_index("geo")
 
-    def hand(near, far, dest):
+    def hand(row, dest):
         last = pl.ds(pl.multiple_of(dest * block + block - SUB, SUB), SUB)
-        values = jnp.concatenate(
-            [
-                slots[last, :][0:1, :],
-                wind[0:1, lanes(near)],
-                wind[1:2, lanes(far)],
-                wind[1:2, lanes(near)],
-                sea[far][0:1, :],
-                sea[near][0:1, :],
-                own[0:1, lanes(near)],
-                own[1:2, lanes(near)],
-            ],
-            axis=0,
-        )
-        slots[last, :] = values
+        values = jnp.where(sub == SUB - 2, own[0:1, lanes(row)], slots[last, :])
+        slots[last, :] = jnp.where(sub == SUB - 1, own[1:2, lanes(row)], values)
 
     @pl.when(me < ranks - 1)
     def _():
-        hand(ROWS - 1, ROWS - 2, me + 1)
+        hand(ROWS - 1, me + 1)
 
     @pl.when(me > 0)
     def _():
-        hand(0, 1, me - 1)
+        hand(0, me - 1)
+
+    even = lax.rem(me, 2) == 0
+
+    @pl.when(even)
+    def _():
+        pack_all(cells, 2 * W, sea[2:4], near_out, 0, GROUPS // 2, True)
+        pack_small(near_out, wind, sea_in, 2)
+
+    @pl.when(jnp.logical_not(even))
+    def _():
+        pack_all(cells, 0, sea[0:2], near_out, 0, GROUPS // 2, False)
+        pack_small(near_out, wind, sea_in, 0)
 
 
 def local(field, sea, wind, courant, rate, damp, steep, table, owner, point, value, weight, ranks):
-    rows = owner.shape[0]
+    rows = owner.shape[1]
     _, block = layout(rows, ranks)
 
     def kernel(*refs):
@@ -369,11 +453,10 @@
         kernel,
         "local",
         [(arg, False) for arg in args],
-        [(CELLS, True)] + [(BINS, True)] * 7 + [((SUB, ROWS * W), True), ((ranks * block, W), False)],
+        [(CELLS, True)] + [(BINS, True)] * 7 + [((SUB, ROWS * W), True), ((ranks * block, W), False), (HALO, False)],
         [
             pltpu.VMEM(CELLS, F32),
-            pltpu.VMEM((SUB, rows), F32),
-            pltpu.VMEM((2 * rows, W), F32),
+            pltpu.VMEM((16, 11 * W), F32),
             pltpu.SemaphoreType.DMA((CHUNKS,)),
         ],
         smem=(3,),
@@ -384,20 +467,22 @@
 def place(arrived, ranks, rows, wanted, gain):
     lines, block = layout(rows, ranks)
     size = ranks * block
-    held = lax.rem(lax.broadcasted_iota(jnp.int32, (size, W), 0), block) < lines
+    shape = (size, W)
+    lane = lax.broadcasted_iota(jnp.int32, shape, 1)
+    held = lax.rem(lax.broadcasted_iota(jnp.int32, shape, 0), block) < lines
     load = jnp.where(held, arrived[...], 0.0)
+    spots = lax.broadcasted_iota(jnp.int32, (size, ROWS * W), 1)
     sums = 0.0
-    for half in range(2):
-        mine = load[:, half * (W // 2) : (half + 1) * (W // 2)]
+    for k in range(3):
+        mine = pltpu.roll(load, W - LOAD * k, 1) if k else load
         point = mine[:, NF + 1 : NF + 2].astype(jnp.int32)
-        hits = (point == lax.broadcasted_iota(jnp.int32, (size, ROWS * W), 1)).astype(F32)
+        hits = (point == spots).astype(F32).astype(BF16)
+        high, middle, low = [piece.astype(F32) for piece in pieces(jnp.where(lane < LOAD, mine, 0.0))]
+        mine = high + pltpu.roll(middle, LOAD, 1) + pltpu.roll(low, 2 * LOAD, 1)
         sums = sums + lax.dot_general(
-            mine,
-            hits,
-            (((0,), (0,)), ((), ())),
-            precision=lax.Precision.HIGHEST,
-            preferred_element_type=F32,
+            mine.astype(BF16), hits, (((0,), (0,)), ((), ())), preferred_element_type=F32
         )
+    sums = sums[0:LOAD] + sums[LOAD : 2 * LOAD] + sums[2 * LOAD : 3 * LOAD]
     for f in range(NF):
         rows_of = slice(4 * (f % 2), 4 * (f % 2) + 4)
         wanted[f // 2, rows_of, :] = jnp.broadcast_to(sums[f : f + 1, :] * (1.0 / ND), (4, ROWS * W))
@@ -420,12 +505,6 @@
 
     south, north = aux(me - 1, me > 0), aux(me + 1, me < ranks - 1)
     state[...] = jnp.zeros_like(state)
-    for near, far, values in ((-1, -2, south), (4, 5, north)):
-        state[WIND0 : WIND0 + 1, column(near)] = values[1:2, :]
-        state[WIND1 : WIND1 + 1, column(far)] = values[2:3, :]
-        state[WIND1 : WIND1 + 1, column(near)] = values[3:4, :]
-        state[SEA : SEA + 1, column(far)] = values[4:5, :]
-        state[SEA : SEA + 1, column(near)] = values[5:6, :]
     here = pl.ds(2 * W, ROWS * W)
     state[WIND0 : WIND0 + 1, here] = wind[0:1, :]
     state[WIND1 : WIND1 + 1, here] = wind[1:2, :]
@@ -433,10 +512,10 @@
     steeps = {r: own[0:1, lanes(r)] for r in range(ROWS)}
     steeps[0] = steeps[0] + south[7:8, :]
     steeps[3] = steeps[3] + north[7:8, :]
-    steeps[-1] = south[6:7, :] + own[1:2, lanes(0)]
-    steeps[4] = north[6:7, :] + own[1:2, lanes(3)]
     for r, value in steeps.items():
         state[STEEP0 : STEEP0 + 1, column(r)] = jnp.where(state[SEA : SEA + 1, column(r)] > 0.5, value, LAND)
+    state[STEEP0 : STEEP0 + 1, column(-1)] = south[6:7, :] + own[1:2, lanes(0)]
+    state[STEEP0 : STEEP0 + 1, column(4)] = north[6:7, :] + own[1:2, lanes(3)]
     steep0 = [full(state[STEEP0 : STEEP0 + 1, column(r)]) for r in range(ROWS)]
     wind0 = [full(state[WIND0 : WIND0 + 1, column(r)]) for r in range(ROWS)]
 
@@ -459,7 +538,7 @@
                 sums[r] = sums[r] + heavy * value
         return tuple(sums)
 
-    sums = lax.fori_loop(0, GROUPS, step, (jnp.zeros((SUB, W), F32),) * ROWS)
+    sums = loop(0, GROUPS, 3, step, (jnp.zeros((SUB, W), F32),) * ROWS)
     for r in range(ROWS):
         state[STEEP1 : STEEP1 + 1, column(r)] = total(sums[r])
 
@@ -487,21 +566,44 @@
 
 
 def late_kernel(
-    next_in, factor, moved, from_south, from_north, wanted, gain, state_in, rate, damp, steep, centre, ahead, back, across,
+    next_in, factor, moved, from_far, from_near, wanted, gain, state_in, rate, damp, steep, centre, ahead, back, across,
     next_, next_south, next_north, source, edges, state, send_a, send_b,
     fixed, growth, lam, halo_south, halo_north, sems,
 ):
     sub = sublane()
     zero = jnp.zeros((SUB, W), F32)
-    each = GROUPS // 2 // 3
-    copies = []
-    for c in range(3):
-        here = pl.ds(c * each, each)
-        copies.append(pltpu.make_async_copy(from_south.at[here], halo_south.at[here], sems.at[2 * c]))
-        copies.append(pltpu.make_async_copy(from_north.at[here], halo_north.at[here], sems.at[2 * c + 1]))
-    for copy in copies:
-        copy.start()
+    even = lax.rem(lax.axis_index("geo"), 2) == 0
+    each = HALF // 3
+    parts = [pl.ds(HALF, SUB)] + [pl.ds(c * each, each) for c in range(3)]
+
+    def bring(first, second):
+        copies = []
+        for c, here in enumerate(parts):
+            copies.append(pltpu.make_async_copy(first.at[here], halo_south.at[here], sems.at[2 * c]))
+            copies.append(pltpu.make_async_copy(second.at[here], halo_north.at[here], sems.at[2 * c + 1]))
+        return copies
+
+    @pl.when(even)
+    def _():
+        for copy in bring(from_far, from_near):
+            copy.start()
+
+    @pl.when(jnp.logical_not(even))
+    def _():
+        for copy in bring(from_near, from_far):
+            copy.start()
+
+    copies = bring(from_far, from_near)
+    copies[0].wait()
+    copies[1].wait()
     state[...] = state_in[...]
+    for halo, rows in ((halo_south, (-2, -1)), (halo_north, (4, 5))):
+        here = pl.ds((rows[0] + 2) * W, 2 * W)
+        for place, name in enumerate((WIND0, WIND1, SEA)):
+            state[name : name + 1, here] = halo[HALF + place : HALF + place + 1, :]
+    for r in (-1, 4):
+        known = state[SEA : SEA + 1, column(r)] > 0.5
+        state[STEEP0 : STEEP0 + 1, column(r)] = jnp.where(known, state[STEEP0 : STEEP0 + 1, column(r)], LAND)
 
     def held(place, r):
         return full(state[place : place + 1, column(r)])
@@ -552,9 +654,9 @@
 
     sums = (zero,) * ROWS
     for c in range(3):
-        copies[2 * c].wait()
-        copies[2 * c + 1].wait()
-        sums = lax.fori_loop(c * each, (c + 1) * each, first, sums)
+        copies[2 * c + 2].wait()
+        copies[2 * c + 3].wait()
+        sums = loop(3 * c, 3 * c + 3, 3, first, sums)
     for r in range(ROWS):
         value = state[STEEP1 : STEEP1 + 1, column(r)] + total(sums[r])
         state[STEEP1 : STEEP1 + 1, column(r)] = jnp.where(state[SEA : SEA + 1, column(r)] > 0.5, value, LAND)
@@ -595,7 +697,7 @@
             sums[ROWS + r] = sums[ROWS + r] + (up * downs[r][0] + down * downs[r][1])
         return tuple(sums)
 
-    sums = lax.fori_loop(0, GROUPS, second, (zero,) * (2 * ROWS))
+    sums = loop(0, GROUPS, 1, second, (zero,) * (2 * ROWS))
     for r in range(ROWS):
         state[GRAD1 : GRAD1 + 1, column(r)] = total(sums[r]) * LN2
         state[TEND1 : TEND1 + 1, column(r)] = total(sums[ROWS + r]) * (-LN2)
@@ -620,7 +722,7 @@
                 sums[2 + place] = sums[2 + place] + fade * value
         return tuple(sums)
 
-    sums = lax.fori_loop(0, GROUPS, third, (zero,) * 4)
+    sums = loop(0, GROUPS, 3, third, (zero,) * 4)
     for place, r in enumerate((0, ROWS - 1)):
         state[GRAD0 : GRAD0 + 1, column(r)] = total(sums[place]) * LN2
         state[TEND0 : TEND0 + 1, column(r)] = total(sums[2 + place]) * (-LN2)
@@ -632,8 +734,6 @@
         for place, name in enumerate((STEEP1, TEND1, TEND0, TEND0)):
             ref[NF + place : NF + place + 1, :] = state[name : name + 1, here]
 
-    even = lax.rem(lax.axis_index("geo"), 2) == 0
-
     @pl.when(even)
     def _():
         fill(send_a, 2)
@@ -645,10 +745,9 @@
         fill(send_b, 2)
 
 
-def late(next_, factor, moved, from_south, from_north, wanted, gain, state, coefficients):
-    inputs = [(next_, True), (factor, True), (moved, True), (from_south, False), (from_north, False)]
+def late(next_, factor, moved, from_far, from_near, wanted, gain, state, coefficients):
+    inputs = [(next_, True), (factor, True), (moved, True), (from_far, False), (from_near, False)]
     inputs += [(value, True) for value in (wanted, gain, state) + coefficients]
-    halo = (GROUPS // 2, GROUP, 2 * W)
     return call(
         late_kernel,
         "late",
@@ -659,9 +758,9 @@
             pltpu.VMEM(CELLS, F32),
             pltpu.VMEM(CELLS, F32),
             pltpu.VMEM((GROUPS, SUB, ROWS * W), F32),
-            pltpu.VMEM(halo, F32),
-            pltpu.VMEM(halo, F32),
-            pltpu.SemaphoreType.DMA((6,)),
+            pltpu.VMEM(HALO, F32),
+            pltpu.VMEM(HALO, F32),
+            pltpu.SemaphoreType.DMA((8,)),
         ],
         away=(3, 4),
         aliases={0: 0},
@@ -705,7 +804,7 @@
                 sums[5] = sums[5] + gone * value
         return tuple(sums)
 
-    sums = lax.fori_loop(0, GROUPS, step, (zero,) * 6)
+    sums = loop(0, GROUPS, 3, step, (zero,) * 6)
     for place, r in enumerate((1, 2)):
         state[GRAD0 : GRAD0 + 1, column(r)] = total(sums[place]) * LN2
         state[TEND0 : TEND0 + 1, column(r)] = total(sums[2 + place]) * (-LN2)
@@ -772,7 +871,7 @@
                 sums[2 + place] = sums[2 + place] + fade * value
         return tuple(sums)
 
-    sums = lax.fori_loop(0, GROUPS, first, (zero,) * 4)
+    sums = loop(0, GROUPS, 3, first, (zero,) * 4)
     sums = [total(value) * LN2 for value in sums]
     tend0 = {r: state[TEND0 : TEND0 + 1, column(r)] for r in range(-1, 5)}
     grad0 = [state[GRAD0 : GRAD0 + 1, column(r)] for r in range(ROWS)]
@@ -818,7 +917,7 @@
     each = GROUPS // CHUNKS
     copies = []
     for c in range(CHUNKS):
-        lax.fori_loop(c * each, (c + 1) * each, second, 0)
+        loop(c * each, (c + 1) * each, 3, second, 0)
         here = pl.ds(c * each, each)
         copies.append(pltpu.make_async_copy(cells.at[here], out.at[here], sems.at[c]))
         copies[c].start()
@@ -874,10 +973,8 @@
     near, far = swaps(count)
     field = initial_spectrum.reshape(CELLS)
     sea = sea_mask.reshape(1, ROWS * W)
-    north, south = pack(field, sea)
-    from_south = lax.ppermute(north, "geo", [(i, i + 1) for i in range(count - 1)])
-    from_north = lax.ppermute(south, "geo", [(i + 1, i) for i in range(count - 1)])
-    flow, rate, damp, steep, centre, ahead, back, across, own, slots = local(
+    from_far = lax.ppermute(far_rows(field, sea, wind_forcing), "geo", far)
+    flow, rate, damp, steep, centre, ahead, back, across, own, slots, rows = local(
         field,
         sea,
         wind_forcing,
@@ -886,18 +983,19 @@
         damping.reshape(1, NB),
         steep_weight.reshape(1, NB),
         jnp.asarray(direction_tables()),
-        obs_owner,
+        obs_owner.reshape(1, held),
         obs_point.reshape(1, held),
-        obs_value,
+        obs_value.T,
         obs_weight.reshape(1, held),
         count,
     )
+    from_near = lax.ppermute(rows, "geo", near)
     arrived = lax.all_to_all(slots, "geo", split_axis=0, concat_axis=0, tiled=True)
     next_, factor, moved, wanted, gain, state = early(
         arrived, flow, own, wind_forcing, sea, rate, damp, steep, centre, ahead, across, count, held
     )
     next_, next_south, next_north, source, edges, state, send_a, send_b = late(
-        next_, factor, moved, from_south, from_north, wanted, gain, state,
+        next_, factor, moved, from_far, from_near, wanted, gain, state,
         (rate, damp, steep, centre, ahead, back, across),
     )
     back_b = lax.ppermute(send_b, "geo", far)

time: 52.5 us -> 41.3 us (0.79); the launches traced: 52.3 us -> 40.5 us
  Pallas kernels: 26.2 us -> 18.4 us
  blocking collectives: 13.1 us -> 11.4 us
  local copies, waits for them, and re-layouts: 0.99 us -> 0.07 us
  waiting for transfers between devices: 1.44 us -> 0.56 us
    pallas_call x5 -> x6, Pallas kernels: 23.7 us -> 18.4 us  [call(): pl.pallas_call(kernel, in_specs=specs, out_specs=[whole(pl.ANY if place i...]
    pallas_call x1 -> x0, Pallas kernels: 2.58 us -> none  [pack(): pl.pallas_call(pack_kernel, grid=(steps,), in_specs=[pl.BlockSpec((each,...]
    ppermute x2, starting transfers between devices: 6.43 us -> 4.58 us  [the longest x1 4.51 us: body(): from_far = lax.ppermute(far_rows(field, sea, wind_forcing), 'geo', far)]
    ppermute x1, starting transfers between devices: 1.91 us -> 3.67 us  [body(): back_b = lax.ppermute(send_b, 'geo', far)]
    all_to_all x1, blocking collectives: 13.1 us -> 11.4 us  [body(): lax.all_to_all(slots, 'geo', split_axis=0, concat_axis=0, tiled=True)]
    unnamed x26 -> x22, local copies, waits for them, and re-layouts: 0.98 us -> 0.05 us
    ppermute x1, waiting for transfers between devices: 1.43 us -> 0.56 us  [body(): back_b = lax.ppermute(send_b, 'geo', far)]
  transfers between devices with their start and end apart: 4 -> 4, of which waited for: 1 -> 1; matrix products, arithmetic and copies ran while one was open for 0% -> 0% of each run, Pallas kernels for 21% -> 18%
where the time goes in v3:
time: 41.3 us; the launch traced here: 40.5 us
  Pallas kernels  18.4 us (45%)
  blocking collectives  11.4 us (28%)
  starting transfers between devices  9.1 us (22%)
  between operations  0.92 us (2%)
  waiting for transfers between devices  0.56 us (1%)
    pallas_call x6, Pallas kernels, call(): pl.pallas_call(kernel, in_specs=specs, out_specs=[whole(pl.ANY if place i...  18.4 us
    all_to_all x1, blocking collectives, body(): lax.all_to_all(slots, 'geo', split_axis=0, concat_axis=0, tiled=True)  11.4 us
    ppermute x1, starting transfers between devices, body(): from_far = lax.ppermute(far_rows(field, sea, wind_forcing), 'geo', far)  4.51 us
    ppermute x1, starting transfers between devices, body(): back_b = lax.ppermute(send_b, 'geo', far)  3.67 us
    ppermute x1, starting transfers between devices, body(): back_a = lax.ppermute(send_a, 'geo', near)  0.84 us
  transfers between devices with their start and end apart: 4, of which 1 were waited for; matrix products, arithmetic and copies ran while one was open for 0% of the time, Pallas kernels for 18%

profile of v3, /device:TPU:1, one launch (start us, length us, event | category | flops | bytes accessed | tf_op | source)
XLA Modules:
  0.0 40.5 jit_solution(17943686486926186864)
XLA Ops:
  0.6 0.0 copy-start
  0.6 0.0 copy-start.1
  0.7 0.0 copy-start.3
  0.7 0.0 copy-start.8
  0.7 0.0 copy-start.9
  0.7 0.0 copy-start.10
  0.7 0.0 copy-start.7
  0.7 0.0 copy-start.2
  0.7 0.0 copy-start.6
  0.7 0.0 copy-start.5
  0.7 0.0 copy-start.4
  0.7 1.5 %far.1 = f32[656,256]{1,0:T(8,128)S(1)} custom-call(f32[18,72,512]{2,1,0:T(8,128)} %bitcast.18, s32[1,512]{1,0:T(1,128)} %bitcast.12, f32[2,512]{1,0:T(2,128)} %wind_in.1), custom_call_target="tpu_custom_call" | custom-call | tf_op jit(solution)/shard_map/far/pallas_call | solution.py:148
  2.2 4.5 %collective-permute-start = (f32[656,256]{1,0:T(8,128)S(1)}, f32[656,256]{1,0:T(8,128)S(1)}, u32[]{:S(2)}, u32[]{:S(2)}) collective-permute-start(f32[656,256]{1,0:T(8,128)S(1)} %far.1), channel_id=1, source_target_pairs={{1,2},{2,1},{3,4},{4,3},{5,6},{6,5},{7,8},{8,7},{9,10},{10,9},{11,... | collective-permute-start | bytes 2015240 | tf_op jit(solution)/shard_map/ppermute | solution.py:976
  6.8 0.0 copy-done.8
  6.8 0.0 copy-done.9
  6.8 0.0 copy-done.10
  6.8 0.0 copy-done
  6.8 0.0 copy-done.1
  6.9 0.0 copy-done.3
  6.9 0.0 copy-done.7
  6.9 0.0 copy-done.2
  6.9 0.0 copy-done.6
  6.9 0.0 copy-done.5
  6.9 0.0 copy-done.4
  6.9 4.0 %local.1 = (f32[18,72,512]{2,1,0:T(8,128)S(1)}, f32[1296,128]{1,0:T(8,128)S(1)}, f32[1296,128]{1,0:T(8,128)S(1)}, f32[1296,128]{1,0:T(8,128)S(1)}, f32[1296,128]...) custom-call(f32[18,72,512]{2,1,0:T(8,128)} %bitcast.19, ...), custom_call_target="tpu_custom_call" | custom-call | tf_op jit(solution)/shard_map/local/pallas_call | solution.py:148
  10.9 0.1 collective-permute-start.1
  11.0 11.4 %all_to_all.11 = f32[16,8,128]{2,1,0:T(8,128)S(1)} all-to-all(f32[16,8,128]{2,1,0:T(8,128)S(1)} %bitcast.10), channel_id=1, replica_groups=mesh['groups'=2,'geo'=16] {'geo'}, dimensions={0} | all-to-all | bytes 131072 | tf_op jit(solution)/shard_map/all_to_all | solution.py:993
  22.3 2.1 %early.1 = (f32[18,72,512]{2,1,0:T(8,128)S(1)}, f32[18,72,512]{2,1,0:T(8,128)S(1)}, f32[18,72,512]{2,1,0:T(8,128)S(1)}, f32[18,8,512]{2,1,0:T(8,128)S(1)}, f32[8,512]{1,0:T(8,128)S(1)}, /*index=5*/f32[16,1024]{1,0:T(8,128)S(1)}) custom-call(f32[128,128]{1,0:T(8,128)S(1)} %bitcast.9, f32[18,72,512]{2,1,0:T(8,128)S(1)} %get-tuple-element.34.refs_1_, ...), custom_call_target="tpu_custom_call" | custom-call | tf_op jit(solution)/shard_map/early/pallas_call | solution.py:148
  24.4 0.0 collective-permute-done.from_far
  24.4 0.0 collective-permute-done.1.from_near
  24.4 6.1 %late.1 = (f32[18,72,512]{2,1,0:T(8,128)S(1)}, f32[18,72,128]{2,1,0:T(8,128)S(1)}, f32[18,72,128]{2,1,0:T(8,128)S(1)}, f32[18,72,512]{2,1,0:T(8,128)S(1)}, f32[1...) custom-call(f32[18,72,512]{2,1,0:T(8,128)S(1)} %get-tuple-element.42, ...), custom_call_target="tpu_custom_call", output_to_operand_aliasing={{0}: (0, {})} | custom-call | tf_op jit(solution)/shard_map/late/pallas_call | solution.py:148
  30.5 0.8 %collective-permute-start.2 = (f32[40,256]{1,0:T(8,128)S(1)}, f32[40,256]{1,0:T(8,128)S(1)}, u32[]{:S(2)}, u32[]{:S(2)}) collective-permute-start(f32[40,256]{1,0:T(8,128)S(1)} %get-tuple-element.60), channel_id=1, source_target_pairs={{0,1},{1,0},{2,3},{3,2},{4,5},{5,4},{6,7},{7,6},{8,9},{9,8},{10,11... | collective-permute-start | bytes 122888 | tf_op jit(solution)/shard_map/ppermute | solution.py:1002
  31.4 3.7 %collective-permute-start.3 = (f32[40,256]{1,0:T(8,128)S(1)}, f32[40,256]{1,0:T(8,128)S(1)}, u32[]{:S(2)}, u32[]{:S(2)}) collective-permute-start(f32[40,256]{1,0:T(8,128)S(1)} %get-tuple-element.61), channel_id=1, source_target_pairs={{1,2},{2,1},{3,4},{4,3},{5,6},{6,5},{7,8},{8,7},{9,10},{10,9},{11,... | collective-permute-start | bytes 122888 | tf_op jit(solution)/shard_map/ppermute | solution.py:1001
  35.0 1.1 %inner.1 = (f32[18,72,256]{2,1,0:T(8,128)S(1)}, f32[18,72,128]{2,1,0:T(8,128)S(1)}, f32[18,72,128]{2,1,0:T(8,128)S(1)}, f32[16,1024]{1,0:T(8,128)S(1)}) custom-call(f32[18,72,512]{2,1,0:T(8,128)S(1)} %get-tuple-element.50.next_, f32[18,72,128]{2,1,0:T(8,128)S(1)} %get-tuple-element.51.next_south, f32[18,72,128]{2,1,0:T(8,128)S(1)} %get-tuple-element.52.next_north, ...), custom_call_target="tpu_custom_call" | custom-call | flops 4194304 | bytes 4194304 | tf_op jit(solution)/shard_map/inner/pallas_call | solution.py:148
  36.1 0.0 collective-permute-done.2.back_a
  36.2 0.6 %collective-permute-done.3.back_b = f32[40,256]{1,0:T(8,128)S(1)} collective-permute-done((f32[40,256]{1,0:T(8,128)S(1)}, f32[40,256]{1,0:T(8,128)S(1)}, u32[]{:S(2)}, u32[]{:S(2)}) %collective-permute-start.3) | collective-permute-done | bytes 40992 | tf_op jit(solution)/shard_map/ppermute | solution.py:1001
  36.7 3.7 %last.1 = (f32[18,72,512]{2,1,0:T(8,128)}, f32[2,512]{1,0:T(2,128)}) custom-call(f32[18,72,512]{2,1,0:T(8,128)S(1)} %get-tuple-element.50.next_, f32[18,72,512]{2,1,0:T(8,128)S(1)} %get-tuple-element.43.factor, f32[18,72,128]{2,1,0:T(8,128)S(1)} %get-tuple-element.55.factor_south, f32[18,72,128]{2,1,0:T(8,128)S(1)} %get-tuple-element.56.factor_north, ...), custom_call_target="tpu_custom_call" | custom-call | tf_op jit(solution)/shard_map/last/pallas_call | solution.py:148
  (3 shorter events, 0.0 us)
Async XLA Ops:
  0.6 6.2 %copy-start = (f32[4,72,128]{2,1,0:T(8,128)S(1)}, f32[4,72,128]{2,1,0:T(8,128)}, u32[]{:S(2)}) copy-start(f32[4,72,128]{2,1,0:T(8,128)} %constant.2.clone.refs_7_) | copy-start | bytes 442372
  0.6 6.2 %copy-start.1 = (f32[2,512]{1,0:T(2,128)S(1)}, f32[2,512]{1,0:T(2,128)}, u32[]{:S(2)}) copy-start(f32[2,512]{1,0:T(2,128)} %wind_in.1) | copy-start | bytes 12292
  0.7 6.2 %copy-start.3 = (s32[512]{0:T(512)S(1)}, s32[512]{0:T(512)}, u32[]{:S(2)}) copy-start(s32[512]{0:T(512)} %param.14) | copy-start | bytes 6148
  0.7 6.1 %copy-start.8 = (f32[1296]{0:T(1024)S(1)}, f32[1296]{0:T(1024)}, u32[]{:S(2)}) copy-start(f32[1296]{0:T(1024)} %param.16) | copy-start | bytes 15556
  0.7 6.1 %copy-start.9 = (f32[1296]{0:T(1024)S(1)}, f32[1296]{0:T(1024)}, u32[]{:S(2)}) copy-start(f32[1296]{0:T(1024)} %param.17) | copy-start | bytes 15556
  0.7 6.1 %copy-start.10 = (f32[1296]{0:T(1024)S(1)}, f32[1296]{0:T(1024)}, u32[]{:S(2)}) copy-start(f32[1296]{0:T(1024)} %param.18) | copy-start | bytes 15556
  0.7 6.2 %copy-start.7 = (f32[128]{0:T(128)S(1)}, f32[128]{0:T(128)}, u32[]{:S(2)}) copy-start(f32[128]{0:T(128)} %param.22) | copy-start | bytes 1540
  0.7 6.2 %copy-start.2 = (f32[128,36]{0,1:T(8,128)S(1)}, f32[128,36]{0,1:T(8,128)}, u32[]{:S(2)}) copy-start(f32[128,36]{0,1:T(8,128)} %param.21) | copy-start | bytes 55300
  0.7 6.2 %copy-start.6 = (s32[128]{0:T(128)S(1)}, s32[128]{0:T(128)}, u32[]{:S(2)}) copy-start(s32[128]{0:T(128)} %param.20) | copy-start | bytes 1540
  0.7 6.2 %copy-start.5 = (s32[128,1]{0,1:T(1,128)S(1)}, s32[128,1]{0,1:T(1,128)}, u32[]{:S(2)}) copy-start(s32[128,1]{0,1:T(1,128)} %param.19) | copy-start | bytes 1540
  0.7 6.2 %copy-start.4 = (f32[36]{0:T(128)S(1)}, f32[36]{0:T(128)}, u32[]{:S(2)}) copy-start(f32[36]{0:T(128)} %refs_3_.2) | copy-start | bytes 436
  2.2 22.2 %collective-permute-start = (f32[656,256]{1,0:T(8,128)S(1)}, f32[656,256]{1,0:T(8,128)S(1)}, u32[]{:S(2)}, u32[]{:S(2)}) collective-permute-start(f32[656,256]{1,0:T(8,128)S(1)} %far.1), channel_id=1, source_target_pairs={{1,2},{2,1},{3,4},{4,3},{5,6},{6,5},{7,8},{8,7},{9,10},{10,9},{11,... | collective-permute-start | bytes 2015240 | tf_op jit(solution)/shard_map/ppermute | solution.py:976
  10.9 13.6 %collective-permute-start.1 = (f32[656,256]{1,0:T(8,128)S(1)}, f32[656,256]{1,0:T(8,128)S(1)}, u32[]{:S(2)}, u32[]{:S(2)}) collective-permute-start(f32[656,256]{1,0:T(8,128)S(1)} %get-tuple-element.45), channel_id=1, source_target_pairs={{0,1},{1,0},{2,3},{3,2},{4,5},{5,4},{6,7},{7,6},{8,9},{9,8},{10,11... | collective-permute-start | bytes 2015240 | tf_op jit(solution)/shard_map/ppermute | solution.py:992
  30.5 5.6 %collective-permute-start.2 = (f32[40,256]{1,0:T(8,128)S(1)}, f32[40,256]{1,0:T(8,128)S(1)}, u32[]{:S(2)}, u32[]{:S(2)}) collective-permute-start(f32[40,256]{1,0:T(8,128)S(1)} %get-tuple-element.60), channel_id=1, source_target_pairs={{0,1},{1,0},{2,3},{3,2},{4,5},{5,4},{6,7},{7,6},{8,9},{9,8},{10,11... | collective-permute-start | bytes 122888 | tf_op jit(solution)/shard_map/ppermute | solution.py:1002
  31.4 5.3 %collective-permute-start.3 = (f32[40,256]{1,0:T(8,128)S(1)}, f32[40,256]{1,0:T(8,128)S(1)}, u32[]{:S(2)}, u32[]{:S(2)}) collective-permute-start(f32[40,256]{1,0:T(8,128)S(1)} %get-tuple-element.61), channel_id=1, source_target_pairs={{1,2},{2,1},{3,4},{4,3},{5,6},{6,5},{7,8},{8,7},{9,10},{10,9},{11,... | collective-permute-start | bytes 122888 | tf_op jit(solution)/shard_map/ppermute | solution.py:1001

commit v4 on v3

--- a/solution.py
+++ b/solution.py
@@ -202,21 +202,41 @@
 def far_kernel(field, sea_in, wind_in, out, cells, sea, wind, sems):
     even = lax.rem(lax.axis_index("geo"), 2) == 0
     each = GROUPS // 3
-    lane = pl.multiple_of(jnp.where(even, 0, 2 * W), 2 * W)
     small = [
-        pltpu.make_async_copy(sea_in, sea, sems.at[3]),
-        pltpu.make_async_copy(wind_in, wind, sems.at[4]),
+        pltpu.make_async_copy(sea_in, sea, sems.at[6]),
+        pltpu.make_async_copy(wind_in, wind, sems.at[7]),
     ]
-    copies = []
-    for c in range(3):
-        here = pl.ds(c * each, each)
-        copies.append(pltpu.make_async_copy(field.at[here, :, pl.ds(lane, 2 * W)], cells.at[here], sems.at[c]))
-    for copy in small + copies:
+
+    def bring(first, lane):
+        copies = []
+        for c in range(3):
+            for run in range(2):
+                here, rows = pl.ds(c * each, each), pl.ds((first + 4 * run) * SUB, 3 * SUB)
+                copies.append(
+                    pltpu.make_async_copy(
+                        field.at[here, rows, pl.ds(lane, 2 * W)], cells.at[here, rows], sems.at[2 * c + run]
+                    )
+                )
+        return copies
+
+    @pl.when(even)
+    def _():
+        for copy in bring(2, 0):
+            copy.start()
+
+    @pl.when(jnp.logical_not(even))
+    def _():
+        for copy in bring(0, 2 * W):
+            copy.start()
+
+    copies = bring(0, 0)
+    for copy in small:
         copy.start()
     for copy in small:
         copy.wait()
     for c in range(3):
-        copies[c].wait()
+        copies[2 * c].wait()
+        copies[2 * c + 1].wait()
 
         @pl.when(even)
         def _():
@@ -247,10 +267,31 @@
             pltpu.VMEM((GROUPS, GROUP, 2 * W), F32),
             pltpu.VMEM((1, ROWS * W), jnp.int32),
             pltpu.VMEM((2, ROWS * W), F32),
-            pltpu.SemaphoreType.DMA((5,)),
+            pltpu.SemaphoreType.DMA((8,)),
         ],
         away=(0, 1, 2),
     )[0]
+
+
+def near_kernel(cells, sea_in, wind, after, out):
+    even = lax.rem(lax.axis_index("geo"), 2) == 0
+
+    def rows(base, north):
+        mask = [full(sea_in[:, lanes(base + r)].astype(F32)) for r in range(2)]
+        pack_all(cells, base * W, mask, out, 0, GROUPS // 2, north)
+        pack_small(out, wind, sea_in, base)
+
+    @pl.when(even)
+    def _():
+        rows(2, True)
+
+    @pl.when(jnp.logical_not(even))
+    def _():
+        rows(0, False)
+
+
+def near_rows(field, sea, wind, after):
+    return call(near_kernel, "near", [(field, True), (sea, False), (wind, False), (after, True)], [(HALO, False)])[0]
 
 
 def unpack_north(halo, pair, half, row, sub):
@@ -355,18 +396,10 @@
 
 
 def local_kernel(
-    field, sea_in, wind, courant, rate_in, damp_in, steep_in, table, owner, point, value, weight,
-    flow, rate, damp, steep, centre, ahead, back, across, own, slots, near_out,
-    cells, flat, sems, *, ranks,
+    cells, sea_in, courant, rate_in, damp_in, steep_in, table, owner, point, value, weight,
+    flow, rate, damp, steep, centre, ahead, back, across, own, slots, flat, *, ranks,
 ):
     sub = sublane()
-    each = GROUPS // CHUNKS
-    copies = [
-        pltpu.make_async_copy(field.at[pl.ds(c * each, each)], cells.at[pl.ds(c * each, each)], sems.at[c])
-        for c in range(CHUNKS)
-    ]
-    for copy in copies:
-        copy.start()
     spread(((rate_in, LOG2E), (damp_in, LOG2E), (steep_in, 1.0)), (rate, damp, steep), flat)
     slots[...] = sort(owner, point, value, weight, ranks)
     sea = [full(sea_in[:, lanes(r)].astype(F32)) for r in range(ROWS)]
@@ -398,10 +431,7 @@
                 sums[ROWS + 1] = sums[ROWS + 1] + pick(tile, sub, None, gone * cell[0])
         return tuple(sums)
 
-    sums = (zero,) * (ROWS + 2)
-    for c in range(CHUNKS):
-        copies[c].wait()
-        sums = loop(c * each, (c + 1) * each, 3, step, sums)
+    sums = loop(0, GROUPS, 3, step, (zero,) * (ROWS + 2))
     sums = [total(value) for value in sums]
     own[...] = jnp.zeros_like(own)
     for r in range(ROWS):
@@ -425,42 +455,22 @@
     def _():
         hand(0, me - 1)
 
-    even = lax.rem(me, 2) == 0
-
-    @pl.when(even)
-    def _():
-        pack_all(cells, 2 * W, sea[2:4], near_out, 0, GROUPS // 2, True)
-        pack_small(near_out, wind, sea_in, 2)
-
-    @pl.when(jnp.logical_not(even))
-    def _():
-        pack_all(cells, 0, sea[0:2], near_out, 0, GROUPS // 2, False)
-        pack_small(near_out, wind, sea_in, 0)
-
-
-def local(field, sea, wind, courant, rate, damp, steep, table, owner, point, value, weight, ranks):
+
+def local(field, sea, courant, rate, damp, steep, table, owner, point, value, weight, ranks):
     rows = owner.shape[1]
     _, block = layout(rows, ranks)
 
     def kernel(*refs):
         local_kernel(*refs, ranks=ranks)
 
-    args = (
-        pltpu.with_memory_space_constraint(field, pltpu.HBM), sea, wind, courant, rate, damp, steep, table,
-        owner, point, value, weight,
-    )
+    args = (sea, courant, rate, damp, steep, table, owner, point, value, weight)
     return call(
         kernel,
         "local",
-        [(arg, False) for arg in args],
-        [(CELLS, True)] + [(BINS, True)] * 7 + [((SUB, ROWS * W), True), ((ranks * block, W), False), (HALO, False)],
-        [
-            pltpu.VMEM(CELLS, F32),
-            pltpu.VMEM((16, 11 * W), F32),
-            pltpu.SemaphoreType.DMA((CHUNKS,)),
-        ],
-        smem=(3,),
-        away=(0,),
+        [(field, True)] + [(arg, False) for arg in args],
+        [(CELLS, True)] + [(BINS, True)] * 7 + [((SUB, ROWS * W), True), ((ranks * block, W), False)],
+        [pltpu.VMEM((16, 11 * W), F32)],
+        smem=(2,),
     )
 
 
@@ -566,52 +576,18 @@
 
 
 def late_kernel(
-    next_in, factor, moved, from_far, from_near, wanted, gain, state_in, rate, damp, steep, centre, ahead, back, across,
-    next_, next_south, next_north, source, edges, state, send_a, send_b,
-    fixed, growth, lam, halo_south, halo_north, sems,
+    next_in, factor, moved_in, from_far, from_near, wanted, gain, state_in, rate, damp, steep, centre, ahead, back, across,
+    next_, next_south, next_north, source, edges, state, send_a, send_b, moved, growth, lam, partial,
 ):
     sub = sublane()
     zero = jnp.zeros((SUB, W), F32)
     even = lax.rem(lax.axis_index("geo"), 2) == 0
-    each = HALF // 3
-    parts = [pl.ds(HALF, SUB)] + [pl.ds(c * each, each) for c in range(3)]
-
-    def bring(first, second):
-        copies = []
-        for c, here in enumerate(parts):
-            copies.append(pltpu.make_async_copy(first.at[here], halo_south.at[here], sems.at[2 * c]))
-            copies.append(pltpu.make_async_copy(second.at[here], halo_north.at[here], sems.at[2 * c + 1]))
-        return copies
-
-    @pl.when(even)
-    def _():
-        for copy in bring(from_far, from_near):
-            copy.start()
-
-    @pl.when(jnp.logical_not(even))
-    def _():
-        for copy in bring(from_near, from_far):
-            copy.start()
-
-    copies = bring(from_far, from_near)
-    copies[0].wait()
-    copies[1].wait()
     state[...] = state_in[...]
-    for halo, rows in ((halo_south, (-2, -1)), (halo_north, (4, 5))):
-        here = pl.ds((rows[0] + 2) * W, 2 * W)
-        for place, name in enumerate((WIND0, WIND1, SEA)):
-            state[name : name + 1, here] = halo[HALF + place : HALF + place + 1, :]
-    for r in (-1, 4):
-        known = state[SEA : SEA + 1, column(r)] > 0.5
-        state[STEEP0 : STEEP0 + 1, column(r)] = jnp.where(known, state[STEEP0 : STEEP0 + 1, column(r)], LAND)
 
     def held(place, r):
         return full(state[place : place + 1, column(r)])
 
-    steep0 = {r: held(STEEP0, r) for r in (-1, 4)}
-    wind0 = {r: held(WIND0, r) for r in (-1, 4)}
-
-    def first(pair, sums):
+    def first(pair, sums, halo_south, halo_north, steep0, wind0):
         sums = list(sums)
         for half in range(2):
             group = 2 * pair + half
@@ -646,19 +622,37 @@
                     changes[second] = plus(over * extra, changes.get(second))
                 for r, change in changes.items():
                     sums[r] = sums[r] + heavy * change
-                    fixed[group, rows, lanes(r)] = moved[group, rows, lanes(r)] + change
-                for r in range(ROWS):
-                    if r not in changes:
-                        fixed[group, rows, lanes(r)] = moved[group, rows, lanes(r)]
+                    moved[group, rows, lanes(r)] = moved_in[group, rows, lanes(r)] + change
         return tuple(sums)
 
-    sums = (zero,) * ROWS
-    for c in range(3):
-        copies[2 * c + 2].wait()
-        copies[2 * c + 3].wait()
-        sums = loop(3 * c, 3 * c + 3, 3, first, sums)
+    def halo_terms(halo_south, halo_north):
+        for halo, rows in ((halo_south, (-2, -1)), (halo_north, (4, 5))):
+            here = pl.ds((rows[0] + 2) * W, 2 * W)
+            for place, name in enumerate((WIND0, WIND1, SEA)):
+                state[name : name + 1, here] = halo[HALF + place : HALF + place + 1, :]
+        for r in (-1, 4):
+            known = state[SEA : SEA + 1, column(r)] > 0.5
+            state[STEEP0 : STEEP0 + 1, column(r)] = jnp.where(known, state[STEEP0 : STEEP0 + 1, column(r)], LAND)
+        steep0 = {r: held(STEEP0, r) for r in (-1, 4)}
+        wind0 = {r: held(WIND0, r) for r in (-1, 4)}
+
+        def step(pair, sums):
+            return first(pair, sums, halo_south, halo_north, steep0, wind0)
+
+        sums = loop(0, GROUPS // 2, 3, step, (zero,) * ROWS)
+        for r in range(ROWS):
+            partial[r] = sums[r]
+
+    @pl.when(even)
+    def _():
+        halo_terms(from_far, from_near)
+
+    @pl.when(jnp.logical_not(even))
+    def _():
+        halo_terms(from_near, from_far)
+
     for r in range(ROWS):
-        value = state[STEEP1 : STEEP1 + 1, column(r)] + total(sums[r])
+        value = state[STEEP1 : STEEP1 + 1, column(r)] + total(partial[r])
         state[STEEP1 : STEEP1 + 1, column(r)] = jnp.where(state[SEA : SEA + 1, column(r)] > 0.5, value, LAND)
     steep1 = [held(STEEP1, r) for r in range(ROWS)]
     wind1 = [held(WIND1, r) for r in range(ROWS)]
@@ -675,7 +669,7 @@
             for r in range(ROWS):
                 value = jnp.exp2(grow * wind1[r] - fade * steep1[r])
                 growth[group, rows, lanes(r)] = value
-                value = value * fixed[group, rows, lanes(r)]
+                value = value * moved[group, rows, lanes(r)]
                 for parts, term in ((means, value), (ups, grow * value), (downs, fade * value)):
                     if tile == 4:
                         parts[r][0] = plus(jnp.where(sub < 4, term, 0.0), parts[r][0])
@@ -746,24 +740,20 @@
 
 
 def late(next_, factor, moved, from_far, from_near, wanted, gain, state, coefficients):
-    inputs = [(next_, True), (factor, True), (moved, True), (from_far, False), (from_near, False)]
+    inputs = [(next_, True), (factor, True), (moved, True), (from_far, True), (from_near, True)]
     inputs += [(value, True) for value in (wanted, gain, state) + coefficients]
     return call(
         late_kernel,
         "late",
         inputs,
         [(CELLS, True)] + [(EDGE, True)] * 2 + [(CELLS, True), (EDGES, True), (STATE, True)]
-        + [((NF + 4, 2 * W), False)] * 2,
+        + [((NF + 4, 2 * W), False)] * 2 + [(CELLS, True)],
         [
             pltpu.VMEM(CELLS, F32),
-            pltpu.VMEM(CELLS, F32),
             pltpu.VMEM((GROUPS, SUB, ROWS * W), F32),
-            pltpu.VMEM(HALO, F32),
-            pltpu.VMEM(HALO, F32),
-            pltpu.SemaphoreType.DMA((8,)),
+            pltpu.VMEM((ROWS, SUB, W), F32),
         ],
-        away=(3, 4),
-        aliases={0: 0},
+        aliases={0: 0, 2: 8},
     )
 
 
@@ -974,10 +964,9 @@
     field = initial_spectrum.reshape(CELLS)
     sea = sea_mask.reshape(1, ROWS * W)
     from_far = lax.ppermute(far_rows(field, sea, wind_forcing), "geo", far)
-    flow, rate, damp, steep, centre, ahead, back, across, own, slots, rows = local(
+    flow, rate, damp, steep, centre, ahead, back, across, own, slots = local(
         field,
         sea,
-        wind_forcing,
         courant,
         input_rate.reshape(1, NB),
         damping.reshape(1, NB),
@@ -989,12 +978,12 @@
         obs_weight.reshape(1, held),
         count,
     )
-    from_near = lax.ppermute(rows, "geo", near)
+    from_near = lax.ppermute(near_rows(field, sea, wind_forcing, own), "geo", near)
     arrived = lax.all_to_all(slots, "geo", split_axis=0, concat_axis=0, tiled=True)
     next_, factor, moved, wanted, gain, state = early(
         arrived, flow, own, wind_forcing, sea, rate, damp, steep, centre, ahead, across, count, held
     )
-    next_, next_south, next_north, source, edges, state, send_a, send_b = late(
+    next_, next_south, next_north, source, edges, state, send_a, send_b, _ = late(
         next_, factor, moved, from_far, from_near, wanted, gain, state,
         (rate, damp, steep, centre, ahead, back, across),
     )

time: 41.3 us -> 39.8 us (0.964)
  Pallas kernels: 18.4 us -> 16.1 us
  blocking collectives: 11.4 us -> 12.3 us
    pallas_call x6 -> x7, Pallas kernels: 18.4 us -> 16.1 us  [call(): pl.pallas_call(kernel, in_specs=specs, out_specs=[whole(pl.ANY if place i...]
    all_to_all x1, blocking collectives: 11.4 us -> 12.3 us  [body(): lax.all_to_all(slots, 'geo', split_axis=0, concat_axis=0, tiled=True)]
    ppermute x1, starting transfers between devices: 0.84 us -> 0.07 us  [body(): back_a = lax.ppermute(send_a, 'geo', near)]
    ppermute x1, starting transfers between devices: 3.67 us -> 4.44 us  [body(): back_b = lax.ppermute(send_b, 'geo', far)]
  transfers between devices with their start and end apart: 4 -> 4, of which waited for: 1 -> 1; matrix products, arithmetic and copies ran while one was open for 0% -> 0% of each run, Pallas kernels for 18% -> 16%
where the time goes in v4:
time: 39.8 us; the launch traced here: 39 us
  Pallas kernels  16.1 us (40%)
  blocking collectives  12.3 us (31%)
  starting transfers between devices  9.06 us (23%)
  between operations  0.95 us (2%)
  waiting for transfers between devices  0.55 us (1%)
    pallas_call x7, Pallas kernels, call(): pl.pallas_call(kernel, in_specs=specs, out_specs=[whole(pl.ANY if place i...  16.1 us
    all_to_all x1, blocking collectives, body(): lax.all_to_all(slots, 'geo', split_axis=0, concat_axis=0, tiled=True)  12.3 us
    ppermute x1, starting transfers between devices, body(): from_far = lax.ppermute(far_rows(field, sea, wind_forcing), 'geo', far)  4.48 us
    ppermute x1, starting transfers between devices, body(): back_b = lax.ppermute(send_b, 'geo', far)  4.44 us
  transfers between devices with their start and end apart: 4, of which 1 were waited for; matrix products, arithmetic and copies ran while one was open for 0% of the time, Pallas kernels for 16%

profile of v4, /device:TPU:1, one launch (start us, length us, event | category | flops | bytes accessed | tf_op | source)
XLA Modules:
  0.0 39.0 jit_solution(2562921067449234648)
XLA Ops:
  0.6 0.0 copy-start.1
  0.6 0.0 copy-start.3
  0.7 0.0 copy-start
  0.7 0.0 copy-start.9
  0.7 0.0 copy-start.10
  0.7 0.0 copy-start.11
  0.7 0.0 copy-start.8
  0.7 0.0 copy-start.4
  0.7 0.0 copy-start.7
  0.7 0.0 copy-start.6
  0.7 0.0 copy-start.5
  0.7 0.0 copy-start.2
  0.8 1.6 %far.1 = f32[656,256]{1,0:T(8,128)S(1)} custom-call(f32[18,72,512]{2,1,0:T(8,128)} %bitcast.9, s32[1,512]{1,0:T(1,128)} %bitcast.14, f32[2,512]{1,0:T(2,128)} %wind.1), custom_call_target="tpu_custom_call" | custom-call | tf_op jit(solution)/shard_map/far/pallas_call | solution.py:148
  2.3 4.5 %collective-permute-start = (f32[656,256]{1,0:T(8,128)S(1)}, f32[656,256]{1,0:T(8,128)S(1)}, u32[]{:S(2)}, u32[]{:S(2)}) collective-permute-start(f32[656,256]{1,0:T(8,128)S(1)} %far.1), channel_id=1, source_target_pairs={{1,2},{2,1},{3,4},{4,3},{5,6},{6,5},{7,8},{8,7},{9,10},{10,9},{11,... | collective-permute-start | bytes 2015240 | tf_op jit(solution)/shard_map/ppermute | solution.py:966
  6.8 0.0 copy-done.9
  6.8 0.0 copy-done.10
  6.9 0.0 copy-done.11
  6.9 0.0 copy-done.1
  6.9 0.0 copy-done.3
  6.9 0.0 copy-done
  6.9 0.0 copy-done.8
  6.9 0.0 copy-done.4
  6.9 0.0 copy-done.7
  7.0 0.0 copy-done.6
  7.0 0.0 copy-done.5
  7.0 2.9 %local.1 = (f32[18,72,512]{2,1,0:T(8,128)S(1)}, f32[1296,128]{1,0:T(8,128)S(1)}, f32[1296,128]{1,0:T(8,128)S(1)}, f32[1296,128]{1,0:T(8,128)S(1)}, f32[1296,128]...) custom-call(f32[18,72,512]{2,1,0:T(8,128)S(1)} %bitcast.10, ...), custom_call_target="tpu_custom_call" | custom-call | tf_op jit(solution)/shard_map/local/pallas_call | solution.py:148
  9.9 0.0 copy-done.2
  9.9 0.2 near.1
  10.1 0.1 collective-permute-start.1
  10.1 12.3 %all_to_all.11 = f32[16,8,128]{2,1,0:T(8,128)S(1)} all-to-all(f32[16,8,128]{2,1,0:T(8,128)S(1)} %bitcast.13), channel_id=1, replica_groups=mesh['groups'=2,'geo'=16] {'geo'}, dimensions={0} | all-to-all | bytes 131072 | tf_op jit(solution)/shard_map/all_to_all | solution.py:982
  22.4 2.1 %early.1 = (f32[18,72,512]{2,1,0:T(8,128)S(1)}, f32[18,72,512]{2,1,0:T(8,128)S(1)}, f32[18,72,512]{2,1,0:T(8,128)S(1)}, f32[18,8,512]{2,1,0:T(8,128)S(1)}, f32[8,512]{1,0:T(8,128)S(1)}, /*index=5*/f32[16,1024]{1,0:T(8,128)S(1)}) custom-call(f32[128,128]{1,0:T(8,128)S(1)} %bitcast.12, f32[18,72,512]{2,1,0:T(8,128)S(1)} %get-tuple-element.33.refs_1_, ...), custom_call_target="tpu_custom_call" | custom-call | tf_op jit(solution)/shard_map/early/pallas_call | solution.py:148
  24.5 0.0 collective-permute-done.from_far
  24.5 0.0 collective-permute-done.1.from_near
  24.5 4.5 %late.1 = (f32[18,72,512]{2,1,0:T(8,128)S(1)}, f32[18,72,128]{2,1,0:T(8,128)S(1)}, f32[18,72,128]{2,1,0:T(8,128)S(1)}, f32[18,72,512]{2,1,0:T(8,128)S(1)}, f32[1...) custom-call(f32[18,72,512]{2,1,0:T(8,128)S(1)} %get-tuple-element.41, ...), custom_call_target="tpu_custom_call", output_to_operand_aliasing={{0}: (0, {}), {8}: (2, {})} | custom-call | tf_op jit(solution)/shard_map/late/pallas_call | solution.py:148
  29.0 0.1 collective-permute-start.2
  29.1 4.4 %collective-permute-start.3 = (f32[40,256]{1,0:T(8,128)S(1)}, f32[40,256]{1,0:T(8,128)S(1)}, u32[]{:S(2)}, u32[]{:S(2)}) collective-permute-start(f32[40,256]{1,0:T(8,128)S(1)} %get-tuple-element.59), channel_id=1, source_target_pairs={{1,2},{2,1},{3,4},{4,3},{5,6},{6,5},{7,8},{8,7},{9,10},{10,9},{11,... | collective-permute-start | bytes 122888 | tf_op jit(solution)/shard_map/ppermute | solution.py:990
  33.6 1.1 %inner.1 = (f32[18,72,256]{2,1,0:T(8,128)S(1)}, f32[18,72,128]{2,1,0:T(8,128)S(1)}, f32[18,72,128]{2,1,0:T(8,128)S(1)}, f32[16,1024]{1,0:T(8,128)S(1)}) custom-call(f32[18,72,512]{2,1,0:T(8,128)S(1)} %get-tuple-element.48.next_, f32[18,72,128]{2,1,0:T(8,128)S(1)} %get-tuple-element.49.next_south, f32[18,72,128]{2,1,0:T(8,128)S(1)} %get-tuple-element.50.next_north, ...), custom_call_target="tpu_custom_call" | custom-call | flops 4194304 | bytes 4194304 | tf_op jit(solution)/shard_map/inner/pallas_call | solution.py:148
  34.7 0.0 collective-permute-done.2.back_a
  34.7 0.5 %collective-permute-done.3.back_b = f32[40,256]{1,0:T(8,128)S(1)} collective-permute-done((f32[40,256]{1,0:T(8,128)S(1)}, f32[40,256]{1,0:T(8,128)S(1)}, u32[]{:S(2)}, u32[]{:S(2)}) %collective-permute-start.3) | collective-permute-done | bytes 40992 | tf_op jit(solution)/shard_map/ppermute | solution.py:990
  35.2 3.8 %last.1 = (f32[18,72,512]{2,1,0:T(8,128)}, f32[2,512]{1,0:T(2,128)}) custom-call(f32[18,72,512]{2,1,0:T(8,128)S(1)} %get-tuple-element.48.next_, f32[18,72,512]{2,1,0:T(8,128)S(1)} %get-tuple-element.42.factor, f32[18,72,128]{2,1,0:T(8,128)S(1)} %get-tuple-element.53.factor_south, f32[18,72,128]{2,1,0:T(8,128)S(1)} %get-tuple-element.54.factor_north, ...), custom_call_target="tpu_custom_call" | custom-call | tf_op jit(solution)/shard_map/last/pallas_call | solution.py:148
  (3 shorter events, 0.0 us)
Async XLA Ops:
  0.6 6.3 %copy-start.1 = (f32[4,72,128]{2,1,0:T(8,128)S(1)}, f32[4,72,128]{2,1,0:T(8,128)}, u32[]{:S(2)}) copy-start(f32[4,72,128]{2,1,0:T(8,128)} %constant.2.clone.refs_6_) | copy-start | bytes 442372
  0.6 6.3 %copy-start.3 = (s32[512]{0:T(512)S(1)}, s32[512]{0:T(512)}, u32[]{:S(2)}) copy-start(s32[512]{0:T(512)} %param.14) | copy-start | bytes 6148
  0.7 6.3 %copy-start = (f32[1296,512]{1,0:T(8,128)S(1)}, f32[1296,512]{1,0:T(8,128)}, u32[]{:S(2)}) copy-start(f32[1296,512]{1,0:T(8,128)} %param.12) | copy-start | bytes 7962628
  0.7 6.2 %copy-start.9 = (f32[1296]{0:T(1024)S(1)}, f32[1296]{0:T(1024)}, u32[]{:S(2)}) copy-start(f32[1296]{0:T(1024)} %param.16) | copy-start | bytes 15556
  0.7 6.2 %copy-start.10 = (f32[1296]{0:T(1024)S(1)}, f32[1296]{0:T(1024)}, u32[]{:S(2)}) copy-start(f32[1296]{0:T(1024)} %param.17) | copy-start | bytes 15556
  0.7 6.2 %copy-start.11 = (f32[1296]{0:T(1024)S(1)}, f32[1296]{0:T(1024)}, u32[]{:S(2)}) copy-start(f32[1296]{0:T(1024)} %param.18) | copy-start | bytes 15556
  0.7 6.2 %copy-start.8 = (f32[128]{0:T(128)S(1)}, f32[128]{0:T(128)}, u32[]{:S(2)}) copy-start(f32[128]{0:T(128)} %param.22) | copy-start | bytes 1540
  0.7 6.2 %copy-start.4 = (f32[128,36]{0,1:T(8,128)S(1)}, f32[128,36]{0,1:T(8,128)}, u32[]{:S(2)}) copy-start(f32[128,36]{0,1:T(8,128)} %param.21) | copy-start | bytes 55300
  0.7 6.2 %copy-start.7 = (s32[128]{0:T(128)S(1)}, s32[128]{0:T(128)}, u32[]{:S(2)}) copy-start(s32[128]{0:T(128)} %param.20) | copy-start | bytes 1540
  0.7 6.2 %copy-start.6 = (s32[128,1]{0,1:T(1,128)S(1)}, s32[128,1]{0,1:T(1,128)}, u32[]{:S(2)}) copy-start(s32[128,1]{0,1:T(1,128)} %param.19) | copy-start | bytes 1540
  0.7 6.2 %copy-start.5 = (f32[36]{0:T(128)S(1)}, f32[36]{0:T(128)}, u32[]{:S(2)}) copy-start(f32[36]{0:T(128)} %refs_2_.1) | copy-start | bytes 436
  0.7 9.1 %copy-start.2 = (f32[2,512]{1,0:T(2,128)S(1)}, f32[2,512]{1,0:T(2,128)}, u32[]{:S(2)}) copy-start(f32[2,512]{1,0:T(2,128)} %wind.1) | copy-start | bytes 12292
  2.3 22.1 %collective-permute-start = (f32[656,256]{1,0:T(8,128)S(1)}, f32[656,256]{1,0:T(8,128)S(1)}, u32[]{:S(2)}, u32[]{:S(2)}) collective-permute-start(f32[656,256]{1,0:T(8,128)S(1)} %far.1), channel_id=1, source_target_pairs={{1,2},{2,1},{3,4},{4,3},{5,6},{6,5},{7,8},{8,7},{9,10},{10,9},{11,... | collective-permute-start | bytes 2015240 | tf_op jit(solution)/shard_map/ppermute | solution.py:966
  10.1 14.4 %collective-permute-start.1 = (f32[656,256]{1,0:T(8,128)S(1)}, f32[656,256]{1,0:T(8,128)S(1)}, u32[]{:S(2)}, u32[]{:S(2)}) collective-permute-start(f32[656,256]{1,0:T(8,128)S(1)} %near.1), channel_id=1, source_target_pairs={{0,1},{1,0},{2,3},{3,2},{4,5},{5,4},{6,7},{7,6},{8,9},{9,8},{10,11... | collective-permute-start | bytes 2015240 | tf_op jit(solution)/shard_map/ppermute | solution.py:981
  29.0 5.6 %collective-permute-start.2 = (f32[40,256]{1,0:T(8,128)S(1)}, f32[40,256]{1,0:T(8,128)S(1)}, u32[]{:S(2)}, u32[]{:S(2)}) collective-permute-start(f32[40,256]{1,0:T(8,128)S(1)} %get-tuple-element.58), channel_id=1, source_target_pairs={{0,1},{1,0},{2,3},{3,2},{4,5},{5,4},{6,7},{7,6},{8,9},{9,8},{10,11... | collective-permute-start | bytes 122888 | tf_op jit(solution)/shard_map/ppermute | solution.py:991
  29.1 6.1 %collective-permute-start.3 = (f32[40,256]{1,0:T(8,128)S(1)}, f32[40,256]{1,0:T(8,128)S(1)}, u32[]{:S(2)}, u32[]{:S(2)}) collective-permute-start(f32[40,256]{1,0:T(8,128)S(1)} %get-tuple-element.59), channel_id=1, source_target_pairs={{1,2},{2,1},{3,4},{4,3},{5,6},{6,5},{7,8},{8,7},{9,10},{10,9},{11,... | collective-permute-start | bytes 122888 | tf_op jit(solution)/shard_map/ppermute | solution.py:990

commit v5 on v4

--- a/solution.py
+++ b/solution.py
@@ -20,7 +20,7 @@
 CHUNKS = 6
 F32 = jnp.float32
 BF16 = jnp.bfloat16
-LIMIT = 14 * 1024 * 1024
+LIMIT = 7 * 1024 * 1024
 LOG2E = math.log2(math.e)
 LN2 = math.log(2.0)
 LAND = 1.0e5
@@ -290,8 +290,8 @@
         rows(0, False)
 
 
-def near_rows(field, sea, wind, after):
-    return call(near_kernel, "near", [(field, True), (sea, False), (wind, False), (after, True)], [(HALO, False)])[0]
+def near_rows(field, sea, wind, own):
+    return call(near_kernel, "near", [(field, True), (sea, False), (wind, False), (own, True)], [(HALO, False)])[0]
 
 
 def unpack_north(halo, pair, half, row, sub):
@@ -396,12 +396,11 @@
 
 
 def local_kernel(
-    cells, sea_in, courant, rate_in, damp_in, steep_in, table, owner, point, value, weight,
-    flow, rate, damp, steep, centre, ahead, back, across, own, slots, flat, *, ranks,
+    cells, sea_in, courant, rate_in, damp_in, steep_in, table,
+    flow, rate, damp, steep, centre, ahead, back, across, own, flat,
 ):
     sub = sublane()
     spread(((rate_in, LOG2E), (damp_in, LOG2E), (steep_in, 1.0)), (rate, damp, steep), flat)
-    slots[...] = sort(owner, point, value, weight, ranks)
     sea = [full(sea_in[:, lanes(r)].astype(F32)) for r in range(ROWS)]
     zero = jnp.zeros((SUB, W), F32)
 
@@ -439,42 +438,19 @@
     own[1:2, lanes(ROWS - 1)] = sums[ROWS]
     own[1:2, lanes(0)] = sums[ROWS + 1]
 
-    _, block = layout(owner.shape[1], ranks)
-    me = lax.axis_index("geo")
-
-    def hand(row, dest):
-        last = pl.ds(pl.multiple_of(dest * block + block - SUB, SUB), SUB)
-        values = jnp.where(sub == SUB - 2, own[0:1, lanes(row)], slots[last, :])
-        slots[last, :] = jnp.where(sub == SUB - 1, own[1:2, lanes(row)], values)
-
-    @pl.when(me < ranks - 1)
-    def _():
-        hand(ROWS - 1, me + 1)
-
-    @pl.when(me > 0)
-    def _():
-        hand(0, me - 1)
-
-
-def local(field, sea, courant, rate, damp, steep, table, owner, point, value, weight, ranks):
-    rows = owner.shape[1]
-    _, block = layout(rows, ranks)
-
-    def kernel(*refs):
-        local_kernel(*refs, ranks=ranks)
-
-    args = (sea, courant, rate, damp, steep, table, owner, point, value, weight)
+
+def local(field, sea, courant, rate, damp, steep, table):
     return call(
-        kernel,
+        local_kernel,
         "local",
-        [(field, True)] + [(arg, False) for arg in args],
-        [(CELLS, True)] + [(BINS, True)] * 7 + [((SUB, ROWS * W), True), ((ranks * block, W), False)],
+        [(field, True)] + [(arg, False) for arg in (sea, courant, rate, damp, steep, table)],
+        [(CELLS, True)] + [(BINS, True)] * 7 + [((SUB, ROWS * W), True)],
         [pltpu.VMEM((16, 11 * W), F32)],
         smem=(2,),
     )
 
 
-def place(arrived, ranks, rows, wanted, gain):
+def settle(arrived, wanted, gain, ranks, rows):
     lines, block = layout(rows, ranks)
     size = ranks * block
     shape = (size, W)
@@ -499,35 +475,36 @@
     gain[...] = jnp.broadcast_to(sums[NF : NF + 1, :] * (1.0 / (ND * ND)), gain.shape)
 
 
-def early_kernel(
-    arrived, flow, own, wind, sea_in, rate, damp, steep, centre, ahead, across, next_, factor, moved, wanted, gain, state,
-    *, ranks, rows,
+def middle_kernel(
+    flow, own, wind, sea_in, rate, damp, steep, centre, ahead, across, owner, point, value, weight, after,
+    next_, factor, moved, state, slots, *, ranks,
 ):
     sub = sublane()
-    place(arrived, ranks, rows, wanted, gain)
-    lines, block = layout(rows, ranks)
+    slots[...] = sort(owner, point, value, weight, ranks)
+    _, block = layout(owner.shape[1], ranks)
     me = lax.axis_index("geo")
 
-    def aux(source, there):
-        source = jnp.clip(source, 0, ranks - 1)
-        last = pl.ds(pl.multiple_of(source * block + block - SUB, SUB), SUB)
-        return jnp.where(there, arrived[last, :], 0.0)
-
-    south, north = aux(me - 1, me > 0), aux(me + 1, me < ranks - 1)
+    def hand(row, dest):
+        last = pl.ds(pl.multiple_of(dest * block + block - SUB, SUB), SUB)
+        values = jnp.where(sub == SUB - 2, own[0:1, lanes(row)], slots[last, :])
+        slots[last, :] = jnp.where(sub == SUB - 1, own[1:2, lanes(row)], values)
+
+    @pl.when(me < ranks - 1)
+    def _():
+        hand(ROWS - 1, me + 1)
+
+    @pl.when(me > 0)
+    def _():
+        hand(0, me - 1)
+
     state[...] = jnp.zeros_like(state)
     here = pl.ds(2 * W, ROWS * W)
     state[WIND0 : WIND0 + 1, here] = wind[0:1, :]
     state[WIND1 : WIND1 + 1, here] = wind[1:2, :]
     state[SEA : SEA + 1, here] = sea_in[...].astype(F32)
-    steeps = {r: own[0:1, lanes(r)] for r in range(ROWS)}
-    steeps[0] = steeps[0] + south[7:8, :]
-    steeps[3] = steeps[3] + north[7:8, :]
-    for r, value in steeps.items():
-        state[STEEP0 : STEEP0 + 1, column(r)] = jnp.where(state[SEA : SEA + 1, column(r)] > 0.5, value, LAND)
-    state[STEEP0 : STEEP0 + 1, column(-1)] = south[6:7, :] + own[1:2, lanes(0)]
-    state[STEEP0 : STEEP0 + 1, column(4)] = north[6:7, :] + own[1:2, lanes(3)]
-    steep0 = [full(state[STEEP0 : STEEP0 + 1, column(r)]) for r in range(ROWS)]
-    wind0 = [full(state[WIND0 : WIND0 + 1, column(r)]) for r in range(ROWS)]
+    state[STEEP0 : STEEP0 + 1, here] = jnp.where(state[SEA : SEA + 1, here] > 0.5, own[0:1, :], LAND)
+    steep0 = {r: full(state[STEEP0 : STEEP0 + 1, column(r)]) for r in (1, 2)}
+    wind0 = {r: full(state[WIND0 : WIND0 + 1, column(r)]) for r in (1, 2)}
 
     def step(group, sums):
         sums = list(sums)
@@ -535,15 +512,20 @@
             rows, spot = pl.ds(tile * SUB, SUB), bins(group, tile)
             grow, fade, heavy = rate[spot, :], damp[spot, :], steep[spot, :]
             middle, along, over = centre[spot, :], ahead[spot, :], across[spot, :]
-            cell = {}
-            for r in range(ROWS):
+            cell, new = {}, {}
+            for r in (1, 2):
                 gained = jnp.exp2(grow * wind0[r] - fade * steep0[r])
                 factor[group, rows, lanes(r)] = gained
                 cell[r] = flow[group, rows, lanes(r)] * gained
                 next_[group, rows, lanes(r)] = cell[r]
-            for r in range(ROWS):
-                value = middle * cell[r] + along * side(tile, sub, cell[r], False)
-                value = plus(value, times(over, pick(tile, sub, cell.get(r - 1), cell.get(r + 1))))
+                new[r] = middle * cell[r] + along * side(tile, sub, cell[r], False)
+            new[1] = plus(new[1], pick(tile, sub, None, over * cell[2]))
+            new[2] = plus(new[2], pick(tile, sub, over * cell[1], None))
+            if tile in SOUTH:
+                new[0] = pick(tile, sub, None, over * cell[1])
+            if tile in NORTH:
+                new[3] = pick(tile, sub, over * cell[2], None)
+            for r, value in new.items():
                 moved[group, rows, lanes(r)] = value
                 sums[r] = sums[r] + heavy * value
         return tuple(sums)
@@ -553,17 +535,21 @@
         state[STEEP1 : STEEP1 + 1, column(r)] = total(sums[r])
 
 
-def early(arrived, flow, own, wind, sea, rate, damp, steep, centre, ahead, across, ranks, rows):
+def middle(flow, own, wind, sea, coefficients, observed, after, ranks):
+    _, block = layout(observed[0].shape[1], ranks)
+
     def kernel(*refs):
-        early_kernel(*refs, ranks=ranks, rows=rows)
-
-    inputs = [(arrived, False), (flow, True), (own, True), (wind, False), (sea, False)]
-    inputs += [(value, True) for value in (rate, damp, steep, centre, ahead, across)]
+        middle_kernel(*refs, ranks=ranks)
+
+    inputs = [(flow, True), (own, True), (wind, False), (sea, False)]
+    inputs += [(value, True) for value in coefficients] + [(value, False) for value in observed + (after,)]
     return call(
         kernel,
-        "early",
+        "middle",
         inputs,
-        [(CELLS, True)] * 3 + [((GROUPS, SUB, ROWS * W), True), ((SUB, ROWS * W), True), (STATE, True)],
+        [(CELLS, True)] * 3 + [(STATE, True), ((ranks * block, W), False)],
+        away=(len(inputs) - 1,),
+        aliases={0: 0},
     )
 
 
@@ -576,13 +562,16 @@
 
 
 def late_kernel(
-    next_in, factor, moved_in, from_far, from_near, wanted, gain, state_in, rate, damp, steep, centre, ahead, back, across,
-    next_, next_south, next_north, source, edges, state, send_a, send_b, moved, growth, lam, partial,
+    next_in, factor_in, moved_in, from_far, from_near, arrived, own, state_in,
+    rate, damp, steep, centre, ahead, back, across,
+    next_, factor, moved, next_south, next_north, edges, state, send_b, lam, growth, partial, wanted, gain,
+    *, ranks, held_rows,
 ):
     sub = sublane()
     zero = jnp.zeros((SUB, W), F32)
     even = lax.rem(lax.axis_index("geo"), 2) == 0
     state[...] = state_in[...]
+    settle(arrived, wanted, gain, ranks, held_rows)
 
     def held(place, r):
         return full(state[place : place + 1, column(r)])
@@ -601,40 +590,54 @@
                 rows, spot = pl.ds(tile * SUB, SUB), bins(group, tile)
                 grow, fade, heavy = rate[spot, :], damp[spot, :], steep[spot, :]
                 middle, along, over = centre[spot, :], ahead[spot, :], across[spot, :]
-                beyond = {}
-                changes = {}
-                for near, far, mine, second, tiles, north in ((-1, -2, 0, 1, NORTH, True), (4, 5, 3, 2, SOUTH, False)):
-                    if tile not in tiles:
-                        continue
+                for near, far, mine, second, north in ((-1, -2, 0, 1, True), (4, 5, 3, 2, False)):
+                    inward = tile in (NORTH if north else SOUTH)
+                    held_back = tile in (SOUTH if north else NORTH)
 
                     def only(value):
                         return pick(tile, sub, value, None) if north else pick(tile, sub, None, value)
 
-                    cell = ghosts[near][tile]
-                    gained = jnp.exp2(grow * wind0[near] - fade * steep0[near])
-                    value = middle * cell + along * side(tile, sub, cell, False) + over * ghosts[far][tile]
-                    value = value * gained
-                    (next_south if north else next_north)[group, rows, :] = value
-                    extra = only(over * cell) * factor[group, rows, lanes(mine)]
-                    next_[group, rows, lanes(mine)] = next_in[group, rows, lanes(mine)] + extra
-                    change = middle * extra + along * side(tile, sub, extra, False) + only(over * value)
-                    changes[mine] = plus(change, changes.get(mine))
-                    changes[second] = plus(over * extra, changes.get(second))
-                for r, change in changes.items():
-                    sums[r] = sums[r] + heavy * change
-                    moved[group, rows, lanes(r)] = moved_in[group, rows, lanes(r)] + change
+                    here = next_in[group, rows, lanes(mine)]
+                    if inward:
+                        cell = ghosts[near][tile]
+                        gained = jnp.exp2(grow * wind0[near] - fade * steep0[near])
+                        value = middle * cell + along * side(tile, sub, cell, False) + over * ghosts[far][tile]
+                        value = value * gained
+                        (next_south if north else next_north)[group, rows, :] = value
+                        here = here + only(over * cell)
+                    gained = jnp.exp2(grow * wind0[mine] - fade * steep0[mine])
+                    factor[group, rows, lanes(mine)] = gained
+                    here = here * gained
+                    next_[group, rows, lanes(mine)] = here
+                    change = middle * here + along * side(tile, sub, here, False)
+                    if inward:
+                        change = change + only(over * value)
+                    sums[mine] = sums[mine] + heavy * change
+                    if held_back:
+                        change = change + moved_in[group, rows, lanes(mine)]
+                    moved[group, rows, lanes(mine)] = change
+                    if inward:
+                        change = only(over * here)
+                        sums[second] = sums[second] + heavy * change
+                        moved[group, rows, lanes(second)] = moved_in[group, rows, lanes(second)] + change
         return tuple(sums)
 
-    def halo_terms(halo_south, halo_north):
+    def halo_terms(halo_south, halo_north, south, north):
         for halo, rows in ((halo_south, (-2, -1)), (halo_north, (4, 5))):
             here = pl.ds((rows[0] + 2) * W, 2 * W)
             for place, name in enumerate((WIND0, WIND1, SEA)):
                 state[name : name + 1, here] = halo[HALF + place : HALF + place + 1, :]
-        for r in (-1, 4):
+        steeps = {
+            -1: south[0] + own[1:2, lanes(0)],
+            0: own[0:1, lanes(0)] + south[1],
+            3: own[0:1, lanes(3)] + north[1],
+            4: north[0] + own[1:2, lanes(3)],
+        }
+        for r, value in steeps.items():
             known = state[SEA : SEA + 1, column(r)] > 0.5
-            state[STEEP0 : STEEP0 + 1, column(r)] = jnp.where(known, state[STEEP0 : STEEP0 + 1, column(r)], LAND)
-        steep0 = {r: held(STEEP0, r) for r in (-1, 4)}
-        wind0 = {r: held(WIND0, r) for r in (-1, 4)}
+            state[STEEP0 : STEEP0 + 1, column(r)] = jnp.where(known, value, LAND)
+        steep0 = {r: held(STEEP0, r) for r in steeps}
+        wind0 = {r: held(WIND0, r) for r in steeps}
 
         def step(pair, sums):
             return first(pair, sums, halo_south, halo_north, steep0, wind0)
@@ -643,13 +646,22 @@
         for r in range(ROWS):
             partial[r] = sums[r]
 
+    _, block = layout(held_rows, ranks)
+    me = lax.axis_index("geo")
+
+    def sent(source, there):
+        source = jnp.clip(source, 0, ranks - 1)
+        last = pl.ds(pl.multiple_of(source * block + block - SUB, SUB), SUB)
+        values = jnp.where(there, arrived[last, :], 0.0)
+        return values[SUB - 2 : SUB - 1, :], values[SUB - 1 : SUB, :]
+
     @pl.when(even)
     def _():
-        halo_terms(from_far, from_near)
+        halo_terms(from_far, from_near, sent(me - 1, me > 0), sent(me + 1, me < ranks - 1))
 
     @pl.when(jnp.logical_not(even))
     def _():
-        halo_terms(from_near, from_far)
+        halo_terms(from_near, from_far, sent(me - 1, me > 0), sent(me + 1, me < ranks - 1))
 
     for r in range(ROWS):
         value = state[STEEP1 : STEEP1 + 1, column(r)] + total(partial[r])
@@ -706,7 +718,7 @@
             cell = {}
             for r in range(ROWS):
                 cell[r] = split_lam(lam, group, tile, lanes(r)) * growth[group, rows, lanes(r)] + heavy * tend1[r]
-                source[group, rows, lanes(r)] = cell[r]
+                moved[group, rows, lanes(r)] = cell[r]
             for place, r in enumerate((0, ROWS - 1)):
                 value = middle * cell[r] + along * side(tile, sub, cell[r], True)
                 value = plus(value, times(over, pick(tile, sub, cell.get(r + 1), cell.get(r - 1))))
@@ -721,49 +733,61 @@
         state[GRAD0 : GRAD0 + 1, column(r)] = total(sums[place]) * LN2
         state[TEND0 : TEND0 + 1, column(r)] = total(sums[2 + place]) * (-LN2)
 
-    def fill(ref, base):
-        for f in range(NF):
-            ref[f : f + 1, :] = lam[f // 2, 4 * (f % 2) : 4 * (f % 2) + 1, pl.ds(base * W, 2 * W)]
-        here = pl.ds((base + 2) * W, 2 * W)
-        for place, name in enumerate((STEEP1, TEND1, TEND0, TEND0)):
-            ref[NF + place : NF + place + 1, :] = state[name : name + 1, here]
-
     @pl.when(even)
     def _():
-        fill(send_a, 2)
-        fill(send_b, 0)
+        fill(send_b, lam, state, 0)
 
     @pl.when(jnp.logical_not(even))
     def _():
-        fill(send_a, 0)
-        fill(send_b, 2)
-
-
-def late(next_, factor, moved, from_far, from_near, wanted, gain, state, coefficients):
-    inputs = [(next_, True), (factor, True), (moved, True), (from_far, True), (from_near, True)]
-    inputs += [(value, True) for value in (wanted, gain, state) + coefficients]
+        fill(send_b, lam, state, 2)
+
+
+def fill(ref, lam, state, base):
+    for f in range(NF):
+        ref[f : f + 1, :] = lam[f // 2, 4 * (f % 2) : 4 * (f % 2) + 1, pl.ds(base * W, 2 * W)]
+    here = pl.ds((base + 2) * W, 2 * W)
+    for place, name in enumerate((STEEP1, TEND1, TEND0, TEND0)):
+        ref[NF + place : NF + place + 1, :] = state[name : name + 1, here]
+
+
+def late(next_, factor, moved, from_far, from_near, arrived, own, state, coefficients, ranks, rows):
+    def kernel(*refs):
+        late_kernel(*refs, ranks=ranks, held_rows=rows)
+
+    inputs = (next_, factor, moved, from_far, from_near, arrived, own, state) + coefficients
     return call(
-        late_kernel,
+        kernel,
         "late",
-        inputs,
-        [(CELLS, True)] + [(EDGE, True)] * 2 + [(CELLS, True), (EDGES, True), (STATE, True)]
-        + [((NF + 4, 2 * W), False)] * 2 + [(CELLS, True)],
+        [(value, True) for value in inputs],
+        [(CELLS, True)] * 3 + [(EDGE, True)] * 2 + [(EDGES, True), (STATE, True), ((NF + 4, 2 * W), False)]
+        + [((GROUPS, SUB, ROWS * W), True)],
         [
             pltpu.VMEM(CELLS, F32),
+            pltpu.VMEM((ROWS, SUB, W), F32),
             pltpu.VMEM((GROUPS, SUB, ROWS * W), F32),
-            pltpu.VMEM((ROWS, SUB, W), F32),
+            pltpu.VMEM((SUB, ROWS * W), F32),
         ],
-        aliases={0: 0, 2: 8},
+        aliases={0: 0, 1: 1, 2: 2},
     )
 
 
 def inner_kernel(
-    next_, next_south, next_north, source, state_in, rate, damp, centre, back, across,
-    inside, factor_south, factor_north, state,
+    next_, next_south, next_north, source, state_in, lam, rate, damp, centre, back, across,
+    inside, factor_south, factor_north, state, send_a,
 ):
     sub = sublane()
     zero = jnp.zeros((SUB, W), F32)
     state[...] = state_in[...]
+    even = lax.rem(lax.axis_index("geo"), 2) == 0
+
+    @pl.when(even)
+    def _():
+        fill(send_a, lam, state, 2)
+
+    @pl.when(jnp.logical_not(even))
+    def _():
+        fill(send_a, lam, state, 0)
+
     wind0 = {r: full(state[WIND0 : WIND0 + 1, column(r)]) for r in (-1, 4)}
     steep0 = {r: full(state[STEEP0 : STEEP0 + 1, column(r)]) for r in (-1, 4)}
 
@@ -807,7 +831,7 @@
         inner_kernel,
         "inner",
         [(arg, True) for arg in args],
-        [(EDGES, True), (EDGE, True), (EDGE, True), (STATE, True)],
+        [(EDGES, True), (EDGE, True), (EDGE, True), (STATE, True), ((NF + 4, 2 * W), False)],
         cost=1 << 22,
     )
 
@@ -964,7 +988,7 @@
     field = initial_spectrum.reshape(CELLS)
     sea = sea_mask.reshape(1, ROWS * W)
     from_far = lax.ppermute(far_rows(field, sea, wind_forcing), "geo", far)
-    flow, rate, damp, steep, centre, ahead, back, across, own, slots = local(
+    flow, rate, damp, steep, centre, ahead, back, across, own = local(
         field,
         sea,
         courant,
@@ -972,24 +996,23 @@
         damping.reshape(1, NB),
         steep_weight.reshape(1, NB),
         jnp.asarray(direction_tables()),
-        obs_owner.reshape(1, held),
-        obs_point.reshape(1, held),
-        obs_value.T,
-        obs_weight.reshape(1, held),
-        count,
-    )
-    from_near = lax.ppermute(near_rows(field, sea, wind_forcing, own), "geo", near)
+    )
+    rows = near_rows(field, sea, wind_forcing, own)
+    from_near = lax.ppermute(rows, "geo", near)
+    next_, factor, moved, state, slots = middle(
+        flow, own, wind_forcing, sea, (rate, damp, steep, centre, ahead, across),
+        (obs_owner.reshape(1, held), obs_point.reshape(1, held), obs_value.T, obs_weight.reshape(1, held)), rows, count,
+    )
     arrived = lax.all_to_all(slots, "geo", split_axis=0, concat_axis=0, tiled=True)
-    next_, factor, moved, wanted, gain, state = early(
-        arrived, flow, own, wind_forcing, sea, rate, damp, steep, centre, ahead, across, count, held
-    )
-    next_, next_south, next_north, source, edges, state, send_a, send_b, _ = late(
-        next_, factor, moved, from_far, from_near, wanted, gain, state,
-        (rate, damp, steep, centre, ahead, back, across),
+    next_, factor, source, next_south, next_north, edges, state, send_b, lam = late(
+        next_, factor, moved, from_far, from_near, arrived, own, state,
+        (rate, damp, steep, centre, ahead, back, across), count, held,
     )
     back_b = lax.ppermute(send_b, "geo", far)
+    inside, factor_south, factor_north, state, send_a = inner(
+        next_, next_south, next_north, source, state, lam, rate, damp, centre, back, across
+    )
     back_a = lax.ppermute(send_a, "geo", near)
-    inside, factor_south, factor_north, state = inner(next_, next_south, next_north, source, state, rate, damp, centre, back, across)
     out, grad = last(
         next_, factor, factor_south, factor_north, edges, inside, state, back_a, back_b,
         (rate, damp, steep, centre, back, across),

time: 39.8 us -> 38.9 us (0.977); the launches traced: 39 us -> 38.6 us
  Pallas kernels: 16.1 us -> 17.4 us
  starting transfers between devices: 9.06 us -> 7.77 us
  blocking collectives: 12.3 us -> 11.2 us
  waiting for transfers between devices: 0.55 us -> 1.21 us
    pallas_call x7, Pallas kernels: 16.1 us -> 17.4 us  [call(): pl.pallas_call(kernel, in_specs=specs, out_specs=[whole(pl.ANY if place i...]
    ppermute x1, starting transfers between devices: 4.44 us -> 3.14 us  [body(): back_b = lax.ppermute(send_b, 'geo', far)]
    all_to_all x1, blocking collectives: 12.3 us -> 11.2 us  [body(): lax.all_to_all(slots, 'geo', split_axis=0, concat_axis=0, tiled=True)]
  transfers between devices with their start and end apart: 4 -> 4, of which waited for: 1 -> 2; matrix products, arithmetic and copies ran while one was open for 0% -> 0% of each run, Pallas kernels for 16% -> 17%
where the time goes in v5:
time: 38.9 us; the launch traced here: 38.6 us
  Pallas kernels  17.4 us (45%)
  blocking collectives  11.2 us (29%)
  starting transfers between devices  7.77 us (20%)
  waiting for transfers between devices  1.21 us (3%)
  between operations  0.92 us (2%)
    pallas_call x7, Pallas kernels, call(): pl.pallas_call(kernel, in_specs=specs, out_specs=[whole(pl.ANY if place i...  17.4 us
    all_to_all x1, blocking collectives, body(): lax.all_to_all(slots, 'geo', split_axis=0, concat_axis=0, tiled=True)  11.2 us
    ppermute x1, starting transfers between devices, body(): from_far = lax.ppermute(far_rows(field, sea, wind_forcing), 'geo', far)  4.49 us
    ppermute x1, starting transfers between devices, body(): back_b = lax.ppermute(send_b, 'geo', far)  3.14 us
    ppermute x1, waiting for transfers between devices, body(): back_b = lax.ppermute(send_b, 'geo', far)  0.92 us
  transfers between devices with their start and end apart: 4, of which 2 were waited for; matrix products, arithmetic and copies ran while one was open for 0% of the time, Pallas kernels for 17%

profile of v5, /device:TPU:1, one launch (start us, length us, event | category | flops | bytes accessed | tf_op | source)
XLA Modules:
  0.0 38.6 jit_solution(4491359218806231776)
XLA Ops:
  0.6 0.0 copy-start.1
  0.6 0.0 copy-start.3
  0.7 0.0 copy-start
  0.7 0.0 copy-start.9
  0.7 0.0 copy-start.10
  0.7 0.0 copy-start.11
  0.7 0.0 copy-start.5
  0.7 0.0 copy-start.2
  0.7 1.6 %far.1 = f32[656,256]{1,0:T(8,128)S(1)} custom-call(f32[18,72,512]{2,1,0:T(8,128)} %bitcast.9, s32[1,512]{1,0:T(1,128)} %bitcast.14, f32[2,512]{1,0:T(2,128)} %wind_in.1), custom_call_target="tpu_custom_call" | custom-call | tf_op jit(solution)/shard_map/far/pallas_call | solution.py:148
  2.3 4.5 %collective-permute-start = (f32[656,256]{1,0:T(8,128)S(1)}, f32[656,256]{1,0:T(8,128)S(1)}, u32[]{:S(2)}, u32[]{:S(2)}) collective-permute-start(f32[656,256]{1,0:T(8,128)S(1)} %far.1), channel_id=1, source_target_pairs={{1,2},{2,1},{3,4},{4,3},{5,6},{6,5},{7,8},{8,7},{9,10},{10,9},{11,... | collective-permute-start | bytes 2015240 | tf_op jit(solution)/shard_map/ppermute | solution.py:990
  6.8 0.0 copy-done.9
  6.8 0.0 copy-done.10
  6.8 0.0 copy-done.11
  6.9 0.0 copy-done.1
  6.9 0.0 copy-done.3
  6.9 0.0 copy-done
  6.9 0.0 copy-done.5
  6.9 0.0 copy-start.4
  6.9 0.0 copy-start.6
  6.9 0.0 copy-start.7
  6.9 0.0 copy-start.8
  6.9 2.6 %local.1 = (f32[18,72,512]{2,1,0:T(8,128)S(1)}, f32[1296,128]{1,0:T(8,128)S(1)}, f32[1296,128]{1,0:T(8,128)S(1)}, f32[1296,128]{1,0:T(8,128)S(1)}, f32[1296,128]...) custom-call(f32[18,72,512]{2,1,0:T(8,128)S(1)} %bitcast.10, ...), custom_call_target="tpu_custom_call" | custom-call | tf_op jit(solution)/shard_map/local/pallas_call | solution.py:148
  9.6 0.0 copy-done.2
  9.6 0.2 near.1.refs_14_
  9.8 0.1 collective-permute-start.1
  9.8 0.0 copy-done.4
  9.9 0.0 copy-done.6
  9.9 0.0 copy-done.7
  9.9 0.0 copy-done.8
  9.9 2.5 %middle.1 = (f32[18,72,512]{2,1,0:T(8,128)S(1)}, f32[18,72,512]{2,1,0:T(8,128)S(1)}, f32[18,72,512]{2,1,0:T(8,128)S(1)}, f32[16,1024]{1,0:T(8,128)S(1)}, f32[128,128]{1,0:T(8,128)S(1)}) custom-call(f32[18,72,512]{2,1,0:T(8,128)S(1)} %get-tuple-element.32.refs_0_, ...), custom_call_target="tpu_custom_call", output_to_operand_aliasing={{0}: (0, {})} | custom-call | tf_op jit(solution)/shard_map/middle/pallas_call | solution.py:148
  12.4 11.2 %all_to_all.11 = f32[16,8,128]{2,1,0:T(8,128)S(1)} all-to-all(f32[16,8,128]{2,1,0:T(8,128)S(1)} %bitcast.13), channel_id=1, replica_groups=mesh['groups'=2,'geo'=16] {'geo'}, dimensions={0} | all-to-all | bytes 131072 | tf_op jit(solution)/shard_map/all_to_all | solution.py:1006
  23.6 0.0 collective-permute-done.refs_3_
  23.6 0.0 collective-permute-done.1.refs_4_
  23.6 5.6 %late.1 = (f32[18,72,512]{2,1,0:T(8,128)S(1)}, f32[18,72,512]{2,1,0:T(8,128)S(1)}, f32[18,72,512]{2,1,0:T(8,128)S(1)}, f32[18,72,128]{2,1,0:T(8,128)S(1)}, f32[1...) custom-call(f32[18,72,512]{2,1,0:T(8,128)S(1)} %get-tuple-element.40, ...), custom_call_target="tpu_custom_call", output_to_operand_aliasing={{0}: (0, {}), {1}: (1, {}), {2}: (2, {})} | custom-call | tf_op jit(solution)/shard_map/late/pallas_call | solution.py:148
  29.2 3.1 %collective-permute-start.3 = (f32[40,256]{1,0:T(8,128)S(1)}, f32[40,256]{1,0:T(8,128)S(1)}, u32[]{:S(2)}, u32[]{:S(2)}) collective-permute-start(f32[40,256]{1,0:T(8,128)S(1)} %get-tuple-element.59), channel_id=1, source_target_pairs={{1,2},{2,1},{3,4},{4,3},{5,6},{6,5},{7,8},{8,7},{9,10},{10,9},{11,... | collective-permute-start | bytes 122888 | tf_op jit(solution)/shard_map/ppermute | solution.py:1011
  32.3 1.2 %inner.1 = (f32[18,72,256]{2,1,0:T(8,128)S(1)}, f32[18,72,128]{2,1,0:T(8,128)S(1)}, f32[18,72,128]{2,1,0:T(8,128)S(1)}, f32[16,1024]{1,0:T(8,128)S(1)}, f32[40,256]{1,0:T(8,128)S(1)}) custom-call(f32[18,72,512]{2,1,0:T(8,128)S(1)} %get-tuple-element.46.next_, f32[18,72,128]{2,1,0:T(8,128)S(1)} %get-tuple-element.48.next_south, ...), custom_call_target="tpu_custom_call" | custom-call | flops 4194304 | bytes 4194304 | tf_op jit(solution)/shard_map/inner/pallas_call | solution.py:148
  33.5 0.1 collective-permute-start.2
  33.6 0.9 %collective-permute-done.3.back_b = f32[40,256]{1,0:T(8,128)S(1)} collective-permute-done((f32[40,256]{1,0:T(8,128)S(1)}, f32[40,256]{1,0:T(8,128)S(1)}, u32[]{:S(2)}, u32[]{:S(2)}) %collective-permute-start.3) | collective-permute-done | bytes 40992 | tf_op jit(solution)/shard_map/ppermute | solution.py:1011
  34.5 0.3 collective-permute-done.2.back_a
  34.8 3.8 %last.1 = (f32[18,72,512]{2,1,0:T(8,128)}, f32[2,512]{1,0:T(2,128)}) custom-call(f32[18,72,512]{2,1,0:T(8,128)S(1)} %get-tuple-element.46.next_, f32[18,72,512]{2,1,0:T(8,128)S(1)} %get-tuple-element.47.factor, f32[18,72,128]{2,1,0:T(8,128)S(1)} %get-tuple-element.53.factor_south, f32[18,72,128]{2,1,0:T(8,128)S(1)} %get-tuple-element.54.factor_north, ...), custom_call_target="tpu_custom_call" | custom-call | tf_op jit(solution)/shard_map/last/pallas_call | solution.py:148
  (3 shorter events, 0.0 us)
Async XLA Ops:
  0.6 6.2 %copy-start.1 = (f32[4,72,128]{2,1,0:T(8,128)S(1)}, f32[4,72,128]{2,1,0:T(8,128)}, u32[]{:S(2)}) copy-start(f32[4,72,128]{2,1,0:T(8,128)} %constant.2.clone.table) | copy-start | bytes 442372
  0.6 6.2 %copy-start.3 = (s32[512]{0:T(512)S(1)}, s32[512]{0:T(512)}, u32[]{:S(2)}) copy-start(s32[512]{0:T(512)} %param.14) | copy-start | bytes 6148
  0.7 6.2 %copy-start = (f32[1296,512]{1,0:T(8,128)S(1)}, f32[1296,512]{1,0:T(8,128)}, u32[]{:S(2)}) copy-start(f32[1296,512]{1,0:T(8,128)} %param.12) | copy-start | bytes 7962628
  0.7 6.1 %copy-start.9 = (f32[1296]{0:T(1024)S(1)}, f32[1296]{0:T(1024)}, u32[]{:S(2)}) copy-start(f32[1296]{0:T(1024)} %param.16) | copy-start | bytes 15556
  0.7 6.1 %copy-start.10 = (f32[1296]{0:T(1024)S(1)}, f32[1296]{0:T(1024)}, u32[]{:S(2)}) copy-start(f32[1296]{0:T(1024)} %param.17) | copy-start | bytes 15556
  0.7 6.1 %copy-start.11 = (f32[1296]{0:T(1024)S(1)}, f32[1296]{0:T(1024)}, u32[]{:S(2)}) copy-start(f32[1296]{0:T(1024)} %param.18) | copy-start | bytes 15556
  0.7 6.2 %copy-start.5 = (f32[36]{0:T(128)S(1)}, f32[36]{0:T(128)}, u32[]{:S(2)}) copy-start(f32[36]{0:T(128)} %courant.1) | copy-start | bytes 436
  0.7 8.9 %copy-start.2 = (f32[2,512]{1,0:T(2,128)S(1)}, f32[2,512]{1,0:T(2,128)}, u32[]{:S(2)}) copy-start(f32[2,512]{1,0:T(2,128)} %wind_in.1) | copy-start | bytes 12292
  2.3 21.3 %collective-permute-start = (f32[656,256]{1,0:T(8,128)S(1)}, f32[656,256]{1,0:T(8,128)S(1)}, u32[]{:S(2)}, u32[]{:S(2)}) collective-permute-start(f32[656,256]{1,0:T(8,128)S(1)} %far.1), channel_id=1, source_target_pairs={{1,2},{2,1},{3,4},{4,3},{5,6},{6,5},{7,8},{8,7},{9,10},{10,9},{11,... | collective-permute-start | bytes 2015240 | tf_op jit(solution)/shard_map/ppermute | solution.py:990
  6.9 3.0 %copy-start.4 = (f32[128,36]{0,1:T(8,128)S(1)}, f32[128,36]{0,1:T(8,128)}, u32[]{:S(2)}) copy-start(f32[128,36]{0,1:T(8,128)} %param.21) | copy-start | bytes 55300
  6.9 3.0 %copy-start.6 = (s32[128,1]{0,1:T(1,128)S(1)}, s32[128,1]{0,1:T(1,128)}, u32[]{:S(2)}) copy-start(s32[128,1]{0,1:T(1,128)} %param.19) | copy-start | bytes 1540
  6.9 2.9 %copy-start.7 = (s32[128]{0:T(128)S(1)}, s32[128]{0:T(128)}, u32[]{:S(2)}) copy-start(s32[128]{0:T(128)} %param.20) | copy-start | bytes 1540
  6.9 2.9 %copy-start.8 = (f32[128]{0:T(128)S(1)}, f32[128]{0:T(128)}, u32[]{:S(2)}) copy-start(f32[128]{0:T(128)} %param.22) | copy-start | bytes 1540
  9.8 13.8 %collective-permute-start.1 = (f32[656,256]{1,0:T(8,128)S(1)}, f32[656,256]{1,0:T(8,128)S(1)}, u32[]{:S(2)}, u32[]{:S(2)}) collective-permute-start(f32[656,256]{1,0:T(8,128)S(1)} %near.1.refs_14_), channel_id=1, source_target_pairs={{0,1},{1,0},{2,3},{3,2},{4,5},{5,4},{6,7},{7,6},{8,9},{9,8},{10,11... | collective-permute-start | bytes 2015240 | tf_op jit(solution)/shard_map/ppermute | solution.py:1001
  29.2 5.3 %collective-permute-start.3 = (f32[40,256]{1,0:T(8,128)S(1)}, f32[40,256]{1,0:T(8,128)S(1)}, u32[]{:S(2)}, u32[]{:S(2)}) collective-permute-start(f32[40,256]{1,0:T(8,128)S(1)} %get-tuple-element.59), channel_id=1, source_target_pairs={{1,2},{2,1},{3,4},{4,3},{5,6},{6,5},{7,8},{8,7},{9,10},{10,9},{11,... | collective-permute-start | bytes 122888 | tf_op jit(solution)/shard_map/ppermute | solution.py:1011
  33.5 1.3 %collective-permute-start.2 = (f32[40,256]{1,0:T(8,128)S(1)}, f32[40,256]{1,0:T(8,128)S(1)}, u32[]{:S(2)}, u32[]{:S(2)}) collective-permute-start(f32[40,256]{1,0:T(8,128)S(1)} %get-tuple-element.58), channel_id=1, source_target_pairs={{0,1},{1,0},{2,3},{3,2},{4,5},{5,4},{6,7},{7,6},{8,9},{9,8},{10,11... | collective-permute-start | bytes 122888 | tf_op jit(solution)/shard_map/ppermute | solution.py:1015

commit v6 on v5

--- a/solution.py
+++ b/solution.py
@@ -189,7 +189,7 @@
         pack_rows(cell, put, sub, north)
         return carry
 
-    loop(low, high, 1, step, 0)
+    loop(low, high, high - low, step, 0)
 
 
 def pack_small(out, wind, sea, base):
@@ -430,7 +430,7 @@
                 sums[ROWS + 1] = sums[ROWS + 1] + pick(tile, sub, None, gone * cell[0])
         return tuple(sums)
 
-    sums = loop(0, GROUPS, 3, step, (zero,) * (ROWS + 2))
+    sums = loop(0, GROUPS, 6, step, (zero,) * (ROWS + 2))
     sums = [total(value) for value in sums]
     own[...] = jnp.zeros_like(own)
     for r in range(ROWS):
@@ -530,7 +530,7 @@
                 sums[r] = sums[r] + heavy * value
         return tuple(sums)
 
-    sums = loop(0, GROUPS, 3, step, (jnp.zeros((SUB, W), F32),) * ROWS)
+    sums = loop(0, GROUPS, 6, step, (jnp.zeros((SUB, W), F32),) * ROWS)
     for r in range(ROWS):
         state[STEEP1 : STEEP1 + 1, column(r)] = total(sums[r])
 
@@ -642,7 +642,7 @@
         def step(pair, sums):
             return first(pair, sums, halo_south, halo_north, steep0, wind0)
 
-        sums = loop(0, GROUPS // 2, 3, step, (zero,) * ROWS)
+        sums = loop(0, GROUPS // 2, 9, step, (zero,) * ROWS)
         for r in range(ROWS):
             partial[r] = sums[r]
 
@@ -703,7 +703,7 @@
             sums[ROWS + r] = sums[ROWS + r] + (up * downs[r][0] + down * downs[r][1])
         return tuple(sums)
 
-    sums = loop(0, GROUPS, 1, second, (zero,) * (2 * ROWS))
+    sums = loop(0, GROUPS, 6, second, (zero,) * (2 * ROWS))
     for r in range(ROWS):
         state[GRAD1 : GRAD1 + 1, column(r)] = total(sums[r]) * LN2
         state[TEND1 : TEND1 + 1, column(r)] = total(sums[ROWS + r]) * (-LN2)
@@ -728,7 +728,7 @@
                 sums[2 + place] = sums[2 + place] + fade * value
         return tuple(sums)
 
-    sums = loop(0, GROUPS, 3, third, (zero,) * 4)
+    sums = loop(0, GROUPS, 6, third, (zero,) * 4)
     for place, r in enumerate((0, ROWS - 1)):
         state[GRAD0 : GRAD0 + 1, column(r)] = total(sums[place]) * LN2
         state[TEND0 : TEND0 + 1, column(r)] = total(sums[2 + place]) * (-LN2)
@@ -818,7 +818,7 @@
                 sums[5] = sums[5] + gone * value
         return tuple(sums)
 
-    sums = loop(0, GROUPS, 3, step, (zero,) * 6)
+    sums = loop(0, GROUPS, 6, step, (zero,) * 6)
     for place, r in enumerate((1, 2)):
         state[GRAD0 : GRAD0 + 1, column(r)] = total(sums[place]) * LN2
         state[TEND0 : TEND0 + 1, column(r)] = total(sums[2 + place]) * (-LN2)
@@ -885,7 +885,7 @@
                 sums[2 + place] = sums[2 + place] + fade * value
         return tuple(sums)
 
-    sums = loop(0, GROUPS, 3, first, (zero,) * 4)
+    sums = loop(0, GROUPS, 6, first, (zero,) * 4)
     sums = [total(value) * LN2 for value in sums]
     tend0 = {r: state[TEND0 : TEND0 + 1, column(r)] for r in range(-1, 5)}
     grad0 = [state[GRAD0 : GRAD0 + 1, column(r)] for r in range(ROWS)]

time: 38.9 us -> 37.5 us (0.964)
  Pallas kernels: 17.4 us -> 15.4 us
  starting transfers between devices: 7.77 us -> 8.3 us
    pallas_call x7, Pallas kernels: 17.4 us -> 15.4 us  [call(): pl.pallas_call(kernel, in_specs=specs, out_specs=[whole(pl.ANY if place i...]
    ppermute x1, starting transfers between devices: 3.14 us -> 3.67 us  [body(): back_b = lax.ppermute(send_b, 'geo', far)]
  transfers between devices with their start and end apart: 4 -> 4, of which waited for: 2 -> 2; matrix products, arithmetic and copies ran while one was open for 0% -> 0% of each run, Pallas kernels for 17% -> 16%
where the time goes in v6:
time: 37.5 us; the launch traced here: 37.1 us
  Pallas kernels  15.4 us (41%)
  blocking collectives  11.2 us (30%)
  starting transfers between devices  8.3 us (22%)
  waiting for transfers between devices  1.21 us (3%)
  between operations  0.91 us (2%)
    pallas_call x7, Pallas kernels, call(): pl.pallas_call(kernel, in_specs=specs, out_specs=[whole(pl.ANY if place i...  15.4 us
    all_to_all x1, blocking collectives, body(): lax.all_to_all(slots, 'geo', split_axis=0, concat_axis=0, tiled=True)  11.2 us
    ppermute x1, starting transfers between devices, body(): from_far = lax.ppermute(far_rows(field, sea, wind_forcing), 'geo', far)  4.49 us
    ppermute x1, starting transfers between devices, body(): back_b = lax.ppermute(send_b, 'geo', far)  3.67 us
  transfers between devices with their start and end apart: 4, of which 2 were waited for; matrix products, arithmetic and copies ran while one was open for 0% of the time, Pallas kernels for 16%

profile of v6, /device:TPU:1, one launch (start us, length us, event | category | flops | bytes accessed | tf_op | source)
XLA Modules:
  0.0 37.1 jit_solution(17782267887228440800)
XLA Ops:
  0.6 0.0 copy-start.1
  0.6 0.0 copy-start.3
  0.7 0.0 copy-start
  0.7 0.0 copy-start.9
  0.7 0.0 copy-start.10
  0.7 0.0 copy-start.11
  0.7 0.0 copy-start.5
  0.7 0.0 copy-start.2
  0.7 1.5 %far.1 = f32[656,256]{1,0:T(8,128)S(1)} custom-call(f32[18,72,512]{2,1,0:T(8,128)} %bitcast.9, s32[1,512]{1,0:T(1,128)} %bitcast.14, f32[2,512]{1,0:T(2,128)} %wind_in.1), custom_call_target="tpu_custom_call" | custom-call | tf_op jit(solution)/shard_map/far/pallas_call | solution.py:148
  2.3 4.5 %collective-permute-start = (f32[656,256]{1,0:T(8,128)S(1)}, f32[656,256]{1,0:T(8,128)S(1)}, u32[]{:S(2)}, u32[]{:S(2)}) collective-permute-start(f32[656,256]{1,0:T(8,128)S(1)} %far.1), channel_id=1, source_target_pairs={{1,2},{2,1},{3,4},{4,3},{5,6},{6,5},{7,8},{8,7},{9,10},{10,9},{11,... | collective-permute-start | bytes 2015240 | tf_op jit(solution)/shard_map/ppermute | solution.py:990
  6.8 0.0 copy-done.9
  6.8 0.0 copy-done.10
  6.8 0.0 copy-done.11
  6.8 0.0 copy-done.1
  6.8 0.0 copy-done.3
  6.8 0.0 copy-done
  6.9 0.0 copy-done.5
  6.9 0.0 copy-start.4
  6.9 0.0 copy-start.6
  6.9 0.0 copy-start.7
  6.9 0.0 copy-start.8
  6.9 2.4 %local.1 = (f32[18,72,512]{2,1,0:T(8,128)S(1)}, f32[1296,128]{1,0:T(8,128)S(1)}, f32[1296,128]{1,0:T(8,128)S(1)}, f32[1296,128]{1,0:T(8,128)S(1)}, f32[1296,128]...) custom-call(f32[18,72,512]{2,1,0:T(8,128)S(1)} %bitcast.10, ...), custom_call_target="tpu_custom_call" | custom-call | tf_op jit(solution)/shard_map/local/pallas_call | solution.py:148
  9.4 0.0 copy-done.2
  9.4 0.1 near.1.refs_14_
  9.5 0.1 collective-permute-start.1
  9.5 0.0 copy-done.4
  9.5 0.0 copy-done.6
  9.6 0.0 copy-done.7
  9.6 0.0 copy-done.8
  9.6 2.2 %middle.1 = (f32[18,72,512]{2,1,0:T(8,128)S(1)}, f32[18,72,512]{2,1,0:T(8,128)S(1)}, f32[18,72,512]{2,1,0:T(8,128)S(1)}, f32[16,1024]{1,0:T(8,128)S(1)}, f32[128,128]{1,0:T(8,128)S(1)}) custom-call(f32[18,72,512]{2,1,0:T(8,128)S(1)} %get-tuple-element.32.refs_0_, ...), custom_call_target="tpu_custom_call", output_to_operand_aliasing={{0}: (0, {})} | custom-call | tf_op jit(solution)/shard_map/middle/pallas_call | solution.py:148
  11.8 11.2 %all_to_all.11 = f32[16,8,128]{2,1,0:T(8,128)S(1)} all-to-all(f32[16,8,128]{2,1,0:T(8,128)S(1)} %bitcast.13), channel_id=1, replica_groups=mesh['groups'=2,'geo'=16] {'geo'}, dimensions={0} | all-to-all | bytes 131072 | tf_op jit(solution)/shard_map/all_to_all | solution.py:1006
  23.0 0.0 collective-permute-done.refs_3_
  23.0 0.0 collective-permute-done.1.refs_4_
  23.0 4.4 %late.1 = (f32[18,72,512]{2,1,0:T(8,128)S(1)}, f32[18,72,512]{2,1,0:T(8,128)S(1)}, f32[18,72,512]{2,1,0:T(8,128)S(1)}, f32[18,72,128]{2,1,0:T(8,128)S(1)}, f32[1...) custom-call(f32[18,72,512]{2,1,0:T(8,128)S(1)} %get-tuple-element.40, ...), custom_call_target="tpu_custom_call", output_to_operand_aliasing={{0}: (0, {}), {1}: (1, {}), {2}: (2, {})} | custom-call | tf_op jit(solution)/shard_map/late/pallas_call | solution.py:148
  27.4 3.7 %collective-permute-start.3 = (f32[40,256]{1,0:T(8,128)S(1)}, f32[40,256]{1,0:T(8,128)S(1)}, u32[]{:S(2)}, u32[]{:S(2)}) collective-permute-start(f32[40,256]{1,0:T(8,128)S(1)} %get-tuple-element.59), channel_id=1, source_target_pairs={{1,2},{2,1},{3,4},{4,3},{5,6},{6,5},{7,8},{8,7},{9,10},{10,9},{11,... | collective-permute-start | bytes 122888 | tf_op jit(solution)/shard_map/ppermute | solution.py:1011
  31.1 1.0 %inner.1 = (f32[18,72,256]{2,1,0:T(8,128)S(1)}, f32[18,72,128]{2,1,0:T(8,128)S(1)}, f32[18,72,128]{2,1,0:T(8,128)S(1)}, f32[16,1024]{1,0:T(8,128)S(1)}, f32[40,256]{1,0:T(8,128)S(1)}) custom-call(f32[18,72,512]{2,1,0:T(8,128)S(1)} %get-tuple-element.46.next_, f32[18,72,128]{2,1,0:T(8,128)S(1)} %get-tuple-element.48.next_south, ...), custom_call_target="tpu_custom_call" | custom-call | flops 4194304 | bytes 4194304 | tf_op jit(solution)/shard_map/inner/pallas_call | solution.py:148
  32.2 0.1 collective-permute-start.2
  32.2 0.5 %collective-permute-done.3.back_b = f32[40,256]{1,0:T(8,128)S(1)} collective-permute-done((f32[40,256]{1,0:T(8,128)S(1)}, f32[40,256]{1,0:T(8,128)S(1)}, u32[]{:S(2)}, u32[]{:S(2)}) %collective-permute-start.3) | collective-permute-done | bytes 40992 | tf_op jit(solution)/shard_map/ppermute | solution.py:1011
  32.8 0.7 %collective-permute-done.2.back_a = f32[40,256]{1,0:T(8,128)S(1)} collective-permute-done((f32[40,256]{1,0:T(8,128)S(1)}, f32[40,256]{1,0:T(8,128)S(1)}, u32[]{:S(2)}, u32[]{:S(2)}) %collective-permute-start.2) | collective-permute-done | bytes 40992 | tf_op jit(solution)/shard_map/ppermute | solution.py:1015
  33.4 3.7 %last.1 = (f32[18,72,512]{2,1,0:T(8,128)}, f32[2,512]{1,0:T(2,128)}) custom-call(f32[18,72,512]{2,1,0:T(8,128)S(1)} %get-tuple-element.46.next_, f32[18,72,512]{2,1,0:T(8,128)S(1)} %get-tuple-element.47.factor, f32[18,72,128]{2,1,0:T(8,128)S(1)} %get-tuple-element.53.factor_south, f32[18,72,128]{2,1,0:T(8,128)S(1)} %get-tuple-element.54.factor_north, ...), custom_call_target="tpu_custom_call" | custom-call | tf_op jit(solution)/shard_map/last/pallas_call | solution.py:148
  (3 shorter events, 0.0 us)
Async XLA Ops:
  0.6 6.2 %copy-start.1 = (f32[4,72,128]{2,1,0:T(8,128)S(1)}, f32[4,72,128]{2,1,0:T(8,128)}, u32[]{:S(2)}) copy-start(f32[4,72,128]{2,1,0:T(8,128)} %constant.2.clone.table) | copy-start | bytes 442372
  0.6 6.2 %copy-start.3 = (s32[512]{0:T(512)S(1)}, s32[512]{0:T(512)}, u32[]{:S(2)}) copy-start(s32[512]{0:T(512)} %param.14) | copy-start | bytes 6148
  0.7 6.2 %copy-start = (f32[1296,512]{1,0:T(8,128)S(1)}, f32[1296,512]{1,0:T(8,128)}, u32[]{:S(2)}) copy-start(f32[1296,512]{1,0:T(8,128)} %param.12) | copy-start | bytes 7962628
  0.7 6.1 %copy-start.9 = (f32[1296]{0:T(1024)S(1)}, f32[1296]{0:T(1024)}, u32[]{:S(2)}) copy-start(f32[1296]{0:T(1024)} %param.16) | copy-start | bytes 15556
  0.7 6.1 %copy-start.10 = (f32[1296]{0:T(1024)S(1)}, f32[1296]{0:T(1024)}, u32[]{:S(2)}) copy-start(f32[1296]{0:T(1024)} %param.17) | copy-start | bytes 15556
  0.7 6.1 %copy-start.11 = (f32[1296]{0:T(1024)S(1)}, f32[1296]{0:T(1024)}, u32[]{:S(2)}) copy-start(f32[1296]{0:T(1024)} %param.18) | copy-start | bytes 15556
  0.7 6.2 %copy-start.5 = (f32[36]{0:T(128)S(1)}, f32[36]{0:T(128)}, u32[]{:S(2)}) copy-start(f32[36]{0:T(128)} %courant.1) | copy-start | bytes 436
  0.7 8.7 %copy-start.2 = (f32[2,512]{1,0:T(2,128)S(1)}, f32[2,512]{1,0:T(2,128)}, u32[]{:S(2)}) copy-start(f32[2,512]{1,0:T(2,128)} %wind_in.1) | copy-start | bytes 12292
  2.3 20.7 %collective-permute-start = (f32[656,256]{1,0:T(8,128)S(1)}, f32[656,256]{1,0:T(8,128)S(1)}, u32[]{:S(2)}, u32[]{:S(2)}) collective-permute-start(f32[656,256]{1,0:T(8,128)S(1)} %far.1), channel_id=1, source_target_pairs={{1,2},{2,1},{3,4},{4,3},{5,6},{6,5},{7,8},{8,7},{9,10},{10,9},{11,... | collective-permute-start | bytes 2015240 | tf_op jit(solution)/shard_map/ppermute | solution.py:990
  6.9 2.7 %copy-start.4 = (f32[128,36]{0,1:T(8,128)S(1)}, f32[128,36]{0,1:T(8,128)}, u32[]{:S(2)}) copy-start(f32[128,36]{0,1:T(8,128)} %param.21) | copy-start | bytes 55300
  6.9 2.7 %copy-start.6 = (s32[128,1]{0,1:T(1,128)S(1)}, s32[128,1]{0,1:T(1,128)}, u32[]{:S(2)}) copy-start(s32[128,1]{0,1:T(1,128)} %param.19) | copy-start | bytes 1540
  6.9 2.7 %copy-start.7 = (s32[128]{0:T(128)S(1)}, s32[128]{0:T(128)}, u32[]{:S(2)}) copy-start(s32[128]{0:T(128)} %param.20) | copy-start | bytes 1540
  6.9 2.7 %copy-start.8 = (f32[128]{0:T(128)S(1)}, f32[128]{0:T(128)}, u32[]{:S(2)}) copy-start(f32[128]{0:T(128)} %param.22) | copy-start | bytes 1540
  9.5 13.6 %collective-permute-start.1 = (f32[656,256]{1,0:T(8,128)S(1)}, f32[656,256]{1,0:T(8,128)S(1)}, u32[]{:S(2)}, u32[]{:S(2)}) collective-permute-start(f32[656,256]{1,0:T(8,128)S(1)} %near.1.refs_14_), channel_id=1, source_target_pairs={{0,1},{1,0},{2,3},{3,2},{4,5},{5,4},{6,7},{7,6},{8,9},{9,8},{10,11... | collective-permute-start | bytes 2015240 | tf_op jit(solution)/shard_map/ppermute | solution.py:1001
  27.4 5.4 %collective-permute-start.3 = (f32[40,256]{1,0:T(8,128)S(1)}, f32[40,256]{1,0:T(8,128)S(1)}, u32[]{:S(2)}, u32[]{:S(2)}) collective-permute-start(f32[40,256]{1,0:T(8,128)S(1)} %get-tuple-element.59), channel_id=1, source_target_pairs={{1,2},{2,1},{3,4},{4,3},{5,6},{6,5},{7,8},{8,7},{9,10},{10,9},{11,... | collective-permute-start | bytes 122888 | tf_op jit(solution)/shard_map/ppermute | solution.py:1011
  32.2 1.3 %collective-permute-start.2 = (f32[40,256]{1,0:T(8,128)S(1)}, f32[40,256]{1,0:T(8,128)S(1)}, u32[]{:S(2)}, u32[]{:S(2)}) collective-permute-start(f32[40,256]{1,0:T(8,128)S(1)} %get-tuple-element.58), channel_id=1, source_target_pairs={{0,1},{1,0},{2,3},{3,2},{4,5},{5,4},{6,7},{7,6},{8,9},{9,8},{10,11... | collective-permute-start | bytes 122888 | tf_op jit(solution)/shard_map/ppermute | solution.py:1015

commit v7 on v6

--- a/solution.py
+++ b/solution.py
@@ -430,7 +430,7 @@
                 sums[ROWS + 1] = sums[ROWS + 1] + pick(tile, sub, None, gone * cell[0])
         return tuple(sums)
 
-    sums = loop(0, GROUPS, 6, step, (zero,) * (ROWS + 2))
+    sums = loop(0, GROUPS, GROUPS, step, (zero,) * (ROWS + 2))
     sums = [total(value) for value in sums]
     own[...] = jnp.zeros_like(own)
     for r in range(ROWS):
@@ -530,7 +530,7 @@
                 sums[r] = sums[r] + heavy * value
         return tuple(sums)
 
-    sums = loop(0, GROUPS, 6, step, (jnp.zeros((SUB, W), F32),) * ROWS)
+    sums = loop(0, GROUPS, GROUPS, step, (jnp.zeros((SUB, W), F32),) * ROWS)
     for r in range(ROWS):
         state[STEEP1 : STEEP1 + 1, column(r)] = total(sums[r])
 
@@ -838,7 +838,7 @@
 
 def last_kernel(
     next_, factor, factor_south, factor_north, edges, inside, state, back_a, back_b, rate, damp, steep, centre, back, across,
-    out, grad, rims, low, high, ghosts, lam, cells, sems,
+    out, grad, rims, low, high, ghosts, lam, cells, winds, sems,
 ):
     sub = sublane()
     zero = jnp.zeros((SUB, W), F32)
@@ -894,8 +894,10 @@
     tend0[-1] = tend0[-1] + ghosts[0, NF + 2 : NF + 3, lanes(1)]
     tend0[4] = tend0[4] + ghosts[1, NF + 2 : NF + 3, lanes(0)]
     for r in range(ROWS):
-        grad[0:1, lanes(r)] = grad0[r]
-        grad[1:2, lanes(r)] = state[GRAD1 : GRAD1 + 1, column(r)]
+        winds[0:1, lanes(r)] = grad0[r]
+        winds[1:2, lanes(r)] = state[GRAD1 : GRAD1 + 1, column(r)]
+    sent = pltpu.make_async_copy(winds, grad, sems.at[CHUNKS])
+    sent.start()
     tend0 = {r: full(value) for r, value in tend0.items()}
 
     def second(group, carry):
@@ -935,13 +937,14 @@
         here = pl.ds(c * each, each)
         copies.append(pltpu.make_async_copy(cells.at[here], out.at[here], sems.at[c]))
         copies[c].start()
+    sent.wait()
     for copy in copies:
         copy.wait()
 
 
 def last(next_, factor, factor_south, factor_north, edges, inside, state, back_a, back_b, coefficients):
     inputs = [(value, True) for value in (next_, factor, factor_south, factor_north, edges, inside, state)]
-    inputs += [(back_a, False), (back_b, False)]
+    inputs += [(back_a, True), (back_b, True)]
     inputs += [(value, True) for value in coefficients]
     return call(
         last_kernel,
@@ -955,9 +958,10 @@
             pltpu.VMEM((2, NF + 4, 2 * W), F32),
             pltpu.VMEM((GROUPS, SUB, ROWS * W), F32),
             pltpu.VMEM(CELLS, F32),
-            pltpu.SemaphoreType.DMA((CHUNKS,)),
+            pltpu.VMEM((2, ROWS * W), F32),
+            pltpu.SemaphoreType.DMA((CHUNKS + 1,)),
         ],
-        out_away=(0,),
+        out_away=(0, 1),
     )
 
 

time: 37.5 us -> 36.9 us (0.984)
  Pallas kernels: 15.4 us -> 13.7 us
  starting transfers between devices: 8.3 us -> 8.97 us
  blocking collectives: 11.2 us -> 11.7 us
    pallas_call x7, Pallas kernels: 15.4 us -> 13.7 us  [call(): pl.pallas_call(kernel, in_specs=specs, out_specs=[whole(pl.ANY if place i...]
    ppermute x1, starting transfers between devices: 3.67 us -> 4.34 us  [body(): back_b = lax.ppermute(send_b, 'geo', far)]
    all_to_all x1, blocking collectives: 11.2 us -> 11.7 us  [body(): lax.all_to_all(slots, 'geo', split_axis=0, concat_axis=0, tiled=True)]
  transfers between devices with their start and end apart: 4 -> 4, of which waited for: 2 -> 2; matrix products, arithmetic and copies ran while one was open for 0% -> 0% of each run, Pallas kernels for 16% -> 13%
where the time goes in v7:
time: 36.9 us; the launch traced here: 36.6 us
  Pallas kernels  13.7 us (37%)
  blocking collectives  11.7 us (32%)
  starting transfers between devices  8.97 us (24%)
  waiting for transfers between devices  1.21 us (3%)
  between operations  0.92 us (2%)
    pallas_call x7, Pallas kernels, call(): pl.pallas_call(kernel, in_specs=specs, out_specs=[whole(pl.ANY if place i...  13.7 us
    all_to_all x1, blocking collectives, body(): lax.all_to_all(slots, 'geo', split_axis=0, concat_axis=0, tiled=True)  11.7 us
    ppermute x1, starting transfers between devices, body(): from_far = lax.ppermute(far_rows(field, sea, wind_forcing), 'geo', far)  4.49 us
    ppermute x1, starting transfers between devices, body(): back_b = lax.ppermute(send_b, 'geo', far)  4.34 us
  transfers between devices with their start and end apart: 4, of which 2 were waited for; matrix products, arithmetic and copies ran while one was open for 0% of the time, Pallas kernels for 13%

profile of v7, /device:TPU:1, one launch (start us, length us, event | category | flops | bytes accessed | tf_op | source)
XLA Modules:
  0.0 36.6 jit_solution(3570947100319405376)
XLA Ops:
  0.6 0.0 copy-start.1
  0.6 0.0 copy-start.3
  0.7 0.0 copy-start
  0.7 0.0 copy-start.9
  0.7 0.0 copy-start.10
  0.7 0.0 copy-start.11
  0.7 0.0 copy-start.5
  0.7 0.0 copy-start.2
  0.7 1.5 %far.1 = f32[656,256]{1,0:T(8,128)S(1)} custom-call(f32[18,72,512]{2,1,0:T(8,128)} %bitcast.9, s32[1,512]{1,0:T(1,128)} %bitcast.14, f32[2,512]{1,0:T(2,128)} %wind_in.1), custom_call_target="tpu_custom_call" | custom-call | tf_op jit(solution)/shard_map/far/pallas_call | solution.py:148
  2.3 4.5 %collective-permute-start = (f32[656,256]{1,0:T(8,128)S(1)}, f32[656,256]{1,0:T(8,128)S(1)}, u32[]{:S(2)}, u32[]{:S(2)}) collective-permute-start(f32[656,256]{1,0:T(8,128)S(1)} %far.1), channel_id=1, source_target_pairs={{1,2},{2,1},{3,4},{4,3},{5,6},{6,5},{7,8},{8,7},{9,10},{10,9},{11,... | collective-permute-start | bytes 2015240 | tf_op jit(solution)/shard_map/ppermute | solution.py:994
  6.8 0.0 copy-done.9
  6.8 0.0 copy-done.10
  6.8 0.0 copy-done.11
  6.8 0.0 copy-done.1
  6.8 0.0 copy-done.3
  6.8 0.0 copy-done
  6.9 0.0 copy-done.5
  6.9 0.0 copy-start.4
  6.9 0.0 copy-start.6
  6.9 0.0 copy-start.7
  6.9 0.0 copy-start.8
  6.9 2.0 %local.1 = (f32[18,72,512]{2,1,0:T(8,128)S(1)}, f32[1296,128]{1,0:T(8,128)S(1)}, f32[1296,128]{1,0:T(8,128)S(1)}, f32[1296,128]{1,0:T(8,128)S(1)}, f32[1296,128]...) custom-call(f32[18,72,512]{2,1,0:T(8,128)S(1)} %bitcast.10, ...), custom_call_target="tpu_custom_call" | custom-call | tf_op jit(solution)/shard_map/local/pallas_call | solution.py:148
  8.9 0.0 copy-done.2
  8.9 0.1 near.1.refs_14_
  9.0 0.1 collective-permute-start.1
  9.1 0.0 copy-done.4
  9.1 0.0 copy-done.6
  9.1 0.0 copy-done.7
  9.1 0.0 copy-done.8
  9.1 1.5 %middle.1 = (f32[18,72,512]{2,1,0:T(8,128)S(1)}, f32[18,72,512]{2,1,0:T(8,128)S(1)}, f32[18,72,512]{2,1,0:T(8,128)S(1)}, f32[16,1024]{1,0:T(8,128)S(1)}, f32[128,128]{1,0:T(8,128)S(1)}) custom-call(f32[18,72,512]{2,1,0:T(8,128)S(1)} %get-tuple-element.32.refs_0_, ...), custom_call_target="tpu_custom_call", output_to_operand_aliasing={{0}: (0, {})} | custom-call | tf_op jit(solution)/shard_map/middle/pallas_call | solution.py:148
  10.6 11.7 %all_to_all.11 = f32[16,8,128]{2,1,0:T(8,128)S(1)} all-to-all(f32[16,8,128]{2,1,0:T(8,128)S(1)} %bitcast.13), channel_id=1, replica_groups=mesh['groups'=2,'geo'=16] {'geo'}, dimensions={0} | all-to-all | bytes 131072 | tf_op jit(solution)/shard_map/all_to_all | solution.py:1010
  22.3 0.0 collective-permute-done.refs_3_
  22.3 0.0 collective-permute-done.1.refs_4_
  22.3 4.4 %late.1 = (f32[18,72,512]{2,1,0:T(8,128)S(1)}, f32[18,72,512]{2,1,0:T(8,128)S(1)}, f32[18,72,512]{2,1,0:T(8,128)S(1)}, f32[18,72,128]{2,1,0:T(8,128)S(1)}, f32[1...) custom-call(f32[18,72,512]{2,1,0:T(8,128)S(1)} %get-tuple-element.40, ...), custom_call_target="tpu_custom_call", output_to_operand_aliasing={{0}: (0, {}), {1}: (1, {}), {2}: (2, {})} | custom-call | tf_op jit(solution)/shard_map/late/pallas_call | solution.py:148
  26.8 4.3 %collective-permute-start.3 = (f32[40,256]{1,0:T(8,128)S(1)}, f32[40,256]{1,0:T(8,128)S(1)}, u32[]{:S(2)}, u32[]{:S(2)}) collective-permute-start(f32[40,256]{1,0:T(8,128)S(1)} %get-tuple-element.59), channel_id=1, source_target_pairs={{1,2},{2,1},{3,4},{4,3},{5,6},{6,5},{7,8},{8,7},{9,10},{10,9},{11,... | collective-permute-start | bytes 122888 | tf_op jit(solution)/shard_map/ppermute | solution.py:1015
  31.1 1.0 %inner.1 = (f32[18,72,256]{2,1,0:T(8,128)S(1)}, f32[18,72,128]{2,1,0:T(8,128)S(1)}, f32[18,72,128]{2,1,0:T(8,128)S(1)}, f32[16,1024]{1,0:T(8,128)S(1)}, f32[40,256]{1,0:T(8,128)S(1)}) custom-call(f32[18,72,512]{2,1,0:T(8,128)S(1)} %get-tuple-element.46.next_, f32[18,72,128]{2,1,0:T(8,128)S(1)} %get-tuple-element.48.next_south, ...), custom_call_target="tpu_custom_call" | custom-call | flops 4194304 | bytes 4194304 | tf_op jit(solution)/shard_map/inner/pallas_call | solution.py:148
  32.2 0.1 collective-permute-start.2
  32.2 0.5 %collective-permute-done.3.back_b = f32[40,256]{1,0:T(8,128)S(1)} collective-permute-done((f32[40,256]{1,0:T(8,128)S(1)}, f32[40,256]{1,0:T(8,128)S(1)}, u32[]{:S(2)}, u32[]{:S(2)}) %collective-permute-start.3) | collective-permute-done | bytes 40992 | tf_op jit(solution)/shard_map/ppermute | solution.py:1015
  32.8 0.7 %collective-permute-done.2.back_a = f32[40,256]{1,0:T(8,128)S(1)} collective-permute-done((f32[40,256]{1,0:T(8,128)S(1)}, f32[40,256]{1,0:T(8,128)S(1)}, u32[]{:S(2)}, u32[]{:S(2)}) %collective-permute-start.2) | collective-permute-done | bytes 40992 | tf_op jit(solution)/shard_map/ppermute | solution.py:1019
  33.4 3.1 %last.1 = (f32[18,72,512]{2,1,0:T(8,128)}, f32[2,512]{1,0:T(2,128)}) custom-call(f32[18,72,512]{2,1,0:T(8,128)S(1)} %get-tuple-element.46.next_, f32[18,72,512]{2,1,0:T(8,128)S(1)} %get-tuple-element.47.factor, f32[18,72,128]{2,1,0:T(8,128)S(1)} %get-tuple-element.53.factor_south, f32[18,72,128]{2,1,0:T(8,128)S(1)} %get-tuple-element.54.factor_north, ...), custom_call_target="tpu_custom_call" | custom-call | tf_op jit(solution)/shard_map/last/pallas_call | solution.py:148
  (3 shorter events, 0.0 us)
Async XLA Ops:
  0.6 6.2 %copy-start.1 = (f32[4,72,128]{2,1,0:T(8,128)S(1)}, f32[4,72,128]{2,1,0:T(8,128)}, u32[]{:S(2)}) copy-start(f32[4,72,128]{2,1,0:T(8,128)} %constant.2.clone.table) | copy-start | bytes 442372
  0.6 6.2 %copy-start.3 = (s32[512]{0:T(512)S(1)}, s32[512]{0:T(512)}, u32[]{:S(2)}) copy-start(s32[512]{0:T(512)} %param.14) | copy-start | bytes 6148
  0.7 6.2 %copy-start = (f32[1296,512]{1,0:T(8,128)S(1)}, f32[1296,512]{1,0:T(8,128)}, u32[]{:S(2)}) copy-start(f32[1296,512]{1,0:T(8,128)} %param.12) | copy-start | bytes 7962628
  0.7 6.1 %copy-start.9 = (f32[1296]{0:T(1024)S(1)}, f32[1296]{0:T(1024)}, u32[]{:S(2)}) copy-start(f32[1296]{0:T(1024)} %param.16) | copy-start | bytes 15556
  0.7 6.1 %copy-start.10 = (f32[1296]{0:T(1024)S(1)}, f32[1296]{0:T(1024)}, u32[]{:S(2)}) copy-start(f32[1296]{0:T(1024)} %param.17) | copy-start | bytes 15556
  0.7 6.1 %copy-start.11 = (f32[1296]{0:T(1024)S(1)}, f32[1296]{0:T(1024)}, u32[]{:S(2)}) copy-start(f32[1296]{0:T(1024)} %param.18) | copy-start | bytes 15556
  0.7 6.2 %copy-start.5 = (f32[36]{0:T(128)S(1)}, f32[36]{0:T(128)}, u32[]{:S(2)}) copy-start(f32[36]{0:T(128)} %courant.1) | copy-start | bytes 436
  0.7 8.2 %copy-start.2 = (f32[2,512]{1,0:T(2,128)S(1)}, f32[2,512]{1,0:T(2,128)}, u32[]{:S(2)}) copy-start(f32[2,512]{1,0:T(2,128)} %wind_in.1) | copy-start | bytes 12292
  2.3 20.1 %collective-permute-start = (f32[656,256]{1,0:T(8,128)S(1)}, f32[656,256]{1,0:T(8,128)S(1)}, u32[]{:S(2)}, u32[]{:S(2)}) collective-permute-start(f32[656,256]{1,0:T(8,128)S(1)} %far.1), channel_id=1, source_target_pairs={{1,2},{2,1},{3,4},{4,3},{5,6},{6,5},{7,8},{8,7},{9,10},{10,9},{11,... | collective-permute-start | bytes 2015240 | tf_op jit(solution)/shard_map/ppermute | solution.py:994
  6.9 2.2 %copy-start.4 = (f32[128,36]{0,1:T(8,128)S(1)}, f32[128,36]{0,1:T(8,128)}, u32[]{:S(2)}) copy-start(f32[128,36]{0,1:T(8,128)} %param.21) | copy-start | bytes 55300
  6.9 2.2 %copy-start.6 = (s32[128,1]{0,1:T(1,128)S(1)}, s32[128,1]{0,1:T(1,128)}, u32[]{:S(2)}) copy-start(s32[128,1]{0,1:T(1,128)} %param.19) | copy-start | bytes 1540
  6.9 2.2 %copy-start.7 = (s32[128]{0:T(128)S(1)}, s32[128]{0:T(128)}, u32[]{:S(2)}) copy-start(s32[128]{0:T(128)} %param.20) | copy-start | bytes 1540
  6.9 2.2 %copy-start.8 = (f32[128]{0:T(128)S(1)}, f32[128]{0:T(128)}, u32[]{:S(2)}) copy-start(f32[128]{0:T(128)} %param.22) | copy-start | bytes 1540
  9.0 13.3 %collective-permute-start.1 = (f32[656,256]{1,0:T(8,128)S(1)}, f32[656,256]{1,0:T(8,128)S(1)}, u32[]{:S(2)}, u32[]{:S(2)}) collective-permute-start(f32[656,256]{1,0:T(8,128)S(1)} %near.1.refs_14_), channel_id=1, source_target_pairs={{0,1},{1,0},{2,3},{3,2},{4,5},{5,4},{6,7},{7,6},{8,9},{9,8},{10,11... | collective-permute-start | bytes 2015240 | tf_op jit(solution)/shard_map/ppermute | solution.py:1005
  26.8 6.0 %collective-permute-start.3 = (f32[40,256]{1,0:T(8,128)S(1)}, f32[40,256]{1,0:T(8,128)S(1)}, u32[]{:S(2)}, u32[]{:S(2)}) collective-permute-start(f32[40,256]{1,0:T(8,128)S(1)} %get-tuple-element.59), channel_id=1, source_target_pairs={{1,2},{2,1},{3,4},{4,3},{5,6},{6,5},{7,8},{8,7},{9,10},{10,9},{11,... | collective-permute-start | bytes 122888 | tf_op jit(solution)/shard_map/ppermute | solution.py:1015
  32.2 1.3 %collective-permute-start.2 = (f32[40,256]{1,0:T(8,128)S(1)}, f32[40,256]{1,0:T(8,128)S(1)}, u32[]{:S(2)}, u32[]{:S(2)}) collective-permute-start(f32[40,256]{1,0:T(8,128)S(1)} %get-tuple-element.58), channel_id=1, source_target_pairs={{0,1},{1,0},{2,3},{3,2},{4,5},{5,4},{6,7},{7,6},{8,9},{9,8},{10,11... | collective-permute-start | bytes 122888 | tf_op jit(solution)/shard_map/ppermute | solution.py:1019

commit v8 on v7

--- a/solution.py
+++ b/solution.py
@@ -32,6 +32,8 @@
 HALF = NB // 2
 HALO = (HALF + SUB, 2 * W)
 LOAD = 40
+LINES_A = NF + 4
+LINES_B = NF + 12
 STATE = (16, 8 * W)
 STEEP0, WIND0, WIND1, SEA, STEEP1, TEND1, GRAD1, TEND0, GRAD0, PASS0 = range(10)
 
@@ -201,7 +203,7 @@
 
 def far_kernel(field, sea_in, wind_in, out, cells, sea, wind, sems):
     even = lax.rem(lax.axis_index("geo"), 2) == 0
-    each = GROUPS // 3
+    each = GROUPS
     small = [
         pltpu.make_async_copy(sea_in, sea, sems.at[6]),
         pltpu.make_async_copy(wind_in, wind, sems.at[7]),
@@ -209,7 +211,7 @@
 
     def bring(first, lane):
         copies = []
-        for c in range(3):
+        for c in range(1):
             for run in range(2):
                 here, rows = pl.ds(c * each, each), pl.ds((first + 4 * run) * SUB, 3 * SUB)
                 copies.append(
@@ -234,7 +236,7 @@
         copy.start()
     for copy in small:
         copy.wait()
-    for c in range(3):
+    for c in range(1):
         copies[2 * c].wait()
         copies[2 * c + 1].wait()
 
@@ -748,6 +750,8 @@
     here = pl.ds((base + 2) * W, 2 * W)
     for place, name in enumerate((STEEP1, TEND1, TEND0, TEND0)):
         ref[NF + place : NF + place + 1, :] = state[name : name + 1, here]
+    if ref.shape[0] > NF + 4:
+        ref[NF + 4 :, :] = jnp.zeros((ref.shape[0] - NF - 4, 2 * W), F32)
 
 
 def late(next_, factor, moved, from_far, from_near, arrived, own, state, coefficients, ranks, rows):
@@ -759,7 +763,7 @@
         kernel,
         "late",
         [(value, True) for value in inputs],
-        [(CELLS, True)] * 3 + [(EDGE, True)] * 2 + [(EDGES, True), (STATE, True), ((NF + 4, 2 * W), False)]
+        [(CELLS, True)] * 3 + [(EDGE, True)] * 2 + [(EDGES, True), (STATE, True), ((LINES_B, 2 * W), False)]
         + [((GROUPS, SUB, ROWS * W), True)],
         [
             pltpu.VMEM(CELLS, F32),
@@ -771,23 +775,29 @@
     )
 
 
+def hand_kernel(lam, state, send):
+    even = lax.rem(lax.axis_index("geo"), 2) == 0
+
+    @pl.when(even)
+    def _():
+        fill(send, lam, state, 2)
+
+    @pl.when(jnp.logical_not(even))
+    def _():
+        fill(send, lam, state, 0)
+
+
+def hand(lam, state):
+    return call(hand_kernel, "hand", [(lam, True), (state, True)], [((LINES_A, 2 * W), False)])[0]
+
+
 def inner_kernel(
-    next_, next_south, next_north, source, state_in, lam, rate, damp, centre, back, across,
-    inside, factor_south, factor_north, state, send_a,
+    next_, next_south, next_north, source, state_in, rate, damp, centre, back, across,
+    inside, factor_south, factor_north, state,
 ):
     sub = sublane()
     zero = jnp.zeros((SUB, W), F32)
     state[...] = state_in[...]
-    even = lax.rem(lax.axis_index("geo"), 2) == 0
-
-    @pl.when(even)
-    def _():
-        fill(send_a, lam, state, 2)
-
-    @pl.when(jnp.logical_not(even))
-    def _():
-        fill(send_a, lam, state, 0)
-
     wind0 = {r: full(state[WIND0 : WIND0 + 1, column(r)]) for r in (-1, 4)}
     steep0 = {r: full(state[STEEP0 : STEEP0 + 1, column(r)]) for r in (-1, 4)}
 
@@ -831,7 +841,7 @@
         inner_kernel,
         "inner",
         [(arg, True) for arg in args],
-        [(EDGES, True), (EDGE, True), (EDGE, True), (STATE, True), ((NF + 4, 2 * W), False)],
+        [(EDGES, True), (EDGE, True), (EDGE, True), (STATE, True)],
         cost=1 << 22,
     )
 
@@ -843,8 +853,9 @@
     sub = sublane()
     zero = jnp.zeros((SUB, W), F32)
     even = lax.rem(lax.axis_index("geo"), 2) == 0
-    ghosts[0] = jnp.where(even, back_b[...], back_a[...])
-    ghosts[1] = jnp.where(even, back_a[...], back_b[...])
+    first_b, first_a = back_b[0 : NF + 4, :], back_a[0 : NF + 4, :]
+    ghosts[0] = jnp.where(even, first_b, first_a)
+    ghosts[1] = jnp.where(even, first_a, first_b)
     for group in range(GROUPS):
         for where in range(2):
             for row in range(2):
@@ -1013,10 +1024,10 @@
         (rate, damp, steep, centre, ahead, back, across), count, held,
     )
     back_b = lax.ppermute(send_b, "geo", far)
-    inside, factor_south, factor_north, state, send_a = inner(
-        next_, next_south, next_north, source, state, lam, rate, damp, centre, back, across
-    )
-    back_a = lax.ppermute(send_a, "geo", near)
+    back_a = lax.ppermute(hand(lam, state), "geo", near)
+    inside, factor_south, factor_north, state = inner(
+        next_, next_south, next_north, source, state, rate, damp, centre, back, across
+    )
     out, grad = last(
         next_, factor, factor_south, factor_north, edges, inside, state, back_a, back_b,
         (rate, damp, steep, centre, back, across),

time: 36.9 us -> 36.4 us (0.986)
  waiting for transfers between devices: 1.21 us -> 0.64 us
    ppermute x1, waiting for transfers between devices: 0.66 us -> 0.21 us  [body(): back_a = lax.ppermute(hand(lam, state), 'geo', near)]
    pallas_call x7 -> x8, Pallas kernels: 13.7 us -> 13.6 us  [call(): pl.pallas_call(kernel, in_specs=specs, out_specs=[whole(pl.ANY if place i...]
where the time goes in v8:
time: 36.4 us; the launch traced here: 35.9 us
  Pallas kernels  13.6 us (37%)
  blocking collectives  11.7 us (32%)
  starting transfers between devices  8.99 us (25%)
  between operations  0.92 us (3%)
  waiting for transfers between devices  0.64 us (2%)
    pallas_call x8, Pallas kernels, call(): pl.pallas_call(kernel, in_specs=specs, out_specs=[whole(pl.ANY if place i...  13.6 us
    all_to_all x1, blocking collectives, body(): lax.all_to_all(slots, 'geo', split_axis=0, concat_axis=0, tiled=True)  11.7 us
    ppermute x1, starting transfers between devices, body(): from_far = lax.ppermute(far_rows(field, sea, wind_forcing), 'geo', far)  4.5 us
    ppermute x1, starting transfers between devices, body(): back_b = lax.ppermute(send_b, 'geo', far)  4.35 us
  transfers between devices with their start and end apart: 4, of which 2 were waited for; matrix products, arithmetic and copies ran while one was open for 0% of the time, Pallas kernels for 13%

profile of v8, /device:TPU:1, one launch (start us, length us, event | category | flops | bytes accessed | tf_op | source)
XLA Modules:
  0.0 35.9 jit_solution(8969734392057350970)
XLA Ops:
  0.6 0.0 copy-start.1
  0.6 0.0 copy-start.3
  0.7 0.0 copy-start
  0.7 0.0 copy-start.9
  0.7 0.0 copy-start.10
  0.7 0.0 copy-start.11
  0.7 0.0 copy-start.5
  0.7 0.0 copy-start.2
  0.7 1.5 %far.1 = f32[656,256]{1,0:T(8,128)S(1)} custom-call(f32[18,72,512]{2,1,0:T(8,128)} %bitcast.9, s32[1,512]{1,0:T(1,128)} %bitcast.14, f32[2,512]{1,0:T(2,128)} %wind_in.1), custom_call_target="tpu_custom_call" | custom-call | tf_op jit(solution)/shard_map/far/pallas_call | solution.py:150
  2.2 4.5 %collective-permute-start = (f32[656,256]{1,0:T(8,128)S(1)}, f32[656,256]{1,0:T(8,128)S(1)}, u32[]{:S(2)}, u32[]{:S(2)}) collective-permute-start(f32[656,256]{1,0:T(8,128)S(1)} %far.1), channel_id=1, source_target_pairs={{1,2},{2,1},{3,4},{4,3},{5,6},{6,5},{7,8},{8,7},{9,10},{10,9},{11,... | collective-permute-start | bytes 2015240 | tf_op jit(solution)/shard_map/ppermute | solution.py:1005
  6.7 0.0 copy-done.9
  6.7 0.0 copy-done.10
  6.7 0.0 copy-done.11
  6.8 0.0 copy-done.1
  6.8 0.0 copy-done.3
  6.8 0.0 copy-done
  6.8 0.0 copy-done.5
  6.8 0.0 copy-start.4
  6.8 0.0 copy-start.6
  6.8 0.0 copy-start.7
  6.8 0.0 copy-start.8
  6.9 2.0 %local.1 = (f32[18,72,512]{2,1,0:T(8,128)S(1)}, f32[1296,128]{1,0:T(8,128)S(1)}, f32[1296,128]{1,0:T(8,128)S(1)}, f32[1296,128]{1,0:T(8,128)S(1)}, f32[1296,128]...) custom-call(f32[18,72,512]{2,1,0:T(8,128)S(1)} %bitcast.10, ...), custom_call_target="tpu_custom_call" | custom-call | tf_op jit(solution)/shard_map/local/pallas_call | solution.py:150
  8.9 0.0 copy-done.2
  8.9 0.1 near.1.refs_14_
  9.0 0.1 collective-permute-start.1
  9.0 0.0 copy-done.4
  9.0 0.0 copy-done.6
  9.1 0.0 copy-done.7
  9.1 0.0 copy-done.8
  9.1 1.5 %middle.1 = (f32[18,72,512]{2,1,0:T(8,128)S(1)}, f32[18,72,512]{2,1,0:T(8,128)S(1)}, f32[18,72,512]{2,1,0:T(8,128)S(1)}, f32[16,1024]{1,0:T(8,128)S(1)}, f32[128,128]{1,0:T(8,128)S(1)}) custom-call(f32[18,72,512]{2,1,0:T(8,128)S(1)} %get-tuple-element.31.refs_0_, ...), custom_call_target="tpu_custom_call", output_to_operand_aliasing={{0}: (0, {})} | custom-call | tf_op jit(solution)/shard_map/middle/pallas_call | solution.py:150
  10.6 11.7 %all_to_all.11 = f32[16,8,128]{2,1,0:T(8,128)S(1)} all-to-all(f32[16,8,128]{2,1,0:T(8,128)S(1)} %bitcast.13), channel_id=1, replica_groups=mesh['groups'=2,'geo'=16] {'geo'}, dimensions={0} | all-to-all | bytes 131072 | tf_op jit(solution)/shard_map/all_to_all | solution.py:1021
  22.3 0.0 collective-permute-done.refs_3_
  22.3 0.0 collective-permute-done.1.refs_4_
  22.3 4.4 %late.1 = (f32[18,72,512]{2,1,0:T(8,128)S(1)}, f32[18,72,512]{2,1,0:T(8,128)S(1)}, f32[18,72,512]{2,1,0:T(8,128)S(1)}, f32[18,72,128]{2,1,0:T(8,128)S(1)}, f32[1...) custom-call(f32[18,72,512]{2,1,0:T(8,128)S(1)} %get-tuple-element.39, ...), custom_call_target="tpu_custom_call", output_to_operand_aliasing={{0}: (0, {}), {1}: (1, {}), {2}: (2, {})} | custom-call | tf_op jit(solution)/shard_map/late/pallas_call | solution.py:150
  26.7 4.3 %collective-permute-start.3 = (f32[48,256]{1,0:T(8,128)S(1)}, f32[48,256]{1,0:T(8,128)S(1)}, u32[]{:S(2)}, u32[]{:S(2)}) collective-permute-start(f32[48,256]{1,0:T(8,128)S(1)} %get-tuple-element.57), channel_id=1, source_target_pairs={{1,2},{2,1},{3,4},{4,3},{5,6},{6,5},{7,8},{8,7},{9,10},{10,9},{11,... | collective-permute-start | bytes 147464 | tf_op jit(solution)/shard_map/ppermute | solution.py:1026
  31.1 0.1 collective-permute-start.2
  31.2 1.0 %inner.1 = (f32[18,72,256]{2,1,0:T(8,128)S(1)}, f32[18,72,128]{2,1,0:T(8,128)S(1)}, f32[18,72,128]{2,1,0:T(8,128)S(1)}, f32[16,1024]{1,0:T(8,128)S(1)}) custom-call(f32[18,72,512]{2,1,0:T(8,128)S(1)} %get-tuple-element.45.next_, f32[18,72,128]{2,1,0:T(8,128)S(1)} %get-tuple-element.47.next_south, f32[18,72,128]{2,1,0:T(8,128)S(1)} %get-tuple-element.48.next_north, ...), custom_call_target="tpu_custom_call" | custom-call | flops 4194304 | bytes 4194304 | tf_op jit(solution)/shard_map/inner/pallas_call | solution.py:150
  32.2 0.2 collective-permute-done.2.back_a
  32.4 0.4 %collective-permute-done.3.back_b = f32[48,256]{1,0:T(8,128)S(1)} collective-permute-done((f32[48,256]{1,0:T(8,128)S(1)}, f32[48,256]{1,0:T(8,128)S(1)}, u32[]{:S(2)}, u32[]{:S(2)}) %collective-permute-start.3) | collective-permute-done | bytes 49184 | tf_op jit(solution)/shard_map/ppermute | solution.py:1026
  32.8 3.1 %last.1 = (f32[18,72,512]{2,1,0:T(8,128)}, f32[2,512]{1,0:T(2,128)}) custom-call(f32[18,72,512]{2,1,0:T(8,128)S(1)} %get-tuple-element.45.next_, f32[18,72,512]{2,1,0:T(8,128)S(1)} %get-tuple-element.46.factor, f32[18,72,128]{2,1,0:T(8,128)S(1)} %get-tuple-element.51.factor_south, f32[18,72,128]{2,1,0:T(8,128)S(1)} %get-tuple-element.52.factor_north, ...), custom_call_target="tpu_custom_call" | custom-call | tf_op jit(solution)/shard_map/last/pallas_call | solution.py:150
  (4 shorter events, 0.1 us)
Async XLA Ops:
  0.6 6.1 %copy-start.1 = (f32[4,72,128]{2,1,0:T(8,128)S(1)}, f32[4,72,128]{2,1,0:T(8,128)}, u32[]{:S(2)}) copy-start(f32[4,72,128]{2,1,0:T(8,128)} %constant.2.clone.table) | copy-start | bytes 442372
  0.6 6.1 %copy-start.3 = (s32[512]{0:T(512)S(1)}, s32[512]{0:T(512)}, u32[]{:S(2)}) copy-start(s32[512]{0:T(512)} %param.14) | copy-start | bytes 6148
  0.7 6.1 %copy-start = (f32[1296,512]{1,0:T(8,128)S(1)}, f32[1296,512]{1,0:T(8,128)}, u32[]{:S(2)}) copy-start(f32[1296,512]{1,0:T(8,128)} %param.12) | copy-start | bytes 7962628
  0.7 6.0 %copy-start.9 = (f32[1296]{0:T(1024)S(1)}, f32[1296]{0:T(1024)}, u32[]{:S(2)}) copy-start(f32[1296]{0:T(1024)} %param.16) | copy-start | bytes 15556
  0.7 6.0 %copy-start.10 = (f32[1296]{0:T(1024)S(1)}, f32[1296]{0:T(1024)}, u32[]{:S(2)}) copy-start(f32[1296]{0:T(1024)} %param.17) | copy-start | bytes 15556
  0.7 6.1 %copy-start.11 = (f32[1296]{0:T(1024)S(1)}, f32[1296]{0:T(1024)}, u32[]{:S(2)}) copy-start(f32[1296]{0:T(1024)} %param.18) | copy-start | bytes 15556
  0.7 6.1 %copy-start.5 = (f32[36]{0:T(128)S(1)}, f32[36]{0:T(128)}, u32[]{:S(2)}) copy-start(f32[36]{0:T(128)} %courant.1) | copy-start | bytes 436
  0.7 8.2 %copy-start.2 = (f32[2,512]{1,0:T(2,128)S(1)}, f32[2,512]{1,0:T(2,128)}, u32[]{:S(2)}) copy-start(f32[2,512]{1,0:T(2,128)} %wind_in.1) | copy-start | bytes 12292
  2.2 20.1 %collective-permute-start = (f32[656,256]{1,0:T(8,128)S(1)}, f32[656,256]{1,0:T(8,128)S(1)}, u32[]{:S(2)}, u32[]{:S(2)}) collective-permute-start(f32[656,256]{1,0:T(8,128)S(1)} %far.1), channel_id=1, source_target_pairs={{1,2},{2,1},{3,4},{4,3},{5,6},{6,5},{7,8},{8,7},{9,10},{10,9},{11,... | collective-permute-start | bytes 2015240 | tf_op jit(solution)/shard_map/ppermute | solution.py:1005
  6.8 2.2 %copy-start.4 = (f32[128,36]{0,1:T(8,128)S(1)}, f32[128,36]{0,1:T(8,128)}, u32[]{:S(2)}) copy-start(f32[128,36]{0,1:T(8,128)} %param.21) | copy-start | bytes 55300
  6.8 2.2 %copy-start.6 = (s32[128,1]{0,1:T(1,128)S(1)}, s32[128,1]{0,1:T(1,128)}, u32[]{:S(2)}) copy-start(s32[128,1]{0,1:T(1,128)} %param.19) | copy-start | bytes 1540
  6.8 2.2 %copy-start.7 = (s32[128]{0:T(128)S(1)}, s32[128]{0:T(128)}, u32[]{:S(2)}) copy-start(s32[128]{0:T(128)} %param.20) | copy-start | bytes 1540
  6.8 2.2 %copy-start.8 = (f32[128]{0:T(128)S(1)}, f32[128]{0:T(128)}, u32[]{:S(2)}) copy-start(f32[128]{0:T(128)} %param.22) | copy-start | bytes 1540
  9.0 13.3 %collective-permute-start.1 = (f32[656,256]{1,0:T(8,128)S(1)}, f32[656,256]{1,0:T(8,128)S(1)}, u32[]{:S(2)}, u32[]{:S(2)}) collective-permute-start(f32[656,256]{1,0:T(8,128)S(1)} %near.1.refs_14_), channel_id=1, source_target_pairs={{0,1},{1,0},{2,3},{3,2},{4,5},{5,4},{6,7},{7,6},{8,9},{9,8},{10,11... | collective-permute-start | bytes 2015240 | tf_op jit(solution)/shard_map/ppermute | solution.py:1016
  26.7 6.1 %collective-permute-start.3 = (f32[48,256]{1,0:T(8,128)S(1)}, f32[48,256]{1,0:T(8,128)S(1)}, u32[]{:S(2)}, u32[]{:S(2)}) collective-permute-start(f32[48,256]{1,0:T(8,128)S(1)} %get-tuple-element.57), channel_id=1, source_target_pairs={{1,2},{2,1},{3,4},{4,3},{5,6},{6,5},{7,8},{8,7},{9,10},{10,9},{11,... | collective-permute-start | bytes 147464 | tf_op jit(solution)/shard_map/ppermute | solution.py:1026
  31.1 1.3 %collective-permute-start.2 = (f32[40,256]{1,0:T(8,128)S(1)}, f32[40,256]{1,0:T(8,128)S(1)}, u32[]{:S(2)}, u32[]{:S(2)}) collective-permute-start(f32[40,256]{1,0:T(8,128)S(1)} %hand.1), channel_id=1, source_target_pairs={{0,1},{1,0},{2,3},{3,2},{4,5},{5,4},{6,7},{7,6},{8,9},{9,8},{10,11... | collective-permute-start | bytes 122888 | tf_op jit(solution)/shard_map/ppermute | solution.py:1027

commit v9 on v8

--- a/solution.py
+++ b/solution.py
@@ -791,13 +791,11 @@
     return call(hand_kernel, "hand", [(lam, True), (state, True)], [((LINES_A, 2 * W), False)])[0]
 
 
-def inner_kernel(
-    next_, next_south, next_north, source, state_in, rate, damp, centre, back, across,
-    inside, factor_south, factor_north, state,
+def rim_kernel(
+    next_south, next_north, source, state, rate, damp, across, factor_south, factor_north, beyond,
 ):
     sub = sublane()
     zero = jnp.zeros((SUB, W), F32)
-    state[...] = state_in[...]
     wind0 = {r: full(state[WIND0 : WIND0 + 1, column(r)]) for r in (-1, 4)}
     steep0 = {r: full(state[STEEP0 : STEEP0 + 1, column(r)]) for r in (-1, 4)}
 
@@ -810,6 +808,43 @@
                 factor_south[group, rows, :] = jnp.exp2(grow * wind0[-1] - fade * steep0[-1])
             if tile in NORTH:
                 factor_north[group, rows, :] = jnp.exp2(grow * wind0[4] - fade * steep0[4])
+            gone = fade * across[spot, :]
+            if tile in NORTH:
+                value = pick(tile, sub, source[group, rows, lanes(0)] * next_south[group, rows, :], None)
+                sums[0] = sums[0] + gone * value
+            if tile in SOUTH:
+                value = pick(tile, sub, None, source[group, rows, lanes(3)] * next_north[group, rows, :])
+                sums[1] = sums[1] + gone * value
+        return tuple(sums)
+
+    sums = loop(0, GROUPS, 6, step, (zero,) * 2)
+    beyond[...] = jnp.zeros_like(beyond)
+    for place in range(2):
+        beyond[0:1, lanes(place)] = total(sums[place]) * (-LN2)
+
+
+def rim(*args):
+    return call(
+        rim_kernel,
+        "rim",
+        [(arg, True) for arg in args],
+        [(EDGE, True), (EDGE, True), ((SUB, 2 * W), True)],
+        cost=1 << 24,
+    )
+
+
+def inner_kernel(
+    next_, factor, source, state_in, rate, damp, steep, centre, back, across, grown, part, state, inside,
+):
+    sub = sublane()
+    zero = jnp.zeros((SUB, W), F32)
+    state[...] = state_in[...]
+
+    def step(group, sums):
+        sums = list(sums)
+        for tile in range(TILES):
+            rows, spot = pl.ds(tile * SUB, SUB), bins(group, tile)
+            grow, fade = rate[spot, :], damp[spot, :]
             middle, along, over = centre[spot, :], back[spot, :], across[spot, :]
             cell = {r: source[group, rows, lanes(r)] for r in range(ROWS)}
             for place, r in enumerate((1, 2)):
@@ -819,21 +854,31 @@
                 value = value * next_[group, rows, lanes(r)]
                 sums[place] = sums[place] + grow * value
                 sums[2 + place] = sums[2 + place] + fade * value
-            gone = fade * over
-            if tile in NORTH:
-                value = pick(tile, sub, cell[0] * next_south[group, rows, :], None)
-                sums[4] = sums[4] + gone * value
-            if tile in SOUTH:
-                value = pick(tile, sub, None, cell[3] * next_north[group, rows, :])
-                sums[5] = sums[5] + gone * value
         return tuple(sums)
 
-    sums = loop(0, GROUPS, 6, step, (zero,) * 6)
+    sums = loop(0, GROUPS, 6, step, (zero,) * 4)
     for place, r in enumerate((1, 2)):
         state[GRAD0 : GRAD0 + 1, column(r)] = total(sums[place]) * LN2
         state[TEND0 : TEND0 + 1, column(r)] = total(sums[2 + place]) * (-LN2)
-    state[TEND0 : TEND0 + 1, column(-1)] = total(sums[4]) * (-LN2)
-    state[TEND0 : TEND0 + 1, column(4)] = total(sums[5]) * (-LN2)
+    tend0 = {r: full(state[TEND0 : TEND0 + 1, column(r)]) for r in (1, 2)}
+    sea = {r: full(state[SEA : SEA + 1, column(r)]) for r in (1, 2)}
+
+    def grow_back(group, carry):
+        for tile in range(TILES):
+            rows, spot = pl.ds(tile * SUB, SUB), bins(group, tile)
+            heavy = steep[spot, :]
+            middle, along, over = centre[spot, :], back[spot, :], across[spot, :]
+            cell = {}
+            for place, r in enumerate((1, 2)):
+                cell[r] = inside[group, rows, lanes(place)] * factor[group, rows, lanes(r)] + heavy * tend0[r]
+                grown[group, rows, lanes(place)] = cell[r]
+            met = {1: pick(tile, sub, over * cell[2], None), 2: pick(tile, sub, None, over * cell[1])}
+            for place, r in enumerate((1, 2)):
+                value = middle * cell[r] + along * side(tile, sub, cell[r], True)
+                part[group, rows, lanes(place)] = sea[r] * plus(value, met[r])
+        return carry
+
+    loop(0, GROUPS, 6, grow_back, 0)
 
 
 def inner(*args):
@@ -841,13 +886,15 @@
         inner_kernel,
         "inner",
         [(arg, True) for arg in args],
-        [(EDGES, True), (EDGE, True), (EDGE, True), (STATE, True)],
+        [(EDGES, True), (EDGES, True), (STATE, True)],
+        [pltpu.VMEM(EDGES, F32)],
         cost=1 << 22,
     )
 
 
 def last_kernel(
-    next_, factor, factor_south, factor_north, edges, inside, state, back_a, back_b, rate, damp, steep, centre, back, across,
+    next_, factor, factor_south, factor_north, edges, grown, part, beyond, state, back_a, back_b,
+    rate, damp, steep, centre, back, across,
     out, grad, rims, low, high, ghosts, lam, cells, winds, sems,
 ):
     sub = sublane()
@@ -898,12 +945,12 @@
 
     sums = loop(0, GROUPS, 6, first, (zero,) * 4)
     sums = [total(value) * LN2 for value in sums]
-    tend0 = {r: state[TEND0 : TEND0 + 1, column(r)] for r in range(-1, 5)}
+    tend0 = {r: state[TEND0 : TEND0 + 1, column(r)] for r in (0, 3)}
     grad0 = [state[GRAD0 : GRAD0 + 1, column(r)] for r in range(ROWS)]
     tend0[0], grad0[0] = tend0[0] - sums[2], grad0[0] + sums[0]
     tend0[3], grad0[3] = tend0[3] - sums[3], grad0[3] + sums[1]
-    tend0[-1] = tend0[-1] + ghosts[0, NF + 2 : NF + 3, lanes(1)]
-    tend0[4] = tend0[4] + ghosts[1, NF + 2 : NF + 3, lanes(0)]
+    tend0[-1] = beyond[0:1, lanes(0)] + ghosts[0, NF + 2 : NF + 3, lanes(1)]
+    tend0[4] = beyond[0:1, lanes(1)] + ghosts[1, NF + 2 : NF + 3, lanes(0)]
     for r in range(ROWS):
         winds[0:1, lanes(r)] = grad0[r]
         winds[1:2, lanes(r)] = state[GRAD1 : GRAD1 + 1, column(r)]
@@ -916,29 +963,23 @@
             rows, spot = pl.ds(tile * SUB, SUB), bins(group, tile)
             heavy = steep[spot, :]
             middle, along, over = centre[spot, :], back[spot, :], across[spot, :]
-            cell = {}
-            for r in range(-1, 5):
-                if r == -1:
-                    if tile not in SOUTH:
-                        continue
-                    value = low[group, rows, :] * factor_south[group, rows, :]
-                elif r == 4:
-                    if tile not in NORTH:
-                        continue
-                    value = high[group, rows, :] * factor_north[group, rows, :]
-                else:
-                    if r == 0:
-                        value = (rims if tile in SOUTH else edges)[group, rows, lanes(0)]
-                    elif r == 3:
-                        value = (rims if tile in NORTH else edges)[group, rows, lanes(1)]
-                    else:
-                        value = inside[group, rows, lanes(r - 1)]
-                    value = value * factor[group, rows, lanes(r)]
-                cell[r] = value + heavy * tend0[r]
-            for r in range(ROWS):
+            cell = {1: grown[group, rows, lanes(0)], 2: grown[group, rows, lanes(1)]}
+            for r, mine, ghost, gained in ((-1, SOUTH, low, factor_south), (4, NORTH, high, factor_north)):
+                if tile in mine:
+                    cell[r] = ghost[group, rows, :] * gained[group, rows, :] + heavy * tend0[r]
+            for r, place, mine in ((0, 0, SOUTH), (3, 1, NORTH)):
+                value = (rims if tile in mine else edges)[group, rows, lanes(place)]
+                cell[r] = value * factor[group, rows, lanes(r)] + heavy * tend0[r]
+            for r in (0, 3):
                 value = middle * cell[r] + along * side(tile, sub, cell[r], True)
                 value = value + over * pick(tile, sub, cell.get(r + 1), cell.get(r - 1))
                 cells[group, rows, lanes(r)] = sea[r] * value
+            met = {
+                1: pick(tile, sub, None, sea[1] * (over * cell[0])),
+                2: pick(tile, sub, sea[2] * (over * cell[3]), None),
+            }
+            for r in (1, 2):
+                cells[group, rows, lanes(r)] = plus(part[group, rows, lanes(r - 1)], met[r])
         return carry
 
     each = GROUPS // CHUNKS
@@ -953,8 +994,9 @@
         copy.wait()
 
 
-def last(next_, factor, factor_south, factor_north, edges, inside, state, back_a, back_b, coefficients):
-    inputs = [(value, True) for value in (next_, factor, factor_south, factor_north, edges, inside, state)]
+def last(next_, factor, factor_south, factor_north, edges, grown, part, beyond, state, back_a, back_b, coefficients):
+    inputs = (next_, factor, factor_south, factor_north, edges, grown, part, beyond, state)
+    inputs = [(value, True) for value in inputs]
     inputs += [(back_a, True), (back_b, True)]
     inputs += [(value, True) for value in coefficients]
     return call(
@@ -1025,11 +1067,10 @@
     )
     back_b = lax.ppermute(send_b, "geo", far)
     back_a = lax.ppermute(hand(lam, state), "geo", near)
-    inside, factor_south, factor_north, state = inner(
-        next_, next_south, next_north, source, state, rate, damp, centre, back, across
-    )
+    factor_south, factor_north, beyond = rim(next_south, next_north, source, state, rate, damp, across)
+    grown, part, state = inner(next_, factor, source, state, rate, damp, steep, centre, back, across)
     out, grad = last(
-        next_, factor, factor_south, factor_north, edges, inside, state, back_a, back_b,
+        next_, factor, factor_south, factor_north, edges, grown, part, beyond, state, back_a, back_b,
         (rate, damp, steep, centre, back, across),
     )
     return grad, out.reshape(NB, ROWS * W)

time: 36.4 us -> 36.6 us (level)
  waiting for transfers between devices: 0.64 us -> 0.01 us
  Pallas kernels: 13.6 us -> 14.2 us
    pallas_call x8 -> x9, Pallas kernels: 13.6 us -> 14.2 us  [call(): pl.pallas_call(kernel, in_specs=specs, out_specs=[whole(pl.ANY if place i...]
    ppermute x1, waiting for transfers between devices: 0.43 us -> 0.01 us  [body(): back_b = lax.ppermute(send_b, 'geo', far)]
  transfers between devices with their start and end apart: 4 -> 4, of which waited for: 2 -> 0; matrix products, arithmetic and copies ran while one was open for 0% -> 0% of each run, Pallas kernels for 13% -> 15%
where the time goes in v9:
time: 36.6 us; the launch traced here: 35.9 us
  Pallas kernels  14.2 us (39%)
  blocking collectives  11.7 us (32%)
  starting transfers between devices  8.98 us (25%)
  between operations  0.95 us (3%)
    pallas_call x9, Pallas kernels, call(): pl.pallas_call(kernel, in_specs=specs, out_specs=[whole(pl.ANY if place i...  14.2 us
    all_to_all x1, blocking collectives, body(): lax.all_to_all(slots, 'geo', split_axis=0, concat_axis=0, tiled=True)  11.7 us
    ppermute x1, starting transfers between devices, body(): from_far = lax.ppermute(far_rows(field, sea, wind_forcing), 'geo', far)  4.5 us
    ppermute x1, starting transfers between devices, body(): back_b = lax.ppermute(send_b, 'geo', far)  4.34 us
  transfers between devices with their start and end apart: 4, of which 0 were waited for; matrix products, arithmetic and copies ran while one was open for 0% of the time, Pallas kernels for 15%

profile of v9, /device:TPU:1, one launch (start us, length us, event | category | flops | bytes accessed | tf_op | source)
XLA Modules:
  0.0 35.9 jit_solution(701523870622230335)
XLA Ops:
  0.6 0.0 copy-start.1
  0.6 0.0 copy-start.3
  0.7 0.0 copy-start
  0.7 0.0 copy-start.9
  0.7 0.0 copy-start.10
  0.7 0.0 copy-start.11
  0.7 0.0 copy-start.5
  0.7 0.0 copy-start.2
  0.7 1.5 %far.1 = f32[656,256]{1,0:T(8,128)S(1)} custom-call(f32[18,72,512]{2,1,0:T(8,128)} %bitcast.9, s32[1,512]{1,0:T(1,128)} %bitcast.14, f32[2,512]{1,0:T(2,128)} %wind_in.1), custom_call_target="tpu_custom_call" | custom-call | tf_op jit(solution)/shard_map/far/pallas_call | solution.py:150
  2.2 4.5 %collective-permute-start = (f32[656,256]{1,0:T(8,128)S(1)}, f32[656,256]{1,0:T(8,128)S(1)}, u32[]{:S(2)}, u32[]{:S(2)}) collective-permute-start(f32[656,256]{1,0:T(8,128)S(1)} %far.1), channel_id=1, source_target_pairs={{1,2},{2,1},{3,4},{4,3},{5,6},{6,5},{7,8},{8,7},{9,10},{10,9},{11,... | collective-permute-start | bytes 2015240 | tf_op jit(solution)/shard_map/ppermute | solution.py:1047
  6.7 0.0 copy-done.9
  6.7 0.0 copy-done.10
  6.7 0.0 copy-done.11
  6.8 0.0 copy-done.1
  6.8 0.0 copy-done.3
  6.8 0.0 copy-done
  6.8 0.0 copy-done.5
  6.8 0.0 copy-start.4
  6.8 0.0 copy-start.6
  6.8 0.0 copy-start.7
  6.8 0.0 copy-start.8
  6.9 2.0 %local.1 = (f32[18,72,512]{2,1,0:T(8,128)S(1)}, f32[1296,128]{1,0:T(8,128)S(1)}, f32[1296,128]{1,0:T(8,128)S(1)}, f32[1296,128]{1,0:T(8,128)S(1)}, f32[1296,128]...) custom-call(f32[18,72,512]{2,1,0:T(8,128)S(1)} %bitcast.10, ...), custom_call_target="tpu_custom_call" | custom-call | tf_op jit(solution)/shard_map/local/pallas_call | solution.py:150
  8.9 0.0 copy-done.2
  8.9 0.1 near.1.refs_14_
  9.0 0.1 collective-permute-start.1
  9.0 0.0 copy-done.4
  9.0 0.0 copy-done.6
  9.1 0.0 copy-done.7
  9.1 0.0 copy-done.8
  9.1 1.5 %middle.1 = (f32[18,72,512]{2,1,0:T(8,128)S(1)}, f32[18,72,512]{2,1,0:T(8,128)S(1)}, f32[18,72,512]{2,1,0:T(8,128)S(1)}, f32[16,1024]{1,0:T(8,128)S(1)}, f32[128,128]{1,0:T(8,128)S(1)}) custom-call(f32[18,72,512]{2,1,0:T(8,128)S(1)} %get-tuple-element.33.refs_0_, ...), custom_call_target="tpu_custom_call", output_to_operand_aliasing={{0}: (0, {})} | custom-call | tf_op jit(solution)/shard_map/middle/pallas_call | solution.py:150
  10.6 11.7 %all_to_all.11 = f32[16,8,128]{2,1,0:T(8,128)S(1)} all-to-all(f32[16,8,128]{2,1,0:T(8,128)S(1)} %bitcast.13), channel_id=1, replica_groups=mesh['groups'=2,'geo'=16] {'geo'}, dimensions={0} | all-to-all | bytes 131072 | tf_op jit(solution)/shard_map/all_to_all | solution.py:1063
  22.3 0.0 collective-permute-done.refs_3_
  22.3 0.0 collective-permute-done.1.refs_4_
  22.3 4.4 %late.1 = (f32[18,72,512]{2,1,0:T(8,128)S(1)}, f32[18,72,512]{2,1,0:T(8,128)S(1)}, f32[18,72,512]{2,1,0:T(8,128)S(1)}, f32[18,72,128]{2,1,0:T(8,128)S(1)}, f32[1...) custom-call(f32[18,72,512]{2,1,0:T(8,128)S(1)} %get-tuple-element.41, ...), custom_call_target="tpu_custom_call", output_to_operand_aliasing={{0}: (0, {}), {1}: (1, {}), {2}: (2, {})} | custom-call | tf_op jit(solution)/shard_map/late/pallas_call | solution.py:150
  26.7 4.3 %collective-permute-start.3 = (f32[48,256]{1,0:T(8,128)S(1)}, f32[48,256]{1,0:T(8,128)S(1)}, u32[]{:S(2)}, u32[]{:S(2)}) collective-permute-start(f32[48,256]{1,0:T(8,128)S(1)} %get-tuple-element.61), channel_id=1, source_target_pairs={{1,2},{2,1},{3,4},{4,3},{5,6},{6,5},{7,8},{8,7},{9,10},{10,9},{11,... | collective-permute-start | bytes 147464 | tf_op jit(solution)/shard_map/ppermute | solution.py:1068
  31.1 0.1 collective-permute-start.2
  31.1 1.6 %inner.1 = (f32[18,72,256]{2,1,0:T(8,128)S(1)}, f32[18,72,256]{2,1,0:T(8,128)S(1)}, f32[16,1024]{1,0:T(8,128)S(1)}) custom-call(f32[18,72,512]{2,1,0:T(8,128)S(1)} %get-tuple-element.47.next_, f32[18,72,512]{2,1,0:T(8,128)S(1)} %get-tuple-element.48.factor, f32[18,72,512]{2,1,0:T(8,128)S(1)} %get-tuple-element.51.source, ...), custom_call_target="tpu_custom_call" | custom-call | flops 4194304 | bytes 4194304 | tf_op jit(solution)/shard_map/inner/pallas_call | solution.py:150
  32.7 0.3 rim.1
  33.0 0.0 collective-permute-done.2.back_a
  33.1 0.0 collective-permute-done.3.back_b
  33.1 2.9 %last.1 = (f32[18,72,512]{2,1,0:T(8,128)}, f32[2,512]{1,0:T(2,128)}) custom-call(f32[18,72,512]{2,1,0:T(8,128)S(1)} %get-tuple-element.47.next_, f32[18,72,512]{2,1,0:T(8,128)S(1)} %get-tuple-element.48.factor, f32[18,72,128]{2,1,0:T(8,128)S(1)} %get-tuple-element.53.factor_south, f32[18,72,128]{2,1,0:T(8,128)S(1)} %get-tuple-element.54.factor_north, ...), custom_call_target="tpu_custom_call" | custom-call | tf_op jit(solution)/shard_map/last/pallas_call | solution.py:150
  (4 shorter events, 0.1 us)
Async XLA Ops:
  0.6 6.1 %copy-start.1 = (f32[4,72,128]{2,1,0:T(8,128)S(1)}, f32[4,72,128]{2,1,0:T(8,128)}, u32[]{:S(2)}) copy-start(f32[4,72,128]{2,1,0:T(8,128)} %constant.2.clone.table) | copy-start | bytes 442372
  0.6 6.1 %copy-start.3 = (s32[512]{0:T(512)S(1)}, s32[512]{0:T(512)}, u32[]{:S(2)}) copy-start(s32[512]{0:T(512)} %param.14) | copy-start | bytes 6148
  0.7 6.1 %copy-start = (f32[1296,512]{1,0:T(8,128)S(1)}, f32[1296,512]{1,0:T(8,128)}, u32[]{:S(2)}) copy-start(f32[1296,512]{1,0:T(8,128)} %param.12) | copy-start | bytes 7962628
  0.7 6.0 %copy-start.9 = (f32[1296]{0:T(1024)S(1)}, f32[1296]{0:T(1024)}, u32[]{:S(2)}) copy-start(f32[1296]{0:T(1024)} %param.16) | copy-start | bytes 15556
  0.7 6.0 %copy-start.10 = (f32[1296]{0:T(1024)S(1)}, f32[1296]{0:T(1024)}, u32[]{:S(2)}) copy-start(f32[1296]{0:T(1024)} %param.17) | copy-start | bytes 15556
  0.7 6.1 %copy-start.11 = (f32[1296]{0:T(1024)S(1)}, f32[1296]{0:T(1024)}, u32[]{:S(2)}) copy-start(f32[1296]{0:T(1024)} %param.18) | copy-start | bytes 15556
  0.7 6.1 %copy-start.5 = (f32[36]{0:T(128)S(1)}, f32[36]{0:T(128)}, u32[]{:S(2)}) copy-start(f32[36]{0:T(128)} %courant.1) | copy-start | bytes 436
  0.7 8.2 %copy-start.2 = (f32[2,512]{1,0:T(2,128)S(1)}, f32[2,512]{1,0:T(2,128)}, u32[]{:S(2)}) copy-start(f32[2,512]{1,0:T(2,128)} %wind_in.1) | copy-start | bytes 12292
  2.2 20.1 %collective-permute-start = (f32[656,256]{1,0:T(8,128)S(1)}, f32[656,256]{1,0:T(8,128)S(1)}, u32[]{:S(2)}, u32[]{:S(2)}) collective-permute-start(f32[656,256]{1,0:T(8,128)S(1)} %far.1), channel_id=1, source_target_pairs={{1,2},{2,1},{3,4},{4,3},{5,6},{6,5},{7,8},{8,7},{9,10},{10,9},{11,... | collective-permute-start | bytes 2015240 | tf_op jit(solution)/shard_map/ppermute | solution.py:1047
  6.8 2.2 %copy-start.4 = (f32[128,36]{0,1:T(8,128)S(1)}, f32[128,36]{0,1:T(8,128)}, u32[]{:S(2)}) copy-start(f32[128,36]{0,1:T(8,128)} %param.21) | copy-start | bytes 55300
  6.8 2.2 %copy-start.6 = (s32[128,1]{0,1:T(1,128)S(1)}, s32[128,1]{0,1:T(1,128)}, u32[]{:S(2)}) copy-start(s32[128,1]{0,1:T(1,128)} %param.19) | copy-start | bytes 1540
  6.8 2.2 %copy-start.7 = (s32[128]{0:T(128)S(1)}, s32[128]{0:T(128)}, u32[]{:S(2)}) copy-start(s32[128]{0:T(128)} %param.20) | copy-start | bytes 1540
  6.8 2.2 %copy-start.8 = (f32[128]{0:T(128)S(1)}, f32[128]{0:T(128)}, u32[]{:S(2)}) copy-start(f32[128]{0:T(128)} %param.22) | copy-start | bytes 1540
  9.0 13.3 %collective-permute-start.1 = (f32[656,256]{1,0:T(8,128)S(1)}, f32[656,256]{1,0:T(8,128)S(1)}, u32[]{:S(2)}, u32[]{:S(2)}) collective-permute-start(f32[656,256]{1,0:T(8,128)S(1)} %near.1.refs_14_), channel_id=1, source_target_pairs={{0,1},{1,0},{2,3},{3,2},{4,5},{5,4},{6,7},{7,6},{8,9},{9,8},{10,11... | collective-permute-start | bytes 2015240 | tf_op jit(solution)/shard_map/ppermute | solution.py:1058
  26.7 6.4 %collective-permute-start.3 = (f32[48,256]{1,0:T(8,128)S(1)}, f32[48,256]{1,0:T(8,128)S(1)}, u32[]{:S(2)}, u32[]{:S(2)}) collective-permute-start(f32[48,256]{1,0:T(8,128)S(1)} %get-tuple-element.61), channel_id=1, source_target_pairs={{1,2},{2,1},{3,4},{4,3},{5,6},{6,5},{7,8},{8,7},{9,10},{10,9},{11,... | collective-permute-start | bytes 147464 | tf_op jit(solution)/shard_map/ppermute | solution.py:1068
  31.1 2.0 %collective-permute-start.2 = (f32[40,256]{1,0:T(8,128)S(1)}, f32[40,256]{1,0:T(8,128)S(1)}, u32[]{:S(2)}, u32[]{:S(2)}) collective-permute-start(f32[40,256]{1,0:T(8,128)S(1)} %hand.1), channel_id=1, source_target_pairs={{0,1},{1,0},{2,3},{3,2},{4,5},{5,4},{6,7},{7,6},{8,9},{9,8},{10,11... | collective-permute-start | bytes 122888 | tf_op jit(solution)/shard_map/ppermute | solution.py:1069
